TPU v7x, 256 devices: a whole 4x4x8 slice. The times are simulated.
256 devices in a mesh: gx: 4 (over x), gy: 8 (over y, z_lo), gz: 8 (over z_hi, core).
Axes of the slice: x: 4, y: 4, z: 8 (z_hi: 4, z_lo: 2; z = z_hi * 2 + z_lo), core: 2. Of those that a mesh axis runs over, the one named last changes fastest.
Arguments:
- inputs: bfloat16 [1024, 6144], P(('gx', 'gy'), 'gz'), may hold values from -6 to 6
- weight_in: bfloat16 [6144, 24576], P('gz', ('gx', 'gy')), may hold values from -0.078125 to 0.078125
- weight_out: bfloat16 [24576, 6144], P(('gx', 'gy'), 'gz'), may hold values from -0.0390625 to 0.0390625
- output_grad: bfloat16 [1024, 6144], P(('gx', 'gy'), 'gz'), may hold values from -0.375 to 0.375
Outputs:
- output: bfloat16 [1024, 6144], P(('gx', 'gy'), 'gz')
- input_grad: bfloat16 [1024, 6144], P(('gx', 'gy'), 'gz')
- weight_in_grad: bfloat16 [6144, 24576], P('gz', ('gx', 'gy'))
- weight_out_grad: bfloat16 [24576, 6144], P(('gx', 'gy'), 'gz')
All inputs are finite; a program needn't handle non-finite values.
Results may differ from a plain program's by a relative error of at most 0.0049.
Values may be sent and summed in bfloat16 or wider, within the bound.
No kernel may reach another device: no remote copies, remote signals or barrier semaphores. Data moves between devices by JAX's collectives and lax.ppermute only.
A program may use at most 128 MiB of HBM per device.

v0:
```python
import jax
import jax.numpy as jnp
from jax import lax
from jax.sharding import PartitionSpec as P


def gelu_value(value):
    inner = 0.7978845608 * (value + 0.044715 * value * value * value)
    return 0.5 * value * (1.0 + jnp.tanh(inner))


def gelu_slope(value):
    inner = 0.7978845608 * (value + 0.044715 * value * value * value)
    tangent = jnp.tanh(inner)
    return 0.5 * (1.0 + tangent) + 0.5 * value * (1.0 - tangent * tangent) * 0.7978845608 * (
        1.0 + 0.134145 * value * value
    )


def product(left, right):
    return jnp.dot(left, right, preferred_element_type=jnp.float32)


def against(left, right):
    return lax.dot_general(
        left, right, (((1,), (1,)), ((), ())), preferred_element_type=jnp.float32
    )


def across(left, right):
    return lax.dot_general(
        left, right, (((0,), (0,)), ((), ())), preferred_element_type=jnp.float32
    )


def on_device(inputs, weight_in, weight_out, output_grad):
    groups_x = lax.axis_size("gx")
    local_rows = inputs.shape[0]
    feature_block = inputs.shape[1]
    hidden_block = weight_in.shape[1]
    input_block = lax.all_gather(inputs, "gx", axis=0, tiled=True)
    weight_in_block = lax.all_gather(weight_in, "gy", axis=1, tiled=True)
    hidden_wide = weight_in_block.shape[1]
    preact = lax.psum_scatter(
        product(input_block, weight_in_block), "gz", scatter_dimension=1, tiled=True
    )
    hidden = gelu_value(preact).astype(jnp.bfloat16)
    hidden_block_rows = lax.all_gather(hidden, "gz", axis=1, tiled=True)
    weight_out_block = lax.all_gather(weight_out, "gy", axis=0, tiled=True)
    output = lax.psum_scatter(
        product(hidden_block_rows, weight_out_block), "gx", scatter_dimension=0, tiled=True
    ).astype(jnp.bfloat16)
    grad_block = lax.all_gather(output_grad, "gx", axis=0, tiled=True)
    grad_hidden = lax.psum_scatter(
        against(grad_block, weight_out_block), "gz", scatter_dimension=1, tiled=True
    )
    grad_pre = (grad_hidden * gelu_slope(preact)).astype(jnp.bfloat16)
    grad_pre_block = lax.all_gather(grad_pre, "gz", axis=1, tiled=True)
    hidden_all = lax.all_to_all(
        hidden_block_rows.reshape(groups_x, local_rows, hidden_wide),
        "gy",
        split_axis=2,
        concat_axis=1,
        tiled=True,
    ).reshape(-1, hidden_block)
    grad_all = lax.all_gather(
        grad_block.reshape(groups_x, local_rows, feature_block), "gy", axis=1, tiled=True
    ).reshape(-1, feature_block)
    grad_pre_all = lax.all_to_all(
        grad_pre_block.reshape(groups_x, local_rows, hidden_wide),
        "gy",
        split_axis=2,
        concat_axis=1,
        tiled=True,
    ).reshape(-1, hidden_block)
    input_all = lax.all_gather(
        input_block.reshape(groups_x, local_rows, feature_block), "gy", axis=1, tiled=True
    ).reshape(-1, feature_block)
    input_grad = lax.psum_scatter(
        against(grad_pre_block, weight_in_block), "gx", scatter_dimension=0, tiled=True
    ).astype(jnp.bfloat16)
    weight_in_grad = across(input_all, grad_pre_all).astype(jnp.bfloat16)
    weight_out_grad = across(hidden_all, grad_all).astype(jnp.bfloat16)
    return (output, input_grad, weight_in_grad, weight_out_grad)


def solution(mesh):
    placed = (
        P(("gx", "gy"), "gz"),
        P("gz", ("gx", "gy")),
        P(("gx", "gy"), "gz"),
        P(("gx", "gy"), "gz"),
    )
    return jax.shard_map(
        on_device,
        mesh=mesh,
        in_specs=placed,
        out_specs=(
            P(("gx", "gy"), "gz"),
            P(("gx", "gy"), "gz"),
            P("gz", ("gx", "gy")),
            P(("gx", "gy"), "gz"),
        ),
        check_vma=False,
    )
```

profile of v0, /device:TPU:2, one launch (start us, length us, event | category | flops | bytes accessed | tf_op | source)
XLA Modules:
  0.0 731.6 jit_solution(2276041438809950380)
XLA Ops:
  7.2 0.0 copy-start.4
  7.2 0.0 all-gather.11.cloned.1.call-start
  7.2 0.7 all-gather.11.cloned.1.call-update
  7.9 0.0 all-gather.7.cloned.1.call-start
  8.0 0.7 all-gather.7.cloned.1.call-update
  8.7 0.0 reduce-scatter.9.cloned.1.call-start
  8.7 0.0 copy-done.4
  8.7 12.2 %all_gather.28 = bf16[128,768]{1,0:T(8,128)(2,1)S(1)} all-gather(bf16[32,768]{1,0:T(8,128)(2,1)S(1)} %copy-done.4), channel_id=1, replica_groups=mesh['gx'=4,'gy'=8,'gz'=8] {'gx'}, dimensions={0}, use_global_device_ids=true | all-gather | bytes 245760 | tf_op jit(solution)/shard_map/all_gather | solution.py:53
  20.9 0.0 copy-start.2
  20.9 182.5 %all-gather.11.cloned.1.call-done = bf16[6144,768]{1,0:T(8,128)(2,1)} async-done(((bf16[768,768]{1,0:T(8,128)(2,1)}), bf16[6144,768]{1,0:T(8,128)(2,1)}) %all-gather.11.cloned.1.call-update) | async-done | bytes 9437200 | tf_op jit(solution)/shard_map/all_gather | solution.py:49
  203.4 8.5 %fusion.10 = f32[128,6144]{1,0:T(8,128)} fusion(bf16[128,768]{1,0:T(8,128)(2,1)S(1)} %all_gather.28, bf16[6144,768]{1,0:T(8,128)(2,1)} %all-gather.11.cloned.1.call-done), kind=kOutput, calls=%fused_computation.15 | convolution fusion | flops 1207959552 | bytes 12779520 | tf_op jit(solution)/shard_map/dot_general | solution.py:25
  211.9 0.0 copy-done.2
  211.9 0.0 copy-start.5
  211.9 0.0 reduce-scatter.9.cloned.1.call-update
  211.9 0.0 reduce-scatter.5.cloned.1.call-start
  212.0 0.7 copy-done.5
  212.7 12.1 %all_gather.24 = bf16[128,768]{1,0:T(8,128)(2,1)S(1)} all-gather(bf16[32,768]{1,0:T(8,128)(2,1)S(1)} %copy-done.5), channel_id=1, replica_groups=mesh['gx'=4,'gy'=8,'gz'=8] {'gx'}, dimensions={0}, use_global_device_ids=true | all-gather | bytes 245760 | tf_op jit(solution)/shard_map/all_gather | solution.py:41
  224.8 0.0 copy-start.3
  224.8 172.0 %all-gather.7.cloned.1.call-done = bf16[768,6144]{1,0:T(8,128)(2,1)} async-done(((bf16[768,768]{1,0:T(8,128)(2,1)}), bf16[768,6144]{1,0:T(8,128)(2,1)}) %all-gather.7.cloned.1.call-update) | async-done | bytes 9437200 | tf_op jit(solution)/shard_map/all_gather | solution.py:42
  396.8 6.8 fusion.8
  403.6 0.0 copy-done.3
  403.6 0.0 reduce-scatter.5.cloned.1.call-update
  403.6 0.0 all-gather.9.cloned.1.call-start
  403.7 48.4 %reduce-scatter.9.cloned.1.call-done = f32[128,768]{1,0:T(8,128)} async-done(((f32[128,6144]{1,0:T(8,128)}), f32[128,768]{1,0:T(8,128)}) %reduce-scatter.9.cloned.1.call-update) | async-done | bytes 393232 | tf_op jit(solution)/shard_map/reduce_scatter | solution.py:54
  452.1 52.7 %reduce-scatter.5.cloned.1.call-done = f32[128,768]{1,0:T(8,128)} async-done(((f32[128,6144]{1,0:T(8,128)}), f32[128,768]{1,0:T(8,128)}) %reduce-scatter.5.cloned.1.call-update) | async-done | bytes 393232 | tf_op jit(solution)/shard_map/reduce_scatter | solution.py:44
  504.8 2.1 fusion.7
  506.9 0.0 all-gather.9.cloned.1.call-update
  506.9 0.0 all-gather.13.cloned.1.call-start
  507.0 0.5 all-gather.13.cloned.1.call-update
  507.5 0.0 reduce-scatter.7.cloned.1.call-start
  507.6 29.5 %all-gather.9.cloned.1.call-done = bf16[128,6144]{1,0:T(8,128)(2,1)} async-done(((bf16[128,768]{1,0:T(8,128)(2,1)}), bf16[128,6144]{1,0:T(8,128)(2,1)}) %all-gather.9.cloned.1.call-update) | async-done | bytes 1572880 | tf_op jit(solution)/shard_map/all_gather | solution.py:48
  537.1 6.3 fusion.9
  543.4 0.0 reduce-scatter.7.cloned.1.call-update
  543.4 0.0 reduce-scatter.11.cloned.1.call-start
  543.4 27.2 %all-gather.13.cloned.1.call-done = bf16[128,6144]{1,0:T(8,128)(2,1)} async-done(((bf16[128,768]{1,0:T(8,128)(2,1)}), bf16[128,6144]{1,0:T(8,128)(2,1)}) %all-gather.13.cloned.1.call-update) | async-done | bytes 1572880 | tf_op jit(solution)/shard_map/all_gather | solution.py:58
  570.7 0.0 copy-start.1
  570.7 8.3 %fusion.11 = f32[128,768]{1,0:T(8,128)} fusion(bf16[128,6144]{1,0:T(8,128)(2,1)} %all-gather.13.cloned.1.call-done, bf16[768,6144]{1,0:T(8,128)(2,1)} %all-gather.7.cloned.1.call-done), kind=kOutput, calls=%fused_computation.16 | convolution fusion | flops 1207959552 | bytes 11403264 | tf_op jit(solution)/shard_map/dot_general | solution.py:25
  578.9 0.0 reduce-scatter.11.cloned.1.call-update
  578.9 0.0 copy-done.1
  579.0 6.3 copy.13
  585.2 9.5 %reshape.42 = bf16[8,2,49152]{2,1,0:T(2,128)(2,1)} reshape(bf16[6144,4,32]{2,1,0:T(4,128)(2,1)} %bitcast.34) | data formatting | bytes 3145728
  594.8 6.0 all-to-all-start
  600.8 0.0 all-gather.15.cloned.1.call-start
  600.8 0.7 all-gather.15.cloned.1.call-update
  601.5 0.0 copy-done
  601.5 6.3 copy.16
  607.8 9.5 %reshape.44 = bf16[8,2,49152]{2,1,0:T(2,128)(2,1)} reshape(bf16[6144,4,32]{2,1,0:T(4,128)(2,1)} %bitcast.35) | data formatting | bytes 3145728
  617.3 5.2 all-to-all-done
  622.5 3.6 all-to-all-start.1
  626.1 0.2 all-gather.17.cloned.1.call-start
  626.3 0.4 all-gather.17.cloned.1.call-update
  626.7 0.0 reduce-scatter.7.cloned.1.call-done
  626.7 1.5 convert_element_type.22
  628.2 1.5 convert_element_type.24
  629.8 5.4 reshape.43
  635.2 8.2 %copy.21 = bf16[4,32,8,768]{3,1,2,0:T(8,128)(2,1)S(1)} copy(bf16[4,32,8,768]{1,0,3,2:T(4,128)(2,1)} %bitcast.36) | data formatting | bytes 3145728 | tf_op jit(solution)/shard_map/all_to_all | solution.py:69
  643.4 33.4 %all-gather.15.cloned.1.call-done = bf16[4,256,768]{2,1,0:T(8,128)(2,1)} async-done(((bf16[4,32,768]{2,1,0:T(8,128)(2,1)}), bf16[4,256,768]{2,1,0:T(8,128)(2,1)}) %all-gather.15.cloned.1.call-update) | async-done | bytes 1572880 | tf_op jit(solution)/shard_map/all_gather | solution.py:76
  676.8 3.9 fusion
  680.7 2.4 copy.19
  683.0 0.0 all-to-all-done.1
  683.0 5.4 reshape.45
  688.5 8.2 %copy.23 = bf16[4,32,8,768]{3,1,2,0:T(8,128)(2,1)S(1)} copy(bf16[4,32,8,768]{1,0,3,2:T(4,128)(2,1)} %bitcast.37) | data formatting | bytes 3145728 | tf_op jit(solution)/shard_map/all_to_all | solution.py:59
  696.7 24.2 %all-gather.17.cloned.1.call-done = bf16[4,256,768]{2,1,0:T(8,128)(2,1)} async-done(((bf16[4,32,768]{2,1,0:T(8,128)(2,1)}), bf16[4,256,768]{2,1,0:T(8,128)(2,1)}) %all-gather.17.cloned.1.call-update) | async-done | bytes 1572880 | tf_op jit(solution)/shard_map/all_gather | solution.py:66
  720.9 3.9 convolution_convert_fusion
  (2 shorter events, 0.0 us)
Async XLA Ops:
  7.2 1.5 copy-start.4
  7.2 196.3 %all-gather.11.cloned.1.call-start = ((), (), s32[]{:S(2)}) async-start(), calls=%async_computation.9 | async-start | bytes 10616832 | tf_op jit(solution)/shard_map/all_gather | solution.py:49
  7.9 388.9 %all-gather.7.cloned.1.call-start = ((), (), s32[]{:S(2)}) async-start(), calls=%async_computation.6 | async-start | bytes 10616832 | tf_op jit(solution)/shard_map/all_gather | solution.py:42
  8.7 443.5 %reduce-scatter.9.cloned.1.call-start = ((), (), s32[]{:S(2)}) async-start(), calls=%async_computation.11 | async-start | bytes 3538944 | tf_op jit(solution)/shard_map/reduce_scatter | solution.py:54
  20.9 191.0 %copy-start.2 = (bf16[128,768]{1,0:T(8,128)(2,1)}, bf16[128,768]{1,0:T(8,128)(2,1)S(1)}, u32[]{:S(2)}) copy-start(bf16[128,768]{1,0:T(8,128)(2,1)S(1)} %all_gather.28) | copy-start | bytes 589828
  211.9 0.8 copy-start.5
  211.9 292.8 %reduce-scatter.5.cloned.1.call-start = ((), (), s32[]{:S(2)}) async-start(), calls=%async_computation.7 | async-start | bytes 3538944 | tf_op jit(solution)/shard_map/reduce_scatter | solution.py:44
  224.8 178.8 %copy-start.3 = (bf16[128,768]{1,0:T(8,128)(2,1)}, bf16[128,768]{1,0:T(8,128)(2,1)S(1)}, u32[]{:S(2)}) copy-start(bf16[128,768]{1,0:T(8,128)(2,1)S(1)} %all_gather.24) | copy-start | bytes 589828
  403.6 133.4 %all-gather.9.cloned.1.call-start = ((), (), s32[]{:S(2)}) async-start(), calls=%async_computation.8 | async-start | bytes 1769472 | tf_op jit(solution)/shard_map/all_gather | solution.py:48
  506.9 63.7 %all-gather.13.cloned.1.call-start = ((), (), s32[]{:S(2)}) async-start(), calls=%async_computation.12 | async-start | bytes 1769472 | tf_op jit(solution)/shard_map/all_gather | solution.py:58
  507.5 119.2 %reduce-scatter.7.cloned.1.call-start = ((), (), s32[]{:S(2)}) async-start(), calls=%async_computation.10 | async-start | bytes 491520 | tf_op jit(solution)/shard_map/reduce_scatter | solution.py:50
  543.4 84.9 %reduce-scatter.11.cloned.1.call-start = ((), (), s32[]{:S(2)}) async-start(), calls=%async_computation.13 | async-start | bytes 491520 | tf_op jit(solution)/shard_map/reduce_scatter | solution.py:79
  570.7 8.3 %copy-start.1 = (bf16[128,6144]{1,0:T(8,128)(2,1)S(1)}, bf16[128,6144]{1,0:T(8,128)(2,1)}, u32[]{:S(2)}) copy-start(bf16[128,6144]{1,0:T(8,128)(2,1)} %all-gather.13.cloned.1.call-done) | copy-start | bytes 4718596
  594.8 6.7 copy-start
  594.8 27.7 %all-to-all-start = ((bf16[8,2,49152]{2,1,0:T(2,128)(2,1)}), bf16[8,2,49152]{2,1,0:T(2,128)(2,1)S(1)}, u32[]{:S(2)}, u32[]{:S(2)}) async-start(bf16[8,2,49152]{2,1,0:T(2,128)(2,1)} %reshape.42), calls=%async_computation.4 | async-start | bytes 3145728 | tf_op jit(solution)/shard_map/all_to_all | solution.py:69
  600.8 76.0 %all-gather.15.cloned.1.call-start = ((), (), s32[]{:S(2)}) async-start(), calls=%async_computation.14 | async-start | bytes 1769472 | tf_op jit(solution)/shard_map/all_gather | solution.py:76
  622.5 60.5 %all-to-all-start.1 = ((bf16[8,2,49152]{2,1,0:T(2,128)(2,1)}), bf16[8,2,49152]{2,1,0:T(2,128)(2,1)S(1)}, u32[]{:S(2)}, u32[]{:S(2)}) async-start(bf16[8,2,49152]{2,1,0:T(2,128)(2,1)} %reshape.44), calls=%async_computation.5 | async-start | bytes 3145728 | tf_op jit(solution)/shard_map/all_to_all | solution.py:59
  626.1 94.7 %all-gather.17.cloned.1.call-start = ((), (), s32[]{:S(2)}) async-start(), calls=%async_computation.15 | async-start | bytes 1769472 | tf_op jit(solution)/shard_map/all_gather | solution.py:66
Sparse Core Ops, SparseCore 0:
  9.8 193.5 all-gather.10
  205.2 191.5 all-gather.6
  399.4 52.7 reduce-scatter.8
  454.5 50.2 reduce-scatter.4
  507.1 29.9 all-gather.8
  539.3 31.2 all-gather.12
  573.8 20.5 reduce-scatter.6
  597.6 23.1 reduce-scatter.10
  622.6 54.1 all-gather.14
  678.4 42.3 all-gather.16
where the time goes:
time: 733 us; the launch traced here: 732 us
  waiting for transfers between devices  578 us (79%)
  local copies, waits for them, and re-layouts  61.9 us (8%)
  matrix products  37.6 us (5%)
  blocking collectives  24.3 us (3%)
  between operations  14.2 us (2%)
  starting transfers between devices  10.1 us (1%)
    all_gather x1, waiting for transfers between devices, on_device(): weight_out_block = lax.all_gather(weight_out, 'gy', axis=0, tiled=True)  183 us
    all_gather x1, waiting for transfers between devices, on_device(): weight_in_block = lax.all_gather(weight_in, 'gy', axis=1, tiled=True)  172 us
    reduce_scatter x1, waiting for transfers between devices, on_device(): lax.psum_scatter(product(input_block, weight_in_block), 'gz', scatter_dim...  52.7 us
    reduce_scatter x1, waiting for transfers between devices, on_device(): lax.psum_scatter(against(grad_block, weight_out_block), 'gz', scatter_dim...  48.4 us
    all_gather x1, waiting for transfers between devices, on_device(): lax.all_gather(input_block.reshape(groups_x, local_rows, feature_block),...  33.4 us
    unnamed x17, local copies, waits for them, and re-layouts  33 us
    all_gather x1, waiting for transfers between devices, on_device(): hidden_block_rows = lax.all_gather(hidden, 'gz', axis=1, tiled=True)  29.5 us
    all_gather x1, waiting for transfers between devices, on_device(): grad_pre_block = lax.all_gather(grad_pre, 'gz', axis=1, tiled=True)  27.2 us
  transfers between devices with their start and end apart: 12, of which 9 were waited for; matrix products, arithmetic and copies ran while one was open for 13% of the time, Pallas kernels for 0%

commit v1 on v0

v1 whole, which is shorter than its diff:
```python
import jax
import jax.numpy as jnp
from jax import lax
from jax.sharding import PartitionSpec as P

F32 = jnp.float32
BF16 = jnp.bfloat16
ROWS = ("gx", "gy")


def gelu_both(value):
    inner = 0.7978845608 * (value + 0.044715 * value * value * value)
    tangent = jnp.tanh(inner)
    slope = 0.5 * (1.0 + tangent) + 0.5 * value * (1.0 - tangent * tangent) * 0.7978845608 * (
        1.0 + 0.134145 * value * value
    )
    return 0.5 * value * (1.0 + tangent), slope


def product(left, right):
    return jnp.dot(left, right, preferred_element_type=F32)


def against(left, right):
    return lax.dot_general(left, right, (((1,), (1,)), ((), ())), preferred_element_type=F32)


def across(left, right):
    return lax.dot_general(left, right, (((0,), (0,)), ((), ())), preferred_element_type=F32)


def gather_rows(block, peers):
    copies = jnp.broadcast_to(block[None], (peers,) + block.shape)
    return lax.all_to_all(copies, ROWS, 0, 0).reshape(-1, block.shape[1])


def scatter_rows(partial, peers):
    pieces = partial.astype(BF16).reshape(peers, -1, partial.shape[1])
    return lax.all_to_all(pieces, ROWS, 0, 0).astype(F32).sum(0).astype(BF16)


def on_device(inputs, weight_in, weight_out, output_grad):
    peers = lax.axis_size("gx") * lax.axis_size("gy")
    depth = lax.axis_size("gz")
    ring = depth // 2
    place = lax.axis_index("gz")
    core = place % 2
    spot = place // 2
    tokens = peers * inputs.shape[0]
    half = tokens // 2
    quarter = half // ring
    split = quarter // 2

    def step(block, hops):
        pairs = [(i, ((i // 2 + hops) % ring) * 2 + i % 2) for i in range(depth)]
        return lax.ppermute(block, "gz", pairs)

    def swap(block):
        return lax.ppermute(block, "gz", [(i, i ^ 1) for i in range(depth)])

    def pick(array, index):
        return lax.dynamic_index_in_dim(array, index, 0, keepdims=False)

    def reduce_features(left, multiply):
        halves = left.reshape(2, half, -1)
        away = swap(multiply(pick(halves, 1 - core)).astype(BF16))
        total = multiply(pick(halves, core)) + away.astype(F32)
        blocks = total.reshape(ring, quarter, -1)
        own, ahead, far, behind = (pick(blocks, (spot + d) % ring) for d in range(4))
        far = far.astype(BF16)
        up = step(far[:split], 1)
        down = step(far[split:], -1)
        ahead = jnp.concatenate([ahead[:split] + up.astype(F32), ahead[split:]], 0).astype(BF16)
        behind = jnp.concatenate([behind[:split], behind[split:] + down.astype(F32)], 0).astype(BF16)
        return own + step(ahead, 1).astype(F32) + step(behind, -1).astype(F32)

    def gather_tokens(block):
        up = step(block, 1)
        down = step(block, -1)
        far = jnp.concatenate([step(up[:split], 1), step(down[split:], -1)], 0)
        mine = jnp.zeros((ring, quarter, block.shape[1]), block.dtype)
        for offset, piece in ((0, block), (-1, up), (1, down), (2, far)):
            mine = lax.dynamic_update_index_in_dim(mine, piece, (spot + offset) % ring, 0)
        mine = mine.reshape(half, -1)
        other = swap(mine)
        first = jnp.where(core == 0, mine, other)
        second = jnp.where(core == 0, other, mine)
        return jnp.concatenate([first, second], 0)

    input_all = gather_rows(inputs, peers)
    preact = reduce_features(input_all, lambda rows: product(rows, weight_in))
    grad_all = gather_rows(output_grad, peers)
    hidden, slope = gelu_both(preact)
    hidden_all = gather_tokens(hidden.astype(BF16))
    grad_hidden = reduce_features(grad_all, lambda rows: against(rows, weight_out))
    grad_pre_all = gather_tokens((grad_hidden * slope).astype(BF16))
    output = scatter_rows(product(hidden_all, weight_out), peers)
    input_grad = scatter_rows(against(grad_pre_all, weight_in), peers)
    weight_out_grad = across(hidden_all, grad_all).astype(BF16)
    weight_in_grad = across(input_all, grad_pre_all).astype(BF16)
    return (output, input_grad, weight_in_grad, weight_out_grad)


def solution(mesh):
    rows = P(("gx", "gy"), "gz")
    columns = P("gz", ("gx", "gy"))
    return jax.shard_map(
        on_device,
        mesh=mesh,
        in_specs=(rows, columns, rows, rows),
        out_specs=(rows, rows, columns, rows),
        check_vma=False,
    )
```

time: 733 us -> 217 us (0.30)
  waiting for transfers between devices: 578 us -> 82.3 us
  local copies, waits for them, and re-layouts: 61.9 us -> 7.23 us
  starting transfers between devices: 10.1 us -> 59.8 us
  matrix products: 37.6 us -> 22.7 us
  between operations: 14.2 us -> 1.12 us
    all_gather x6 -> x0, waiting for transfers between devices: 469 us -> none  [the longest x1 183 us: on_device(): weight_out_block = lax.all_gather(weight_out, 'gy', axis=0, tiled=True)]
    reduce_scatter x4 -> x0, waiting for transfers between devices: 101 us -> none  [the longest x1 52.7 us: on_device(): lax.psum_scatter(product(input_block, weight_in_block), 'gz', scatter_dim...]
    ppermute x0 -> x20, waiting for transfers between devices: none -> 54.5 us  [the longest x16 49.9 us: step(): return lax.ppermute(block, 'gz', pairs)]
    ppermute x0 -> x20, starting transfers between devices: none -> 37.9 us  [the longest x16 37.6 us: step(): return lax.ppermute(block, 'gz', pairs)]
    all_to_all x0 -> x1, blocking collectives: none -> 29.9 us  [gather_rows(): return lax.all_to_all(copies, ROWS, 0, 0).reshape(-1, block.shape[1])]
    unnamed x17 -> x31, local copies, waits for them, and re-layouts: 33 us -> 4.29 us
    all_gather x2 -> x0, blocking collectives: 24.3 us -> none  [the longest x1 12.2 us: on_device(): grad_block = lax.all_gather(output_grad, 'gx', axis=0, tiled=True)]
    all_to_all x2 -> x3, waiting for transfers between devices: 5.21 us -> 27.9 us  [the longest x1 16.8 us: gather_rows(): return lax.all_to_all(copies, ROWS, 0, 0).reshape(-1, block.shape[1])]
  transfers between devices with their start and end apart: 12 -> 23, of which waited for: 9 -> 13; matrix products, arithmetic and copies ran while one was open for 13% -> 13% of each run, Pallas kernels for 0% -> 0%
where the time goes in v1:
time: 217 us; the launch traced here: 213 us
  waiting for transfers between devices  82.3 us (38%)
  starting transfers between devices  59.8 us (28%)
  blocking collectives  29.9 us (14%)
  matrix products  22.7 us (10%)
  other arithmetic  9.94 us (5%)
  local copies, waits for them, and re-layouts  7.23 us (3%)
    ppermute x16, waiting for transfers between devices, step(): return lax.ppermute(block, 'gz', pairs)  49.9 us
    ppermute x16, starting transfers between devices, step(): return lax.ppermute(block, 'gz', pairs)  37.6 us
    all_to_all x1, blocking collectives, gather_rows(): return lax.all_to_all(copies, ROWS, 0, 0).reshape(-1, block.shape[1])  29.9 us
    all_to_all x1, waiting for transfers between devices, gather_rows(): return lax.all_to_all(copies, ROWS, 0, 0).reshape(-1, block.shape[1])  16.8 us
    all_to_all x2, starting transfers between devices, scatter_rows(): return lax.all_to_all(pieces, ROWS, 0, 0).astype(F32).sum(0).astype(BF16)  14.8 us
    all_to_all x2, waiting for transfers between devices, scatter_rows(): return lax.all_to_all(pieces, ROWS, 0, 0).astype(F32).sum(0).astype(BF16)  11.1 us
    dot_general x2, matrix products, across(): lax.dot_general(left, right, (((0,), (0,)), ((), ())), preferred_element_...  8.22 us
    dot_general x3, matrix products, against(): lax.dot_general(left, right, (((1,), (1,)), ((), ())), preferred_element_...  7.9 us
  transfers between devices with their start and end apart: 23, of which 13 were waited for; matrix products, arithmetic and copies ran while one was open for 13% of the time, Pallas kernels for 0%

profile of v1, /device:TPU:2, one launch (start us, length us, event | category | flops | bytes accessed | tf_op | source)
XLA Modules:
  0.0 213.0 jit_solution(7331055629232557298)
XLA Ops:
  0.6 0.0 copy-start
  0.6 1.1 broadcast_in_dim.42
  1.7 0.0 copy-start.13
  1.7 29.9 %all_to_all.20 = bf16[32,32,768]{2,1,0:T(8,128)(2,1)S(1)} all-to-all(bf16[32,32,768]{2,1,0:T(8,128)(2,1)S(1)} %broadcast_in_dim.42), channel_id=1, replica_groups=mesh['gx'=4,'gy'=8,'gz'=8] {'gx','gy'}, dimensions={0} | all-to-all | bytes 3145728 | tf_op jit(solution)/shard_map/all_to_all | solution.py:34
  31.6 1.5 broadcast_in_dim.37
  33.1 7.1 %all-to-all-start = ((bf16[32,32,768]{2,1,0:T(8,128)(2,1)}), bf16[32,32,768]{2,1,0:T(8,128)(2,1)}, u32[]{:S(2)}, u32[]{:S(2)}) async-start(bf16[32,32,768]{2,1,0:T(8,128)(2,1)} %broadcast_in_dim.37), calls=%async_computation | async-start | bytes 3145728 | tf_op jit(solution)/shard_map/all_to_all | solution.py:34
  40.3 3.0 %convolution_convert_fusion.4 = bf16[512,768]{1,0:T(8,128)(2,1)} fusion(bf16[768,768]{1,0:T(8,128)(2,1)} %param.6, bf16[2,512,768]{2,1,0:T(8,128)(2,1)S(1)} %bitcast.119, s32[]{:T(128)S(6)} %select_n.113), kind=kOutput, calls=%fused_computation.9 | convolution fusion | flops 604372992 | bytes 2752516 | tf_op jit(solution)/shard_map/dot_general | solution.py:25
  43.2 16.8 %all-to-all-done = bf16[32,32,768]{2,1,0:T(8,128)(2,1)} async-done(((bf16[32,32,768]{2,1,0:T(8,128)(2,1)}), bf16[32,32,768]{2,1,0:T(8,128)(2,1)}, u32[]{:S(2)}, u32[]{:S(2)}) %all-to-all-start) | async-done | bytes 1572896 | tf_op jit(solution)/shard_map/all_to_all | solution.py:34
  60.0 1.9 convolution_convert_fusion.5
  61.9 0.1 collective-permute-start
  62.1 2.3 %convert_add_fusion = f32[512,768]{1,0:T(8,128)S(1)} fusion(bf16[512,768]{1,0:T(8,128)(2,1)} %collective-permute-done.10, bf16[768,768]{1,0:T(8,128)(2,1)} %param.6, bf16[2,512,768]{2,1,0:T(8,128)(2,1)S(1)} %bitcast.120, s32[]{:T(128)S(6)} %select_n.112), kind=kOutput, calls=%fused_computation.4 | convolution fusion | flops 604766208 | bytes 4325380 | tf_op jit(solution)/shard_map/dot_general | solution.py:25
  64.5 3.4 %collective-permute-start.11 = (bf16[64,768]{1,0:T(8,128)(2,1)S(1)}, bf16[64,768]{1,0:T(8,128)(2,1)S(1)}, u32[]{:S(2)}, u32[]{:S(2)}) collective-permute-start(bf16[64,768]{1,0:T(8,128)(2,1)S(1)} %get-tuple-element.24), channel_id=1, source_target_pairs={{0,2},{1,3},{2,4},{3,5},{4,6},{5,7},{6,0},{7,1},{8,10},{9,11},{10,... | collective-permute-start | bytes 294920 | tf_op jit(solution)/shard_map/ppermute | solution.py:56
  67.9 2.2 %collective-permute-start.13 = (bf16[64,768]{1,0:T(8,128)(2,1)S(1)}, bf16[64,768]{1,0:T(8,128)(2,1)S(1)}, u32[]{:S(2)}, u32[]{:S(2)}) collective-permute-start(bf16[64,768]{1,0:T(8,128)(2,1)S(1)} %get-tuple-element.25), channel_id=1, source_target_pairs={{0,6},{1,7},{2,0},{3,1},{4,2},{5,3},{6,4},{7,5},{8,14},{9,15},{10,... | collective-permute-start | bytes 294920 | tf_op jit(solution)/shard_map/ppermute | solution.py:56
  70.1 2.1 %convert_add_fusion.1 = f32[512,768]{1,0:T(8,128)S(1)} fusion(bf16[512,768]{1,0:T(8,128)(2,1)} %collective-permute-done, bf16[768,768]{1,0:T(8,128)(2,1)S(1)} %copy-done, bf16[2,512,768]{2,1,0:T(8,128)(2,1)} %bitcast, s32[]{:T(128)S(6)} %select_n.112), kind=kOutput, calls=%fused_computation.5 | convolution fusion | flops 604766208 | bytes 4325380 | tf_op jit(solution)/shard_map/dot_general | solution.py:21
  72.3 1.4 collective-permute-start.1
  73.8 2.8 %collective-permute-start.3 = (bf16[64,768]{1,0:T(8,128)(2,1)S(1)}, bf16[64,768]{1,0:T(8,128)(2,1)S(1)}, u32[]{:S(2)}, u32[]{:S(2)}) collective-permute-start(bf16[64,768]{1,0:T(8,128)(2,1)S(1)} %get-tuple-element.27), channel_id=1, source_target_pairs={{0,6},{1,7},{2,0},{3,1},{4,2},{5,3},{6,4},{7,5},{8,14},{9,15},{10,... | collective-permute-start | bytes 294920 | tf_op jit(solution)/shard_map/ppermute | solution.py:56
  76.7 0.7 pad_maximum_fusion.8
  77.4 3.9 %collective-permute-start.12 = (bf16[128,768]{1,0:T(8,128)(2,1)}, bf16[128,768]{1,0:T(8,128)(2,1)}, u32[]{:S(2)}, u32[]{:S(2)}) collective-permute-start(bf16[128,768]{1,0:T(8,128)(2,1)} %pad_maximum_fusion.8), channel_id=1, source_target_pairs={{0,2},{1,3},{2,4},{3,5},{4,6},{5,7},{6,0},{7,1},{8,10},{9,11},{10,... | collective-permute-start | bytes 589832 | tf_op jit(solution)/shard_map/ppermute | solution.py:56
  81.3 0.7 pad_maximum_fusion.9
  82.0 0.2 collective-permute-start.14
  82.2 0.3 collective-permute-done.3
  82.5 0.7 pad_maximum_fusion.6
  83.2 4.1 %collective-permute-start.2 = (bf16[128,768]{1,0:T(8,128)(2,1)}, bf16[128,768]{1,0:T(8,128)(2,1)S(1)}, u32[]{:S(2)}, u32[]{:S(2)}) collective-permute-start(bf16[128,768]{1,0:T(8,128)(2,1)} %pad_maximum_fusion.6), channel_id=1, source_target_pairs={{0,2},{1,3},{2,4},{3,5},{4,6},{5,7},{6,0},{7,1},{8,10},{9,11},{10,... | collective-permute-start | bytes 589832 | tf_op jit(solution)/shard_map/ppermute | solution.py:56
  87.3 0.7 pad_maximum_fusion.7
  88.0 0.1 collective-permute-start.4
  88.1 4.0 %collective-permute-done.12 = bf16[128,768]{1,0:T(8,128)(2,1)} collective-permute-done((bf16[128,768]{1,0:T(8,128)(2,1)}, bf16[128,768]{1,0:T(8,128)(2,1)}, u32[]{:S(2)}, u32[]{:S(2)}) %collective-permute-start.12) | collective-permute-done | bytes 196640 | tf_op jit(solution)/shard_map/ppermute | solution.py:56
  92.1 0.8 collective-permute-done.14
  92.9 6.5 %collective-permute-done.2 = bf16[128,768]{1,0:T(8,128)(2,1)S(1)} collective-permute-done((bf16[128,768]{1,0:T(8,128)(2,1)}, bf16[128,768]{1,0:T(8,128)(2,1)S(1)}, u32[]{:S(2)}, u32[]{:S(2)}) %collective-permute-start.2) | collective-permute-done | bytes 196640 | tf_op jit(solution)/shard_map/ppermute | solution.py:56
  99.4 0.7 copy-done.4
  100.1 0.1 broadcast.21.clone.1
  100.1 2.4 %bitcast_dynamic-update-slice_fusion.2 = (bf16[4,128,768]{2,1,0:T(8,128)(2,1)S(1)}, bf16[128,768]{1,0:T(8,128)(2,1)}) fusion(bf16[4,128,768]{2,1,0:T(8,128)(2,1)S(1)} %broadcast.21.clone.1, s32[]{:T(128)S(6)} %select_n.116, bf16[128,768]{1,0:T(8,128)(2,1)} %collective-permute-done.4, bf16[128,768]{1,0:T(8,128)(2,1)} %copy-done.4, ...), kind=kLoop, calls=%fused_computation.67 | loop fusion | flops 2654208 | bytes 1966084 | tf_op jit(solution)/shard_map/jit(dynamic_update_index_in_dim)/dynamic_update_slice | solution.py:83
  102.5 4.6 %collective-permute-start.15 = (bf16[128,768]{1,0:T(8,128)(2,1)}, bf16[128,768]{1,0:T(8,128)(2,1)S(1)}, u32[]{:S(2)}, u32[]{:S(2)}) collective-permute-start(bf16[128,768]{1,0:T(8,128)(2,1)} %get-tuple-element.9), channel_id=1, source_target_pairs={{0,2},{1,3},{2,4},{3,5},{4,6},{5,7},{6,0},{7,1},{8,10},{9,11},{10,... | collective-permute-start | bytes 589832 | tf_op jit(solution)/shard_map/ppermute | solution.py:56
  107.1 4.9 %collective-permute-done.15 = bf16[128,768]{1,0:T(8,128)(2,1)S(1)} collective-permute-done((bf16[128,768]{1,0:T(8,128)(2,1)}, bf16[128,768]{1,0:T(8,128)(2,1)S(1)}, u32[]{:S(2)}, u32[]{:S(2)}) %collective-permute-start.15) | collective-permute-done | bytes 196640 | tf_op jit(solution)/shard_map/ppermute | solution.py:56
  112.0 6.0 %collective-permute-start.17 = (bf16[64,768]{1,0:T(8,128)(2,1)S(1)}, bf16[64,768]{1,0:T(8,128)(2,1)S(1)}, u32[]{:S(2)}, u32[]{:S(2)}) collective-permute-start(bf16[64,768]{1,0:T(8,128)(2,1)S(1)} %slice.122), channel_id=1, source_target_pairs={{0,2},{1,3},{2,4},{3,5},{4,6},{5,7},{6,0},{7,1},{8,10},{9,11},{10,... | collective-permute-start | bytes 294920 | tf_op jit(solution)/shard_map/ppermute | solution.py:56
  117.9 0.5 collective-permute-start.18
  118.5 3.6 %collective-permute-done.17 = bf16[64,768]{1,0:T(8,128)(2,1)S(1)} collective-permute-done((bf16[64,768]{1,0:T(8,128)(2,1)S(1)}, bf16[64,768]{1,0:T(8,128)(2,1)S(1)}, u32[]{:S(2)}, u32[]{:S(2)}) %collective-permute-start.17) | collective-permute-done | bytes 98336 | tf_op jit(solution)/shard_map/ppermute | solution.py:56
  122.1 1.9 collective-permute-done.18
  124.0 0.1 collective-permute-start.19
  124.1 2.3 %collective-permute-done.19 = bf16[512,768]{1,0:T(8,128)(2,1)S(1)} collective-permute-done((bf16[512,768]{1,0:T(8,128)(2,1)S(1)}, bf16[512,768]{1,0:T(8,128)(2,1)S(1)}, u32[]{:S(2)}, u32[]{:S(2)}) %collective-permute-start.19) | collective-permute-done | bytes 786464 | tf_op jit(solution)/shard_map/ppermute | solution.py:59
  126.4 0.2 broadcast_select_fusion.1
  126.6 0.0 copy-start.6
  126.6 2.6 %convolution_convert_fusion = bf16[1024,768]{1,0:T(8,128)(2,1)} fusion(bf16[768,768]{1,0:T(8,128)(2,1)S(1)} %copy-done, bf16[512,768]{1,0:T(8,128)(2,1)S(1)} %get-tuple-element.13, bf16[512,768]{1,0:T(8,128)(2,1)S(1)} %get-tuple-element.12), kind=kOutput, calls=%fused_computation | convolution fusion | flops 1211891712 | bytes 4325376 | tf_op jit(solution)/shard_map/dot_general | solution.py:25
  129.2 7.3 %all-to-all-start.3 = ((bf16[32,32,768]{2,1,0:T(8,128)(2,1)}), bf16[32,32,768]{2,1,0:T(8,128)(2,1)S(1)}, u32[]{:S(2)}, u32[]{:S(2)}) async-start(bf16[32,32,768]{2,1,0:T(8,128)(2,1)} %bitcast.122), calls=%async_computation.3 | async-start | bytes 3145728 | tf_op jit(solution)/shard_map/all_to_all | solution.py:39
  136.5 0.1 broadcast.21.clone
  136.6 1.3 bitcast_dynamic-update-slice_fusion.5
  137.9 2.8 %collective-permute-start.5 = (bf16[128,768]{1,0:T(8,128)(2,1)S(1)}, bf16[128,768]{1,0:T(8,128)(2,1)S(1)}, u32[]{:S(2)}, u32[]{:S(2)}) collective-permute-start(bf16[128,768]{1,0:T(8,128)(2,1)S(1)} %get-tuple-element.11), channel_id=1, source_target_pairs={{0,2},{1,3},{2,4},{3,5},{4,6},{5,7},{6,0},{7,1},{8,10},{9,11},{10,... | collective-permute-start | bytes 589832 | tf_op jit(solution)/shard_map/ppermute | solution.py:56
  140.7 1.4 collective-permute-start.6
  142.1 25.4 %collective-permute-done.5 = bf16[128,768]{1,0:T(8,128)(2,1)S(1)} collective-permute-done((bf16[128,768]{1,0:T(8,128)(2,1)S(1)}, bf16[128,768]{1,0:T(8,128)(2,1)S(1)}, u32[]{:S(2)}, u32[]{:S(2)}) %collective-permute-start.5) | collective-permute-done | bytes 196640 | tf_op jit(solution)/shard_map/ppermute | solution.py:56
  167.5 0.1 collective-permute-start.7
  167.7 4.2 %collective-permute-start.8 = (bf16[64,768]{1,0:T(8,128)(2,1)S(1)}, bf16[64,768]{1,0:T(8,128)(2,1)S(1)}, u32[]{:S(2)}, u32[]{:S(2)}) collective-permute-start(bf16[64,768]{1,0:T(8,128)(2,1)S(1)} %slice.119), channel_id=1, source_target_pairs={{0,6},{1,7},{2,0},{3,1},{4,2},{5,3},{6,4},{7,5},{8,14},{9,15},{10,... | collective-permute-start | bytes 294920 | tf_op jit(solution)/shard_map/ppermute | solution.py:56
  171.9 2.5 %collective-permute-done.7 = bf16[64,768]{1,0:T(8,128)(2,1)S(1)} collective-permute-done((bf16[64,768]{1,0:T(8,128)(2,1)S(1)}, bf16[64,768]{1,0:T(8,128)(2,1)S(1)}, u32[]{:S(2)}, u32[]{:S(2)}) %collective-permute-start.7) | collective-permute-done | bytes 98336 | tf_op jit(solution)/shard_map/ppermute | solution.py:56
  174.4 0.1 collective-permute-start.9
  174.5 2.3 %collective-permute-done.9 = bf16[512,768]{1,0:T(8,128)(2,1)S(1)} collective-permute-done((bf16[512,768]{1,0:T(8,128)(2,1)S(1)}, bf16[512,768]{1,0:T(8,128)(2,1)S(1)}, u32[]{:S(2)}, u32[]{:S(2)}) %collective-permute-start.9) | collective-permute-done | bytes 786464 | tf_op jit(solution)/shard_map/ppermute | solution.py:59
  176.7 0.2 broadcast_select_fusion.3
  176.9 0.9 copy-done.9
  177.8 0.2 copy-done.11
  178.0 2.6 %convolution_convert_fusion.1 = bf16[1024,768]{1,0:T(8,128)(2,1)} fusion(bf16[768,768]{1,0:T(8,128)(2,1)S(1)} %copy-done.14, bf16[512,768]{1,0:T(8,128)(2,1)S(1)} %get-tuple-element.19, bf16[512,768]{1,0:T(8,128)(2,1)S(1)} %get-tuple-element.18), kind=kOutput, calls=%fused_computation.1 | convolution fusion | flops 1211891712 | bytes 4325376 | tf_op jit(solution)/shard_map/dot_general | solution.py:21
  180.6 7.5 %all-to-all-start.1 = ((bf16[32,32,768]{2,1,0:T(8,128)(2,1)}), bf16[32,32,768]{2,1,0:T(8,128)(2,1)}, u32[]{:S(2)}, u32[]{:S(2)}) async-start(bf16[32,32,768]{2,1,0:T(8,128)(2,1)} %bitcast.123), calls=%async_computation.1 | async-start | bytes 3145728 | tf_op jit(solution)/shard_map/all_to_all | solution.py:39
  188.1 4.1 %fusion = bf16[768,768]{0,1:T(8,128)(2,1)} fusion(bf16[1024,768]{1,0:T(8,128)(2,1)} %bitcast.34, bf16[512,768]{1,0:T(8,128)(2,1)} %copy-done.8, bf16[512,768]{1,0:T(8,128)(2,1)S(1)} %copy-done.7), kind=kOutput, calls=%fused_computation.8 | convolution fusion | flops 1211695104 | bytes 4325376 | tf_op jit(solution)/shard_map/dot_general | solution.py:29
  192.3 2.4 %copy.8 = bf16[768,768]{1,0:T(8,128)(2,1)} copy(bf16[768,768]{0,1:T(8,128)(2,1)} %fusion) | data formatting | bytes 2359296
  194.7 4.1 %convolution_convert_fusion.2 = bf16[768,768]{1,0:T(8,128)(2,1)} fusion(bf16[1024,768]{1,0:T(8,128)(2,1)} %bitcast.121, bf16[512,768]{1,0:T(8,128)(2,1)} %copy-done.11, bf16[512,768]{1,0:T(8,128)(2,1)S(1)} %copy-done.10), kind=kOutput, calls=%fused_computation.6 | convolution fusion | flops 1211695104 | bytes 4325376 | tf_op jit(solution)/shard_map/dot_general | solution.py:29
  198.8 0.8 reduce_sum.25
  199.7 11.1 %all-to-all-done.1 = bf16[32,32,768]{2,1,0:T(8,128)(2,1)} async-done(((bf16[32,32,768]{2,1,0:T(8,128)(2,1)}), bf16[32,32,768]{2,1,0:T(8,128)(2,1)}, u32[]{:S(2)}, u32[]{:S(2)}) %all-to-all-start.1) | async-done | bytes 1572896 | tf_op jit(solution)/shard_map/all_to_all | solution.py:39
  210.7 2.3 %reduce_sum.24 = bf16[32,768]{1,0:T(8,128)(2,1)} reduce(bf16[32,32,768]{2,1,0:T(8,128)(2,1)} %all-to-all-done.1, bf16[]{:T(256)} %constant.133.clone.1), dimensions={0}, to_apply=%region_0.1 | reduce | flops 761856 | bytes 1622018 | tf_op jit(solution)/shard_map/reduce_sum | solution.py:39
  (54 shorter events, 0.5 us)
Async XLA Ops:
  0.6 59.4 %copy-start = (bf16[768,768]{1,0:T(8,128)(2,1)S(1)}, bf16[768,768]{1,0:T(8,128)(2,1)}, u32[]{:S(2)}) copy-start(bf16[768,768]{1,0:T(8,128)(2,1)} %param.5) | copy-start | bytes 3538948
  1.7 29.9 %copy-start.13 = (bf16[32,768]{1,0:T(8,128)(2,1)S(1)}, bf16[32,768]{1,0:T(8,128)(2,1)}, u32[]{:S(2)}) copy-start(bf16[32,768]{1,0:T(8,128)(2,1)} %param.4) | copy-start | bytes 147460
  31.6 30.5 %copy-start.1 = (bf16[32,32,768]{2,1,0:T(8,128)(2,1)}, bf16[32,32,768]{2,1,0:T(8,128)(2,1)S(1)}, u32[]{:S(2)}) copy-start(bf16[32,32,768]{2,1,0:T(8,128)(2,1)S(1)} %all_to_all.20) | copy-start | bytes 4718596
  33.1 26.9 %all-to-all-start = ((bf16[32,32,768]{2,1,0:T(8,128)(2,1)}), bf16[32,32,768]{2,1,0:T(8,128)(2,1)}, u32[]{:S(2)}, u32[]{:S(2)}) async-start(bf16[32,32,768]{2,1,0:T(8,128)(2,1)} %broadcast_in_dim.37), calls=%async_computation | async-start | bytes 3145728 | tf_op jit(solution)/shard_map/all_to_all | solution.py:34
  43.2 18.9 %collective-permute-start.10 = (bf16[512,768]{1,0:T(8,128)(2,1)}, bf16[512,768]{1,0:T(8,128)(2,1)}, u32[]{:S(2)}, u32[]{:S(2)}) collective-permute-start(bf16[512,768]{1,0:T(8,128)(2,1)} %convolution_convert_fusion.4), channel_id=1, source_target_pairs={{0,1},{1,0},{2,3},{3,2},{4,5},{5,4},{6,7},{7,6},{8,9},{9,8},{10,11... | collective-permute-start | bytes 2359304 | tf_op jit(solution)/shard_map/ppermute | solution.py:59
  61.9 8.2 %collective-permute-start = (bf16[512,768]{1,0:T(8,128)(2,1)S(1)}, bf16[512,768]{1,0:T(8,128)(2,1)}, u32[]{:S(2)}, u32[]{:S(2)}) collective-permute-start(bf16[512,768]{1,0:T(8,128)(2,1)S(1)} %convolution_convert_fusion.5), channel_id=1, source_target_pairs={{0,1},{1,0},{2,3},{3,2},{4,5},{5,4},{6,7},{7,6},{8,9},{9,8},{10,11... | collective-permute-start | bytes 2359304 | tf_op jit(solution)/shard_map/ppermute | solution.py:59
  64.4 12.2 %copy-start.3 = (f32[512,768]{1,0:T(8,128)}, f32[512,768]{1,0:T(8,128)S(1)}, u32[]{:S(2)}) copy-start(f32[512,768]{1,0:T(8,128)S(1)} %convert_add_fusion) | copy-start | bytes 4718596
  64.5 12.1 %collective-permute-start.11 = (bf16[64,768]{1,0:T(8,128)(2,1)S(1)}, bf16[64,768]{1,0:T(8,128)(2,1)S(1)}, u32[]{:S(2)}, u32[]{:S(2)}) collective-permute-start(bf16[64,768]{1,0:T(8,128)(2,1)S(1)} %get-tuple-element.24), channel_id=1, source_target_pairs={{0,2},{1,3},{2,4},{3,5},{4,6},{5,7},{6,0},{7,1},{8,10},{9,11},{10,... | collective-permute-start | bytes 294920 | tf_op jit(solution)/shard_map/ppermute | solution.py:56
  67.9 8.7 %collective-permute-start.13 = (bf16[64,768]{1,0:T(8,128)(2,1)S(1)}, bf16[64,768]{1,0:T(8,128)(2,1)S(1)}, u32[]{:S(2)}, u32[]{:S(2)}) collective-permute-start(bf16[64,768]{1,0:T(8,128)(2,1)S(1)} %get-tuple-element.25), channel_id=1, source_target_pairs={{0,6},{1,7},{2,0},{3,1},{4,2},{5,3},{6,4},{7,5},{8,14},{9,15},{10,... | collective-permute-start | bytes 294920 | tf_op jit(solution)/shard_map/ppermute | solution.py:56
  72.3 27.8 %copy-start.2 = (f32[512,768]{1,0:T(8,128)}, f32[512,768]{1,0:T(8,128)S(1)}, u32[]{:S(2)}) copy-start(f32[512,768]{1,0:T(8,128)S(1)} %convert_add_fusion.1) | copy-start | bytes 4718596
  72.3 9.9 %collective-permute-start.1 = (bf16[64,768]{1,0:T(8,128)(2,1)S(1)}, bf16[64,768]{1,0:T(8,128)(2,1)S(1)}, u32[]{:S(2)}, u32[]{:S(2)}) collective-permute-start(bf16[64,768]{1,0:T(8,128)(2,1)S(1)} %get-tuple-element.26), channel_id=1, source_target_pairs={{0,2},{1,3},{2,4},{3,5},{4,6},{5,7},{6,0},{7,1},{8,10},{9,11},{10,... | collective-permute-start | bytes 294920 | tf_op jit(solution)/shard_map/ppermute | solution.py:56
  73.8 8.7 %collective-permute-start.3 = (bf16[64,768]{1,0:T(8,128)(2,1)S(1)}, bf16[64,768]{1,0:T(8,128)(2,1)S(1)}, u32[]{:S(2)}, u32[]{:S(2)}) collective-permute-start(bf16[64,768]{1,0:T(8,128)(2,1)S(1)} %get-tuple-element.27), channel_id=1, source_target_pairs={{0,6},{1,7},{2,0},{3,1},{4,2},{5,3},{6,4},{7,5},{8,14},{9,15},{10,... | collective-permute-start | bytes 294920 | tf_op jit(solution)/shard_map/ppermute | solution.py:56
  77.4 14.7 %collective-permute-start.12 = (bf16[128,768]{1,0:T(8,128)(2,1)}, bf16[128,768]{1,0:T(8,128)(2,1)}, u32[]{:S(2)}, u32[]{:S(2)}) collective-permute-start(bf16[128,768]{1,0:T(8,128)(2,1)} %pad_maximum_fusion.8), channel_id=1, source_target_pairs={{0,2},{1,3},{2,4},{3,5},{4,6},{5,7},{6,0},{7,1},{8,10},{9,11},{10,... | collective-permute-start | bytes 589832 | tf_op jit(solution)/shard_map/ppermute | solution.py:56
  82.0 10.9 %collective-permute-start.14 = (bf16[128,768]{1,0:T(8,128)(2,1)}, bf16[128,768]{1,0:T(8,128)(2,1)S(1)}, u32[]{:S(2)}, u32[]{:S(2)}) collective-permute-start(bf16[128,768]{1,0:T(8,128)(2,1)} %pad_maximum_fusion.9), channel_id=1, source_target_pairs={{0,6},{1,7},{2,0},{3,1},{4,2},{5,3},{6,4},{7,5},{8,14},{9,15},{10,... | collective-permute-start | bytes 589832 | tf_op jit(solution)/shard_map/ppermute | solution.py:56
  83.2 16.1 %collective-permute-start.2 = (bf16[128,768]{1,0:T(8,128)(2,1)}, bf16[128,768]{1,0:T(8,128)(2,1)S(1)}, u32[]{:S(2)}, u32[]{:S(2)}) collective-permute-start(bf16[128,768]{1,0:T(8,128)(2,1)} %pad_maximum_fusion.6), channel_id=1, source_target_pairs={{0,2},{1,3},{2,4},{3,5},{4,6},{5,7},{6,0},{7,1},{8,10},{9,11},{10,... | collective-permute-start | bytes 589832 | tf_op jit(solution)/shard_map/ppermute | solution.py:56
  88.0 12.1 %collective-permute-start.4 = (bf16[128,768]{1,0:T(8,128)(2,1)}, bf16[128,768]{1,0:T(8,128)(2,1)}, u32[]{:S(2)}, u32[]{:S(2)}) collective-permute-start(bf16[128,768]{1,0:T(8,128)(2,1)} %pad_maximum_fusion.7), channel_id=1, source_target_pairs={{0,6},{1,7},{2,0},{3,1},{4,2},{5,3},{6,4},{7,5},{8,14},{9,15},{10,... | collective-permute-start | bytes 589832 | tf_op jit(solution)/shard_map/ppermute | solution.py:56
  92.9 6.5 %copy-start.12 = (bf16[128,768]{1,0:T(8,128)(2,1)}, bf16[128,768]{1,0:T(8,128)(2,1)S(1)}, u32[]{:S(2)}) copy-start(bf16[128,768]{1,0:T(8,128)(2,1)S(1)} %collective-permute-done.14) | copy-start | bytes 589828
  99.4 0.7 copy-start.4
  102.5 9.4 %collective-permute-start.15 = (bf16[128,768]{1,0:T(8,128)(2,1)}, bf16[128,768]{1,0:T(8,128)(2,1)S(1)}, u32[]{:S(2)}, u32[]{:S(2)}) collective-permute-start(bf16[128,768]{1,0:T(8,128)(2,1)} %get-tuple-element.9), channel_id=1, source_target_pairs={{0,2},{1,3},{2,4},{3,5},{4,6},{5,7},{6,0},{7,1},{8,10},{9,11},{10,... | collective-permute-start | bytes 589832 | tf_op jit(solution)/shard_map/ppermute | solution.py:56
  107.1 10.8 %collective-permute-start.16 = (bf16[128,768]{1,0:T(8,128)(2,1)}, bf16[128,768]{1,0:T(8,128)(2,1)S(1)}, u32[]{:S(2)}, u32[]{:S(2)}) collective-permute-start(bf16[128,768]{1,0:T(8,128)(2,1)} %get-tuple-element.9), channel_id=1, source_target_pairs={{0,6},{1,7},{2,0},{3,1},{4,2},{5,3},{6,4},{7,5},{8,14},{9,15},{10,... | collective-permute-start | bytes 589832 | tf_op jit(solution)/shard_map/ppermute | solution.py:56
  112.0 10.2 %collective-permute-start.17 = (bf16[64,768]{1,0:T(8,128)(2,1)S(1)}, bf16[64,768]{1,0:T(8,128)(2,1)S(1)}, u32[]{:S(2)}, u32[]{:S(2)}) collective-permute-start(bf16[64,768]{1,0:T(8,128)(2,1)S(1)} %slice.122), channel_id=1, source_target_pairs={{0,2},{1,3},{2,4},{3,5},{4,6},{5,7},{6,0},{7,1},{8,10},{9,11},{10,... | collective-permute-start | bytes 294920 | tf_op jit(solution)/shard_map/ppermute | solution.py:56
  117.9 6.1 %collective-permute-start.18 = (bf16[64,768]{1,0:T(8,128)(2,1)S(1)}, bf16[64,768]{1,0:T(8,128)(2,1)S(1)}, u32[]{:S(2)}, u32[]{:S(2)}) collective-permute-start(bf16[64,768]{1,0:T(8,128)(2,1)S(1)} %slice.123), channel_id=1, source_target_pairs={{0,6},{1,7},{2,0},{3,1},{4,2},{5,3},{6,4},{7,5},{8,14},{9,15},{10,... | collective-permute-start | bytes 294920 | tf_op jit(solution)/shard_map/ppermute | solution.py:56
  124.0 2.4 %collective-permute-start.19 = (bf16[512,768]{1,0:T(8,128)(2,1)S(1)}, bf16[512,768]{1,0:T(8,128)(2,1)S(1)}, u32[]{:S(2)}, u32[]{:S(2)}) collective-permute-start(bf16[512,768]{1,0:T(8,128)(2,1)S(1)} %bitcast.118), channel_id=1, source_target_pairs={{0,1},{1,0},{2,3},{3,2},{4,5},{5,4},{6,7},{7,6},{8,9},{9,8},{10,11... | collective-permute-start | bytes 2359304 | tf_op jit(solution)/shard_map/ppermute | solution.py:59
  126.6 2.7 %copy-start.6 = (bf16[512,768]{1,0:T(8,128)(2,1)}, bf16[512,768]{1,0:T(8,128)(2,1)S(1)}, u32[]{:S(2)}) copy-start(bf16[512,768]{1,0:T(8,128)(2,1)S(1)} %get-tuple-element.12) | copy-start | bytes 2359300
  126.6 2.6 %copy-start.8 = (bf16[512,768]{1,0:T(8,128)(2,1)}, bf16[512,768]{1,0:T(8,128)(2,1)S(1)}, u32[]{:S(2)}) copy-start(bf16[512,768]{1,0:T(8,128)(2,1)S(1)} %get-tuple-element.13) | copy-start | bytes 2359300
  129.2 7.4 %copy-start.5 = (bf16[128,768]{1,0:T(8,128)(2,1)S(1)}, bf16[128,768]{1,0:T(8,128)(2,1)}, u32[]{:S(2)}) copy-start(bf16[128,768]{1,0:T(8,128)(2,1)} %copy-done.4) | copy-start | bytes 589828
  129.2 51.4 %all-to-all-start.3 = ((bf16[32,32,768]{2,1,0:T(8,128)(2,1)}), bf16[32,32,768]{2,1,0:T(8,128)(2,1)S(1)}, u32[]{:S(2)}, u32[]{:S(2)}) async-start(bf16[32,32,768]{2,1,0:T(8,128)(2,1)} %bitcast.122), calls=%async_computation.3 | async-start | bytes 3145728 | tf_op jit(solution)/shard_map/all_to_all | solution.py:39
  137.9 29.6 %collective-permute-start.5 = (bf16[128,768]{1,0:T(8,128)(2,1)S(1)}, bf16[128,768]{1,0:T(8,128)(2,1)S(1)}, u32[]{:S(2)}, u32[]{:S(2)}) collective-permute-start(bf16[128,768]{1,0:T(8,128)(2,1)S(1)} %get-tuple-element.11), channel_id=1, source_target_pairs={{0,2},{1,3},{2,4},{3,5},{4,6},{5,7},{6,0},{7,1},{8,10},{9,11},{10,... | collective-permute-start | bytes 589832 | tf_op jit(solution)/shard_map/ppermute | solution.py:56
  140.7 26.9 %collective-permute-start.6 = (bf16[128,768]{1,0:T(8,128)(2,1)S(1)}, bf16[128,768]{1,0:T(8,128)(2,1)S(1)}, u32[]{:S(2)}, u32[]{:S(2)}) collective-permute-start(bf16[128,768]{1,0:T(8,128)(2,1)S(1)} %get-tuple-element.11), channel_id=1, source_target_pairs={{0,6},{1,7},{2,0},{3,1},{4,2},{5,3},{6,4},{7,5},{8,14},{9,15},{10,... | collective-permute-start | bytes 589832 | tf_op jit(solution)/shard_map/ppermute | solution.py:56
  167.5 6.8 %collective-permute-start.7 = (bf16[64,768]{1,0:T(8,128)(2,1)S(1)}, bf16[64,768]{1,0:T(8,128)(2,1)S(1)}, u32[]{:S(2)}, u32[]{:S(2)}) collective-permute-start(bf16[64,768]{1,0:T(8,128)(2,1)S(1)} %slice.118), channel_id=1, source_target_pairs={{0,2},{1,3},{2,4},{3,5},{4,6},{5,7},{6,0},{7,1},{8,10},{9,11},{10,... | collective-permute-start | bytes 294920 | tf_op jit(solution)/shard_map/ppermute | solution.py:56
  167.7 6.7 %collective-permute-start.8 = (bf16[64,768]{1,0:T(8,128)(2,1)S(1)}, bf16[64,768]{1,0:T(8,128)(2,1)S(1)}, u32[]{:S(2)}, u32[]{:S(2)}) collective-permute-start(bf16[64,768]{1,0:T(8,128)(2,1)S(1)} %slice.119), channel_id=1, source_target_pairs={{0,6},{1,7},{2,0},{3,1},{4,2},{5,3},{6,4},{7,5},{8,14},{9,15},{10,... | collective-permute-start | bytes 294920 | tf_op jit(solution)/shard_map/ppermute | solution.py:56
  174.4 3.7 %copy-start.14 = (bf16[768,768]{1,0:T(8,128)(2,1)S(1)}, bf16[768,768]{1,0:T(8,128)(2,1)}, u32[]{:S(2)}) copy-start(bf16[768,768]{1,0:T(8,128)(2,1)} %param.6) | copy-start | bytes 3538948
  174.4 2.4 %collective-permute-start.9 = (bf16[512,768]{1,0:T(8,128)(2,1)S(1)}, bf16[512,768]{1,0:T(8,128)(2,1)S(1)}, u32[]{:S(2)}, u32[]{:S(2)}) collective-permute-start(bf16[512,768]{1,0:T(8,128)(2,1)S(1)} %bitcast.117), channel_id=1, source_target_pairs={{0,1},{1,0},{2,3},{3,2},{4,5},{5,4},{6,7},{7,6},{8,9},{9,8},{10,11... | collective-permute-start | bytes 2359304 | tf_op jit(solution)/shard_map/ppermute | solution.py:59
  176.9 0.9 copy-start.9
  176.9 1.1 copy-start.11
  180.6 7.5 %copy-start.7 = (bf16[512,768]{1,0:T(8,128)(2,1)S(1)}, bf16[512,768]{1,0:T(8,128)(2,1)}, u32[]{:S(2)}) copy-start(bf16[512,768]{1,0:T(8,128)(2,1)} %copy-done.6) | copy-start | bytes 2359300
  180.6 30.1 %all-to-all-start.1 = ((bf16[32,32,768]{2,1,0:T(8,128)(2,1)}), bf16[32,32,768]{2,1,0:T(8,128)(2,1)}, u32[]{:S(2)}, u32[]{:S(2)}) async-start(bf16[32,32,768]{2,1,0:T(8,128)(2,1)} %bitcast.123), calls=%async_computation.1 | async-start | bytes 3145728 | tf_op jit(solution)/shard_map/all_to_all | solution.py:39
  192.3 2.4 %copy-start.10 = (bf16[512,768]{1,0:T(8,128)(2,1)S(1)}, bf16[512,768]{1,0:T(8,128)(2,1)}, u32[]{:S(2)}) copy-start(bf16[512,768]{1,0:T(8,128)(2,1)} %copy-done.9) | copy-start | bytes 2359300

commit v2 on v1

v2 whole, which is shorter than its diff:
```python
import functools

import jax
import jax.numpy as jnp
from jax import lax
from jax.experimental import pallas as pl
from jax.experimental.pallas import tpu as pltpu
from jax.sharding import Mesh, PartitionSpec as P

F32 = jnp.float32
BF16 = jnp.bfloat16
NEAR = ("x", "l")
FAR = ("y", "x", "l")
VMEM = 32 * 2**20


def gelu_both(value):
    inner = 0.7978845608 * (value + 0.044715 * value * value * value)
    tangent = jnp.tanh(inner)
    slope = 0.5 * (1.0 + tangent) + 0.5 * value * (1.0 - tangent * tangent) * 0.7978845608 * (
        1.0 + 0.134145 * value * value
    )
    return 0.5 * value * (1.0 + tangent), slope


def across(left, right):
    return lax.dot_general(left, right, (((0,), (0,)), ((), ())), preferred_element_type=F32)


def move(block, axis, hops):
    size = lax.axis_size(axis)
    return lax.ppermute(block, axis, [(i, (i + hops) % size) for i in range(size)])


def pick(array, index):
    return lax.dynamic_index_in_dim(array, index, 0, keepdims=False)


def ring_gather(block, axis):
    spot = lax.axis_index(axis)
    cut = block.shape[0] // 2
    up = move(block, axis, 1)
    down = move(block, axis, -1)
    far_up = move(up[:cut], axis, 1)
    far_down = move(down[cut:], axis, -1)
    whole = jnp.zeros((4,) + block.shape, block.dtype)
    for hops, piece in ((0, block), (3, up), (1, down)):
        whole = lax.dynamic_update_index_in_dim(whole, piece, (spot + hops) % 4, 0)
    far = (spot + 2) % 4
    whole = lax.dynamic_update_slice(whole, far_up[None], (far, 0, 0))
    whole = lax.dynamic_update_slice(whole, far_down[None], (far, cut, 0))
    return whole.reshape(-1, block.shape[1])


def ring_sum(blocks, axis):
    spot = lax.axis_index(axis)
    cut = blocks.shape[1] // 2
    own, ahead, far, behind = (pick(blocks, (spot + d) % 4) for d in range(4))
    far = far.astype(BF16)
    up = move(far[:cut], axis, 1).astype(F32)
    down = move(far[cut:], axis, -1).astype(F32)
    ahead = jnp.concatenate([ahead[:cut] + up, ahead[cut:]], 0).astype(BF16)
    behind = jnp.concatenate([behind[:cut], behind[cut:] + down], 0).astype(BF16)
    return own + move(ahead, axis, 1).astype(F32) + move(behind, axis, -1).astype(F32)


def product_kernel(turned, which_ref, rows_ref, weight_ref, out_ref):
    sides = ((1,), (1,)) if turned else ((1,), (0,))
    out_ref[...] = lax.dot_general(
        rows_ref[...], weight_ref[...], (sides, ((), ())), preferred_element_type=F32
    ).astype(out_ref.dtype)


def product(rows, weight, turned, dtype, tile, which=None, weigh=1):
    if which is None:
        stride, which = 1, jnp.zeros((1,), jnp.int32)
    else:
        stride, which = 2, which.astype(jnp.int32).reshape(1)
    steps = rows.shape[0] // tile // stride
    width = weight.shape[0] if turned else weight.shape[1]
    return pl.pallas_call(
        functools.partial(product_kernel, turned),
        grid_spec=pltpu.PrefetchScalarGridSpec(
            num_scalar_prefetch=1,
            grid=(steps,),
            in_specs=[
                pl.BlockSpec((tile, rows.shape[1]), lambda i, which: (stride * i + which[0], 0)),
                pl.BlockSpec(weight.shape, lambda i, which: (0, 0)),
            ],
            out_specs=pl.BlockSpec((tile, width), lambda i, which: (i, 0)),
        ),
        out_shape=jax.ShapeDtypeStruct((steps * tile, width), dtype),
        compiler_params=pltpu.CompilerParams(vmem_limit_bytes=VMEM),
        cost_estimate=pl.CostEstimate(
            flops=2 * weigh * steps * tile * weight.size,
            bytes_accessed=2 * (steps * tile * rows.shape[1] + weight.size) + 4 * steps * tile * width,
            transcendentals=0,
        ),
    )(which, rows, weight)


def on_device(inputs, weight_in, weight_out, output_grad):
    core = lax.axis_index("c")
    rows, features = inputs.shape
    near = lax.axis_size(NEAR)
    peers = lax.axis_size(FAR)
    tokens = peers * rows
    ring = lax.axis_size("h")
    tile = tokens // (2 * ring)

    def pair_sum(left, weight, turned):
        away = move(product(left, weight, turned, BF16, tile, 1 - core), "c", 1)
        total = product(left, weight, turned, F32, tile, core) + away.astype(F32)
        return total.reshape(ring, tile, -1)

    def rows_sum(partial):
        pieces = lax.all_to_all(partial.reshape(peers, rows, -1), FAR, 0, 0)
        return pieces.astype(F32).sum(0).astype(BF16)

    both = jnp.concatenate([inputs, output_grad], 1)
    both = lax.all_to_all(jnp.broadcast_to(both[None], (near,) + both.shape), NEAR, 0, 0)
    both = both.reshape(near * rows, -1)
    grad_all = lax.all_gather(both[:, features:], "y", axis=0, tiled=True)
    input_all = ring_gather(both[:, :features], "y")

    preact = ring_sum(pair_sum(input_all, weight_in, False), "h")
    pairs = pair_sum(grad_all, weight_out, True)
    hidden = gelu_both(preact)[0].astype(BF16)
    mine = ring_gather(hidden, "h").reshape(ring, 1, tile, -1)
    other = move(mine, "c", 1)
    hidden_all = jnp.concatenate(
        [jnp.where(core == 0, mine, other), jnp.where(core == 0, other, mine)], 1
    ).reshape(tokens, -1)
    grad_hidden = ring_sum(pairs, "h")
    grad_hidden, preact = lax.optimization_barrier((grad_hidden, preact))
    grad_pre = (grad_hidden * gelu_both(preact)[1]).astype(BF16)
    grad_pre_all = lax.all_gather(grad_pre, ("h", "c"), axis=0, tiled=True)

    ready = lax.optimization_barrier((hidden_all, grad_pre))[0]
    output = rows_sum(jnp.dot(ready, weight_out, preferred_element_type=F32).astype(BF16))
    input_grad = rows_sum(product(grad_pre_all, weight_in, True, BF16, 2 * tile, weigh=40))
    weight_out_grad = across(hidden_all, grad_all).astype(BF16)
    weight_in_grad = across(input_all, grad_pre_all).astype(BF16)
    return (output, input_grad, weight_in_grad, weight_out_grad)


def solution(mesh):
    fine = Mesh(mesh.devices.reshape(4, 4, 2, 4, 2), ("x", "y", "l", "h", "c"))
    rows = P(("x", "y", "l"), ("h", "c"))
    columns = P(("h", "c"), ("x", "y", "l"))
    return jax.shard_map(
        on_device,
        mesh=fine,
        in_specs=(rows, columns, rows, rows),
        out_specs=(rows, rows, columns, rows),
        check_vma=False,
    )
```

time: 217 us -> 207 us (0.954); the launches traced: 213 us -> 206 us
  matrix products: 22.7 us -> 9.03 us
  between operations: 1.12 us -> 14.5 us
  blocking collectives: 29.9 us -> 17.1 us
  Pallas kernels: 0 us -> 9.1 us
  starting transfers between devices: 59.8 us -> 51.2 us
  local copies, waits for them, and re-layouts: 7.23 us -> 14.1 us
    all_to_all x1, blocking collectives: 29.9 us -> 17.1 us  [on_device(): lax.all_to_all(jnp.broadcast_to(both[None], (near,) + both.shape), NEAR,...]
    dot_general x6 -> x1, matrix products: 14.5 us -> 2.58 us  [on_device(): jnp.dot(ready, weight_out, preferred_element_type=F32).astype(BF16)]
    pallas_call x0 -> x5, Pallas kernels: none -> 9.1 us  [product(): pl.pallas_call(functools.partial(product_kernel, turned), grid_spec=pltpu...]
    ppermute x20 -> x19, waiting for transfers between devices: 54.5 us -> 46.8 us  [move(): lax.ppermute(block, axis, [(i, (i + hops) % size) for i in range(size)])]
    unnamed x31 -> x30, local copies, waits for them, and re-layouts: 4.29 us -> 10.1 us
    all_to_all x3 -> x2, starting transfers between devices: 21.9 us -> 17.4 us  [rows_sum(): pieces = lax.all_to_all(partial.reshape(peers, rows, -1), FAR, 0, 0)]
    all_gather x0 -> x2, waiting for transfers between devices: none -> 4.35 us  [the longest x1 4.33 us: on_device(): grad_all = lax.all_gather(both[:, features:], 'y', axis=0, tiled=True)]
    ppermute x20 -> x19, starting transfers between devices: 37.9 us -> 33.7 us  [move(): lax.ppermute(block, axis, [(i, (i + hops) % size) for i in range(size)])]
  transfers between devices with their start and end apart: 23 -> 23, of which waited for: 13 -> 15; matrix products, arithmetic and copies ran while one was open for 13% -> 9% of each run, Pallas kernels for 0% -> 4%
where the time goes in v2:
time: 207 us; the launch traced here: 206 us
  waiting for transfers between devices  81.3 us (39%)
  starting transfers between devices  51.2 us (25%)
  blocking collectives  17.1 us (8%)
  between operations  14.5 us (7%)
  local copies, waits for them, and re-layouts  14.1 us (7%)
  other arithmetic  9.9 us (5%)
  Pallas kernels  9.1 us (4%)
  matrix products  9.03 us (4%)
    ppermute x19, waiting for transfers between devices, move(): lax.ppermute(block, axis, [(i, (i + hops) % size) for i in range(size)])  46.8 us
    ppermute x19, starting transfers between devices, move(): lax.ppermute(block, axis, [(i, (i + hops) % size) for i in range(size)])  33.7 us
    all_to_all x2, waiting for transfers between devices, rows_sum(): pieces = lax.all_to_all(partial.reshape(peers, rows, -1), FAR, 0, 0)  30.1 us
    all_to_all x2, starting transfers between devices, rows_sum(): pieces = lax.all_to_all(partial.reshape(peers, rows, -1), FAR, 0, 0)  17.4 us
    all_to_all x1, blocking collectives, on_device(): lax.all_to_all(jnp.broadcast_to(both[None], (near,) + both.shape), NEAR,...  17.1 us
    unnamed x30, local copies, waits for them, and re-layouts  10.1 us
    pallas_call x5, Pallas kernels, product(): pl.pallas_call(functools.partial(product_kernel, turned), grid_spec=pltpu...  9.1 us
    dot_general x2, matrix products, across(): lax.dot_general(left, right, (((0,), (0,)), ((), ())), preferred_element_...  6.45 us
  transfers between devices with their start and end apart: 23, of which 15 were waited for; matrix products, arithmetic and copies ran while one was open for 9% of the time, Pallas kernels for 4%

profile of v2, /device:TPU:2, one launch (start us, length us, event | category | flops | bytes accessed | tf_op | source)
XLA Modules:
  0.0 206.2 jit_solution(5319954972288693140)
XLA Ops:
  7.2 0.8 pad_maximum_fusion.5
  8.1 17.1 %all_to_all.15 = bf16[8,32,1536]{2,1,0:T(8,128)(2,1)S(1)} all-to-all(bf16[8,32,1536]{2,1,0:T(8,128)(2,1)S(1)} %broadcast_in_dim.33), channel_id=1, replica_groups=mesh['x'=4,'y'=4,'l'=2,'h'=4,'c'=2] {'x','l'}, dimensions={0} | all-to-all | bytes 1572864 | tf_op jit(solution)/shard_map/all_to_all | solution.py:121
  25.2 0.8 fusion.28
  26.1 1.7 collective-permute-start
  27.7 1.7 collective-permute-start.1
  29.6 7.1 %collective-permute-done = bf16[256,768]{1,0:T(8,128)(2,1)S(1)} collective-permute-done((bf16[256,768]{1,0:T(8,128)(2,1)S(1)}, bf16[256,768]{1,0:T(8,128)(2,1)S(1)}, u32[]{:S(2)}, u32[]{:S(2)}) %collective-permute-start) | collective-permute-done | bytes 393248 | tf_op jit(solution)/shard_map/ppermute | solution.py:32
  36.7 0.4 collective-permute-start.2
  37.1 3.0 %collective-permute-start.3 = (bf16[128,768]{1,0:T(8,128)(2,1)S(1)}, bf16[128,768]{1,0:T(8,128)(2,1)S(1)}, u32[]{:S(2)}, u32[]{:S(2)}) collective-permute-start(bf16[128,768]{1,0:T(8,128)(2,1)S(1)} %slice.126), channel_id=1, source_target_pairs={{0,48},{16,0},{32,16},{48,32},{1,49},{17,1},{33,17},{49,33},{2,50}... | collective-permute-start | bytes 589832 | tf_op jit(solution)/shard_map/ppermute | solution.py:32
  40.2 3.5 %collective-permute-done.2 = bf16[128,768]{1,0:T(8,128)(2,1)S(1)} collective-permute-done((bf16[128,768]{1,0:T(8,128)(2,1)S(1)}, bf16[128,768]{1,0:T(8,128)(2,1)S(1)}, u32[]{:S(2)}, u32[]{:S(2)}) %collective-permute-start.2) | collective-permute-done | bytes 196640 | tf_op jit(solution)/shard_map/ppermute | solution.py:32
  43.7 3.6 %collective-permute-done.3 = bf16[128,768]{1,0:T(8,128)(2,1)S(1)} collective-permute-done((bf16[128,768]{1,0:T(8,128)(2,1)S(1)}, bf16[128,768]{1,0:T(8,128)(2,1)S(1)}, u32[]{:S(2)}, u32[]{:S(2)}) %collective-permute-start.3) | collective-permute-done | bytes 196640 | tf_op jit(solution)/shard_map/ppermute | solution.py:32
  47.3 1.3 shard_map.76
  48.8 1.3 copy-done.8
  50.1 1.3 shard_map.75
  51.4 1.2 copy-done.2
  52.6 4.3 %all-gather.3.cloned.1.call-done.rows_ref = bf16[1024,768]{1,0:T(8,128)(2,1)} async-done(((bf16[256,768]{1,0:T(8,128)(2,1)}), bf16[1024,768]{1,0:T(8,128)(2,1)}) %all-gather.3.cloned.1.call-update) | async-done | bytes 1572880 | tf_op jit(solution)/shard_map/all_gather | solution.py:123
  56.9 1.4 copy-done
  58.3 2.2 %shard_map.78 = bf16[512,768]{1,0:T(8,128)(2,1)S(1)} custom-call(s32[1]{0:T(128)} %bitcast.8.which_ref, bf16[1024,768]{1,0:T(8,128)(2,1)S(1)} %copy-done, bf16[768,768]{1,0:T(8,128)(2,1)S(1)} %copy-done.4), custom_call_target="tpu_custom_call" | custom-call | flops 603979776 | bytes 3538944 | tf_op jit(solution)/shard_map/pallas_call | solution.py:81
  60.7 1.4 convert_add_fusion.1
  62.1 3.1 %collective-permute-start.5 = (bf16[64,768]{1,0:T(8,128)(2,1)S(1)}, bf16[64,768]{1,0:T(8,128)(2,1)S(1)}, u32[]{:S(2)}, u32[]{:S(2)}) collective-permute-start(bf16[64,768]{1,0:T(8,128)(2,1)S(1)} %get-tuple-element.27), channel_id=1, source_target_pairs={{0,2},{2,4},{4,6},{6,0},{1,3},{3,5},{5,7},{7,1},{8,10},{10,12},{12... | collective-permute-start | bytes 294920 | tf_op jit(solution)/shard_map/ppermute | solution.py:32
  65.2 2.2 %collective-permute-start.7 = (bf16[64,768]{1,0:T(8,128)(2,1)S(1)}, bf16[64,768]{1,0:T(8,128)(2,1)S(1)}, u32[]{:S(2)}, u32[]{:S(2)}) collective-permute-start(bf16[64,768]{1,0:T(8,128)(2,1)S(1)} %get-tuple-element.28), channel_id=1, source_target_pairs={{0,6},{2,0},{4,2},{6,4},{1,7},{3,1},{5,3},{7,5},{8,14},{10,8},{12,... | collective-permute-start | bytes 294920 | tf_op jit(solution)/shard_map/ppermute | solution.py:32
  67.5 2.2 %shard_map.77 = f32[512,768]{1,0:T(8,128)S(1)} custom-call(s32[1]{0:T(128)} %bitcast.which_ref, bf16[1024,768]{1,0:T(8,128)(2,1)S(1)} %copy-done.1, bf16[768,768]{1,0:T(8,128)(2,1)S(1)} %copy-done.5), custom_call_target="tpu_custom_call" | custom-call | flops 603979776 | bytes 3538944 | tf_op jit(solution)/shard_map/pallas_call | solution.py:81
  69.7 0.2 convert_add_fusion
  70.0 1.4 collective-permute-start.15
  71.4 2.8 %collective-permute-start.17 = (bf16[64,768]{1,0:T(8,128)(2,1)S(1)}, bf16[64,768]{1,0:T(8,128)(2,1)S(1)}, u32[]{:S(2)}, u32[]{:S(2)}) collective-permute-start(bf16[64,768]{1,0:T(8,128)(2,1)S(1)} %get-tuple-element.26), channel_id=1, source_target_pairs={{0,6},{2,0},{4,2},{6,4},{1,7},{3,1},{5,3},{7,5},{8,14},{10,8},{12,... | collective-permute-start | bytes 294920 | tf_op jit(solution)/shard_map/ppermute | solution.py:32
  74.2 3.0 %collective-permute-done.15 = bf16[64,768]{1,0:T(8,128)(2,1)S(1)} collective-permute-done((bf16[64,768]{1,0:T(8,128)(2,1)S(1)}, bf16[64,768]{1,0:T(8,128)(2,1)S(1)}, u32[]{:S(2)}, u32[]{:S(2)}) %collective-permute-start.15) | collective-permute-done | bytes 98336 | tf_op jit(solution)/shard_map/ppermute | solution.py:32
  77.3 3.0 %collective-permute-done.17 = bf16[64,768]{1,0:T(8,128)(2,1)S(1)} collective-permute-done((bf16[64,768]{1,0:T(8,128)(2,1)S(1)}, bf16[64,768]{1,0:T(8,128)(2,1)S(1)}, u32[]{:S(2)}, u32[]{:S(2)}) %collective-permute-start.17) | collective-permute-done | bytes 98336 | tf_op jit(solution)/shard_map/ppermute | solution.py:32
  80.4 4.1 %collective-permute-start.16 = (bf16[128,768]{1,0:T(8,128)(2,1)S(1)}, bf16[128,768]{1,0:T(8,128)(2,1)S(1)}, u32[]{:S(2)}, u32[]{:S(2)}) collective-permute-start(bf16[128,768]{1,0:T(8,128)(2,1)S(1)} %pad_maximum_fusion.3), channel_id=1, source_target_pairs={{0,2},{2,4},{4,6},{6,0},{1,3},{3,5},{5,7},{7,1},{8,10},{10,12},{12... | collective-permute-start | bytes 589832 | tf_op jit(solution)/shard_map/ppermute | solution.py:32
  84.6 0.2 collective-permute-start.18
  84.7 3.1 %collective-permute-start.6 = (bf16[128,768]{1,0:T(8,128)(2,1)S(1)}, bf16[128,768]{1,0:T(8,128)(2,1)S(1)}, u32[]{:S(2)}, u32[]{:S(2)}) collective-permute-start(bf16[128,768]{1,0:T(8,128)(2,1)S(1)} %pad_maximum_fusion.1), channel_id=1, source_target_pairs={{0,2},{2,4},{4,6},{6,0},{1,3},{3,5},{5,7},{7,1},{8,10},{10,12},{12... | collective-permute-start | bytes 589832 | tf_op jit(solution)/shard_map/ppermute | solution.py:32
  87.8 1.4 collective-permute-start.8
  89.2 3.7 %collective-permute-done.16 = bf16[128,768]{1,0:T(8,128)(2,1)S(1)} collective-permute-done((bf16[128,768]{1,0:T(8,128)(2,1)S(1)}, bf16[128,768]{1,0:T(8,128)(2,1)S(1)}, u32[]{:S(2)}, u32[]{:S(2)}) %collective-permute-start.16) | collective-permute-done | bytes 196640 | tf_op jit(solution)/shard_map/ppermute | solution.py:32
  93.0 6.5 %collective-permute-done.18 = bf16[128,768]{1,0:T(8,128)(2,1)S(1)} collective-permute-done((bf16[128,768]{1,0:T(8,128)(2,1)S(1)}, bf16[128,768]{1,0:T(8,128)(2,1)S(1)}, u32[]{:S(2)}, u32[]{:S(2)}) %collective-permute-start.18) | collective-permute-done | bytes 196640 | tf_op jit(solution)/shard_map/ppermute | solution.py:32
  99.5 2.8 %collective-permute-done.8 = bf16[128,768]{1,0:T(8,128)(2,1)S(1)} collective-permute-done((bf16[128,768]{1,0:T(8,128)(2,1)S(1)}, bf16[128,768]{1,0:T(8,128)(2,1)S(1)}, u32[]{:S(2)}, u32[]{:S(2)}) %collective-permute-start.8) | collective-permute-done | bytes 196640 | tf_op jit(solution)/shard_map/ppermute | solution.py:32
  102.4 0.2 bitcast_dynamic-update-slice_fusion.5
  102.6 0.9 copy-done.13
  103.5 0.9 fusion.11
  104.4 2.8 %collective-permute-start.9 = (bf16[128,768]{1,0:T(8,128)(2,1)S(1)}, bf16[128,768]{1,0:T(8,128)(2,1)S(1)}, u32[]{:S(2)}, u32[]{:S(2)}) collective-permute-start(bf16[128,768]{1,0:T(8,128)(2,1)S(1)} %get-tuple-element.11), channel_id=1, source_target_pairs={{0,2},{2,4},{4,6},{6,0},{1,3},{3,5},{5,7},{7,1},{8,10},{10,12},{12... | collective-permute-start | bytes 589832 | tf_op jit(solution)/shard_map/ppermute | solution.py:32
  107.2 1.5 collective-permute-start.10
  108.6 6.4 %collective-permute-done.9 = bf16[128,768]{1,0:T(8,128)(2,1)S(1)} collective-permute-done((bf16[128,768]{1,0:T(8,128)(2,1)S(1)}, bf16[128,768]{1,0:T(8,128)(2,1)S(1)}, u32[]{:S(2)}, u32[]{:S(2)}) %collective-permute-start.9) | collective-permute-done | bytes 196640 | tf_op jit(solution)/shard_map/ppermute | solution.py:32
  115.0 1.8 collective-permute-start.11
  116.8 2.5 %collective-permute-start.12 = (bf16[64,768]{1,0:T(8,128)(2,1)S(1)}, bf16[64,768]{1,0:T(8,128)(2,1)S(1)}, u32[]{:S(2)}, u32[]{:S(2)}) collective-permute-start(bf16[64,768]{1,0:T(8,128)(2,1)S(1)} %slice.130), channel_id=1, source_target_pairs={{0,6},{2,0},{4,2},{6,4},{1,7},{3,1},{5,3},{7,5},{8,14},{10,8},{12,... | collective-permute-start | bytes 294920 | tf_op jit(solution)/shard_map/ppermute | solution.py:32
  119.3 0.7 bitcast_dynamic-update-slice_fusion.4
  120.0 0.7 bitcast_dynamic-update-slice_fusion.3
  120.7 2.2 %collective-permute-done.11 = bf16[64,768]{1,0:T(8,128)(2,1)S(1)} collective-permute-done((bf16[64,768]{1,0:T(8,128)(2,1)S(1)}, bf16[64,768]{1,0:T(8,128)(2,1)S(1)}, u32[]{:S(2)}, u32[]{:S(2)}) %collective-permute-start.11) | collective-permute-done | bytes 98336 | tf_op jit(solution)/shard_map/ppermute | solution.py:32
  122.9 0.6 bitcast_dynamic-update-slice_fusion.9
  123.5 2.3 %collective-permute-done.12 = bf16[64,768]{1,0:T(8,128)(2,1)S(1)} collective-permute-done((bf16[64,768]{1,0:T(8,128)(2,1)S(1)}, bf16[64,768]{1,0:T(8,128)(2,1)S(1)}, u32[]{:S(2)}, u32[]{:S(2)}) %collective-permute-start.12) | collective-permute-done | bytes 98336 | tf_op jit(solution)/shard_map/ppermute | solution.py:32
  125.8 0.6 bitcast_dynamic-update-slice_fusion.8
  126.5 2.6 %collective-permute-done.13 = bf16[4,1,128,768]{3,2,1,0:T(8,128)(2,1)} collective-permute-done((bf16[4,1,128,768]{3,2,1,0:T(8,128)(2,1)}, bf16[4,1,128,768]{3,2,1,0:T(8,128)(2,1)}, u32[]{:S(2)}, u32[]{:S(2)}) %collective-permute-start.13) | collective-permute-done | bytes 786464 | tf_op jit(solution)/shard_map/ppermute | solution.py:32
  129.1 1.5 broadcast_select_fusion.1
  130.6 0.1 pad_maximum_fusion
  130.8 1.6 copy-done.6
  132.3 2.6 %convolution_convert_fusion = bf16[1024,768]{1,0:T(8,128)(2,1)} fusion(bf16[1024,768]{1,0:T(8,128)(2,1)S(1)} %bitcast.98, bf16[768,768]{1,0:T(8,128)(2,1)S(1)} %copy-done.6), kind=kOutput, calls=%fused_computation | convolution fusion | flops 1208745984 | bytes 4325376 | tf_op jit(solution)/shard_map/dot_general | solution.py:140
  134.9 11.7 %all-to-all-start.1 = ((bf16[32,32,768]{2,1,0:T(8,128)(2,1)}), bf16[32,32,768]{2,1,0:T(8,128)(2,1)}, u32[]{:S(2)}, u32[]{:S(2)}) async-start(bf16[32,32,768]{2,1,0:T(8,128)(2,1)} %bitcast.100), calls=%async_computation.1 | async-start | bytes 3145728 | tf_op jit(solution)/shard_map/all_to_all | solution.py:117
  146.7 1.3 copy-done.9
  148.0 1.4 copy-done.11
  149.4 2.0 shard_map.79
  151.4 1.2 copy-done.10
  152.6 16.9 %all-to-all-done.1 = bf16[32,32,768]{2,1,0:T(8,128)(2,1)} async-done(((bf16[32,32,768]{2,1,0:T(8,128)(2,1)}), bf16[32,32,768]{2,1,0:T(8,128)(2,1)}, u32[]{:S(2)}, u32[]{:S(2)}) %all-to-all-start.1) | async-done | bytes 1572896 | tf_op jit(solution)/shard_map/all_to_all | solution.py:117
  169.5 5.7 %all-to-all-start.2 = ((bf16[32,32,768]{2,1,0:T(8,128)(2,1)}), bf16[32,32,768]{2,1,0:T(8,128)(2,1)}, u32[]{:S(2)}, u32[]{:S(2)}) async-start(bf16[32,32,768]{2,1,0:T(8,128)(2,1)} %bitcast.87), calls=%async_computation.2 | async-start | bytes 3145728 | tf_op jit(solution)/shard_map/all_to_all | solution.py:117
  175.2 4.0 %convolution_convert_fusion.1 = bf16[768,768]{1,0:T(8,128)(2,1)} fusion(bf16[1024,768]{1,0:T(8,128)(2,1)} %bitcast.99, bf16[1024,768]{1,0:T(8,128)(2,1)S(1)} %copy-done.1), kind=kOutput, calls=%fused_computation.4 | convolution fusion | flops 1208549376 | bytes 4325376 | tf_op jit(solution)/shard_map/dot_general | solution.py:27
  179.1 2.5 %convolution_convert_fusion.2 = bf16[768,768]{1,0:T(8,128)(2,1)} fusion(bf16[1024,768]{1,0:T(8,128)(2,1)S(1)} %bitcast.86, bf16[1024,768]{1,0:T(8,128)(2,1)S(1)} %copy-done.12), kind=kOutput, calls=%fused_computation.5 | convolution fusion | flops 1208549376 | bytes 4325376 | tf_op jit(solution)/shard_map/dot_general | solution.py:27
  181.6 2.3 %reduce_sum.24 = bf16[32,768]{1,0:T(8,128)(2,1)} reduce(bf16[32,32,768]{2,1,0:T(8,128)(2,1)} %all-to-all-done.1, bf16[]{:T(256)} %constant.121.clone.1), dimensions={0}, to_apply=%region_0.1 | reduce | flops 761856 | bytes 1622018 | tf_op jit(solution)/shard_map/reduce_sum | solution.py:118
  183.9 13.3 %all-to-all-done.2 = bf16[32,32,768]{2,1,0:T(8,128)(2,1)} async-done(((bf16[32,32,768]{2,1,0:T(8,128)(2,1)}), bf16[32,32,768]{2,1,0:T(8,128)(2,1)}, u32[]{:S(2)}, u32[]{:S(2)}) %all-to-all-start.2) | async-done | bytes 1572896 | tf_op jit(solution)/shard_map/all_to_all | solution.py:117
  197.1 2.3 %reduce_sum.25 = bf16[32,768]{1,0:T(8,128)(2,1)} reduce(bf16[32,32,768]{2,1,0:T(8,128)(2,1)} %all-to-all-done.2, bf16[]{:T(256)} %constant.121.clone.1), dimensions={0}, to_apply=%region_1.2 | reduce | flops 761856 | bytes 1622018 | tf_op jit(solution)/shard_map/reduce_sum | solution.py:118
  (61 shorter events, 1.1 us)
Async XLA Ops:
  7.2 49.8 %all-gather.3.cloned.1.call-start = ((), (), s32[]{:S(2)}) async-start(), calls=%async_computation.3 | async-start | bytes 1966080 | tf_op jit(solution)/shard_map/all_gather | solution.py:123
  26.0 120.7 %all-gather.5.cloned.1.call-start = ((), (), s32[]{:S(2)}) async-start(), calls=%async_computation.4 | async-start | bytes 1769472 | tf_op jit(solution)/shard_map/all_gather | solution.py:137
  26.1 10.6 %collective-permute-start = (bf16[256,768]{1,0:T(8,128)(2,1)S(1)}, bf16[256,768]{1,0:T(8,128)(2,1)S(1)}, u32[]{:S(2)}, u32[]{:S(2)}) collective-permute-start(bf16[256,768]{1,0:T(8,128)(2,1)S(1)} %get-tuple-element.24), channel_id=1, source_target_pairs={{0,16},{16,32},{32,48},{48,0},{1,17},{17,33},{33,49},{49,1},{2,18}... | collective-permute-start | bytes 1179656 | tf_op jit(solution)/shard_map/ppermute | solution.py:32
  27.7 9.3 %collective-permute-start.1 = (bf16[256,768]{1,0:T(8,128)(2,1)S(1)}, bf16[256,768]{1,0:T(8,128)(2,1)S(1)}, u32[]{:S(2)}, u32[]{:S(2)}) collective-permute-start(bf16[256,768]{1,0:T(8,128)(2,1)S(1)} %get-tuple-element.24), channel_id=1, source_target_pairs={{0,48},{16,0},{32,16},{48,32},{1,49},{17,1},{33,17},{49,33},{2,50}... | collective-permute-start | bytes 1179656 | tf_op jit(solution)/shard_map/ppermute | solution.py:32
  29.5 17.7 %copy-start.7 = (bf16[768,768]{1,0:T(8,128)(2,1)S(1)}, bf16[768,768]{1,0:T(8,128)(2,1)}, u32[]{:S(2)}) copy-start(bf16[768,768]{1,0:T(8,128)(2,1)} %weight_ref.9) | copy-start | bytes 3538948
  36.7 7.0 %collective-permute-start.2 = (bf16[128,768]{1,0:T(8,128)(2,1)S(1)}, bf16[128,768]{1,0:T(8,128)(2,1)S(1)}, u32[]{:S(2)}, u32[]{:S(2)}) collective-permute-start(bf16[128,768]{1,0:T(8,128)(2,1)S(1)} %slice.125), channel_id=1, source_target_pairs={{0,16},{16,32},{32,48},{48,0},{1,17},{17,33},{33,49},{49,1},{2,18}... | collective-permute-start | bytes 589832 | tf_op jit(solution)/shard_map/ppermute | solution.py:32
  37.1 10.2 %collective-permute-start.3 = (bf16[128,768]{1,0:T(8,128)(2,1)S(1)}, bf16[128,768]{1,0:T(8,128)(2,1)S(1)}, u32[]{:S(2)}, u32[]{:S(2)}) collective-permute-start(bf16[128,768]{1,0:T(8,128)(2,1)S(1)} %slice.126), channel_id=1, source_target_pairs={{0,48},{16,0},{32,16},{48,32},{1,49},{17,1},{33,17},{49,33},{2,50}... | collective-permute-start | bytes 589832 | tf_op jit(solution)/shard_map/ppermute | solution.py:32
  48.7 12.0 %collective-permute-start.4 = (bf16[512,768]{1,0:T(8,128)(2,1)S(1)}, bf16[512,768]{1,0:T(8,128)(2,1)}, u32[]{:S(2)}, u32[]{:S(2)}) collective-permute-start(bf16[512,768]{1,0:T(8,128)(2,1)S(1)} %shard_map.76), channel_id=1, source_target_pairs={{0,1},{1,0},{2,3},{3,2},{4,5},{5,4},{6,7},{7,6},{8,9},{9,8},{10,11... | collective-permute-start | bytes 2359304 | tf_op jit(solution)/shard_map/ppermute | solution.py:32
  48.8 1.3 copy-start.8
  50.1 6.8 %copy-start.4 = (bf16[768,768]{1,0:T(8,128)(2,1)S(1)}, bf16[768,768]{1,0:T(8,128)(2,1)}, u32[]{:S(2)}) copy-start(bf16[768,768]{1,0:T(8,128)(2,1)} %weight_ref.8) | copy-start | bytes 3538948
  51.4 1.2 copy-start.2
  56.9 1.4 copy-start
  58.3 2.3 %copy-start.3 = (f32[512,768]{1,0:T(8,128)S(1)}, f32[512,768]{1,0:T(8,128)}, u32[]{:S(2)}) copy-start(f32[512,768]{1,0:T(8,128)} %copy-done.2) | copy-start | bytes 4718596
  60.5 9.2 %collective-permute-start.14 = (bf16[512,768]{1,0:T(8,128)(2,1)S(1)}, bf16[512,768]{1,0:T(8,128)(2,1)S(1)}, u32[]{:S(2)}, u32[]{:S(2)}) collective-permute-start(bf16[512,768]{1,0:T(8,128)(2,1)S(1)} %shard_map.78), channel_id=1, source_target_pairs={{0,1},{1,0},{2,3},{3,2},{4,5},{5,4},{6,7},{7,6},{8,9},{9,8},{10,11... | collective-permute-start | bytes 2359304 | tf_op jit(solution)/shard_map/ppermute | solution.py:32
  60.7 6.8 %copy-start.1 = (bf16[1024,768]{1,0:T(8,128)(2,1)S(1)}, bf16[1024,768]{1,0:T(8,128)(2,1)}, u32[]{:S(2)}) copy-start(bf16[1024,768]{1,0:T(8,128)(2,1)} %all-gather.3.cloned.1.call-done.rows_ref) | copy-start | bytes 4718596
  62.1 5.4 %copy-start.5 = (bf16[768,768]{1,0:T(8,128)(2,1)S(1)}, bf16[768,768]{1,0:T(8,128)(2,1)}, u32[]{:S(2)}) copy-start(bf16[768,768]{1,0:T(8,128)(2,1)} %weight_ref.8) | copy-start | bytes 3538948
  62.1 12.1 %collective-permute-start.5 = (bf16[64,768]{1,0:T(8,128)(2,1)S(1)}, bf16[64,768]{1,0:T(8,128)(2,1)S(1)}, u32[]{:S(2)}, u32[]{:S(2)}) collective-permute-start(bf16[64,768]{1,0:T(8,128)(2,1)S(1)} %get-tuple-element.27), channel_id=1, source_target_pairs={{0,2},{2,4},{4,6},{6,0},{1,3},{3,5},{5,7},{7,1},{8,10},{10,12},{12... | collective-permute-start | bytes 294920 | tf_op jit(solution)/shard_map/ppermute | solution.py:32
  65.2 9.0 %collective-permute-start.7 = (bf16[64,768]{1,0:T(8,128)(2,1)S(1)}, bf16[64,768]{1,0:T(8,128)(2,1)S(1)}, u32[]{:S(2)}, u32[]{:S(2)}) collective-permute-start(bf16[64,768]{1,0:T(8,128)(2,1)S(1)} %get-tuple-element.28), channel_id=1, source_target_pairs={{0,6},{2,0},{4,2},{6,4},{1,7},{3,1},{5,3},{7,5},{8,14},{10,8},{12,... | collective-permute-start | bytes 294920 | tf_op jit(solution)/shard_map/ppermute | solution.py:32
  70.0 7.3 %collective-permute-start.15 = (bf16[64,768]{1,0:T(8,128)(2,1)S(1)}, bf16[64,768]{1,0:T(8,128)(2,1)S(1)}, u32[]{:S(2)}, u32[]{:S(2)}) collective-permute-start(bf16[64,768]{1,0:T(8,128)(2,1)S(1)} %get-tuple-element.25), channel_id=1, source_target_pairs={{0,2},{2,4},{4,6},{6,0},{1,3},{3,5},{5,7},{7,1},{8,10},{10,12},{12... | collective-permute-start | bytes 294920 | tf_op jit(solution)/shard_map/ppermute | solution.py:32
  71.4 8.9 %collective-permute-start.17 = (bf16[64,768]{1,0:T(8,128)(2,1)S(1)}, bf16[64,768]{1,0:T(8,128)(2,1)S(1)}, u32[]{:S(2)}, u32[]{:S(2)}) collective-permute-start(bf16[64,768]{1,0:T(8,128)(2,1)S(1)} %get-tuple-element.26), channel_id=1, source_target_pairs={{0,6},{2,0},{4,2},{6,4},{1,7},{3,1},{5,3},{7,5},{8,14},{10,8},{12,... | collective-permute-start | bytes 294920 | tf_op jit(solution)/shard_map/ppermute | solution.py:32
  80.4 12.5 %collective-permute-start.16 = (bf16[128,768]{1,0:T(8,128)(2,1)S(1)}, bf16[128,768]{1,0:T(8,128)(2,1)S(1)}, u32[]{:S(2)}, u32[]{:S(2)}) collective-permute-start(bf16[128,768]{1,0:T(8,128)(2,1)S(1)} %pad_maximum_fusion.3), channel_id=1, source_target_pairs={{0,2},{2,4},{4,6},{6,0},{1,3},{3,5},{5,7},{7,1},{8,10},{10,12},{12... | collective-permute-start | bytes 589832 | tf_op jit(solution)/shard_map/ppermute | solution.py:32
  84.6 14.9 %collective-permute-start.18 = (bf16[128,768]{1,0:T(8,128)(2,1)S(1)}, bf16[128,768]{1,0:T(8,128)(2,1)S(1)}, u32[]{:S(2)}, u32[]{:S(2)}) collective-permute-start(bf16[128,768]{1,0:T(8,128)(2,1)S(1)} %pad_maximum_fusion.4), channel_id=1, source_target_pairs={{0,6},{2,0},{4,2},{6,4},{1,7},{3,1},{5,3},{7,5},{8,14},{10,8},{12,... | collective-permute-start | bytes 589832 | tf_op jit(solution)/shard_map/ppermute | solution.py:32
  84.7 14.8 %collective-permute-start.6 = (bf16[128,768]{1,0:T(8,128)(2,1)S(1)}, bf16[128,768]{1,0:T(8,128)(2,1)S(1)}, u32[]{:S(2)}, u32[]{:S(2)}) collective-permute-start(bf16[128,768]{1,0:T(8,128)(2,1)S(1)} %pad_maximum_fusion.1), channel_id=1, source_target_pairs={{0,2},{2,4},{4,6},{6,0},{1,3},{3,5},{5,7},{7,1},{8,10},{10,12},{12... | collective-permute-start | bytes 589832 | tf_op jit(solution)/shard_map/ppermute | solution.py:32
  87.8 14.5 %collective-permute-start.8 = (bf16[128,768]{1,0:T(8,128)(2,1)S(1)}, bf16[128,768]{1,0:T(8,128)(2,1)S(1)}, u32[]{:S(2)}, u32[]{:S(2)}) collective-permute-start(bf16[128,768]{1,0:T(8,128)(2,1)S(1)} %pad_maximum_fusion.2), channel_id=1, source_target_pairs={{0,6},{2,0},{4,2},{6,4},{1,7},{3,1},{5,3},{7,5},{8,14},{10,8},{12,... | collective-permute-start | bytes 589832 | tf_op jit(solution)/shard_map/ppermute | solution.py:32
  102.6 0.9 copy-start.13
  104.4 10.6 %collective-permute-start.9 = (bf16[128,768]{1,0:T(8,128)(2,1)S(1)}, bf16[128,768]{1,0:T(8,128)(2,1)S(1)}, u32[]{:S(2)}, u32[]{:S(2)}) collective-permute-start(bf16[128,768]{1,0:T(8,128)(2,1)S(1)} %get-tuple-element.11), channel_id=1, source_target_pairs={{0,2},{2,4},{4,6},{6,0},{1,3},{3,5},{5,7},{7,1},{8,10},{10,12},{12... | collective-permute-start | bytes 589832 | tf_op jit(solution)/shard_map/ppermute | solution.py:32
  107.2 9.7 %collective-permute-start.10 = (bf16[128,768]{1,0:T(8,128)(2,1)S(1)}, bf16[128,768]{1,0:T(8,128)(2,1)S(1)}, u32[]{:S(2)}, u32[]{:S(2)}) collective-permute-start(bf16[128,768]{1,0:T(8,128)(2,1)S(1)} %get-tuple-element.11), channel_id=1, source_target_pairs={{0,6},{2,0},{4,2},{6,4},{1,7},{3,1},{5,3},{7,5},{8,14},{10,8},{12,... | collective-permute-start | bytes 589832 | tf_op jit(solution)/shard_map/ppermute | solution.py:32
  115.0 7.9 %collective-permute-start.11 = (bf16[64,768]{1,0:T(8,128)(2,1)S(1)}, bf16[64,768]{1,0:T(8,128)(2,1)S(1)}, u32[]{:S(2)}, u32[]{:S(2)}) collective-permute-start(bf16[64,768]{1,0:T(8,128)(2,1)S(1)} %slice.129), channel_id=1, source_target_pairs={{0,2},{2,4},{4,6},{6,0},{1,3},{3,5},{5,7},{7,1},{8,10},{10,12},{12... | collective-permute-start | bytes 294920 | tf_op jit(solution)/shard_map/ppermute | solution.py:32
  116.8 9.0 %collective-permute-start.12 = (bf16[64,768]{1,0:T(8,128)(2,1)S(1)}, bf16[64,768]{1,0:T(8,128)(2,1)S(1)}, u32[]{:S(2)}, u32[]{:S(2)}) collective-permute-start(bf16[64,768]{1,0:T(8,128)(2,1)S(1)} %slice.130), channel_id=1, source_target_pairs={{0,6},{2,0},{4,2},{6,4},{1,7},{3,1},{5,3},{7,5},{8,14},{10,8},{12,... | collective-permute-start | bytes 294920 | tf_op jit(solution)/shard_map/ppermute | solution.py:32
  126.5 2.6 %collective-permute-start.13 = (bf16[4,1,128,768]{3,2,1,0:T(8,128)(2,1)}, bf16[4,1,128,768]{3,2,1,0:T(8,128)(2,1)}, u32[]{:S(2)}, u32[]{:S(2)}) collective-permute-start(bf16[4,1,128,768]{3,2,1,0:T(8,128)(2,1)} %bitcast_dynamic-update-slice_fusion.8), channel_id=1, source_target_pairs={{0,1},{1,0},{2,3},{3,2},{4,5},{5,4},{6,7},{7,6},{8,9},{9,8},{10,11... | collective-permute-start | bytes 2359304 | tf_op jit(solution)/shard_map/ppermute | solution.py:32
  130.6 1.7 copy-start.6
  130.8 4.1 %copy-start.14 = (bf16[4,2,128,768]{3,2,1,0:T(8,128)(2,1)}, bf16[4,2,128,768]{3,2,1,0:T(8,128)(2,1)S(1)}, u32[]{:S(2)}) copy-start(bf16[4,2,128,768]{3,2,1,0:T(8,128)(2,1)S(1)} %pad_maximum_fusion) | copy-start | bytes 4718596
  134.9 34.5 %all-to-all-start.1 = ((bf16[32,32,768]{2,1,0:T(8,128)(2,1)}), bf16[32,32,768]{2,1,0:T(8,128)(2,1)}, u32[]{:S(2)}, u32[]{:S(2)}) async-start(bf16[32,32,768]{2,1,0:T(8,128)(2,1)} %bitcast.100), calls=%async_computation.1 | async-start | bytes 3145728 | tf_op jit(solution)/shard_map/all_to_all | solution.py:117
  146.7 1.3 copy-start.9
  148.0 1.4 copy-start.11
  151.4 1.2 copy-start.10
  169.5 27.7 %all-to-all-start.2 = ((bf16[32,32,768]{2,1,0:T(8,128)(2,1)}), bf16[32,32,768]{2,1,0:T(8,128)(2,1)}, u32[]{:S(2)}, u32[]{:S(2)}) async-start(bf16[32,32,768]{2,1,0:T(8,128)(2,1)} %bitcast.87), calls=%async_computation.2 | async-start | bytes 3145728 | tf_op jit(solution)/shard_map/all_to_all | solution.py:117
  175.1 4.0 %copy-start.12 = (bf16[1024,768]{1,0:T(8,128)(2,1)S(1)}, bf16[1024,768]{1,0:T(8,128)(2,1)}, u32[]{:S(2)}) copy-start(bf16[1024,768]{1,0:T(8,128)(2,1)} %all-gather.5.cloned.1.call-done.rows_ref) | copy-start | bytes 4718596
Sparse Core Ops, SparseCore 0:
  26.1 30.7 all-gather.2
  104.5 32.8 all-gather.4

commit v3 on v2

v3 whole, which is shorter than its diff:
```python
import functools

import jax
import jax.numpy as jnp
from jax import lax
from jax.experimental import pallas as pl
from jax.experimental.pallas import tpu as pltpu
from jax.sharding import Mesh, PartitionSpec as P

F32 = jnp.float32
BF16 = jnp.bfloat16
NEAR = ("x", "l")
FAR = ("y", "x", "l")
VMEM = 32 * 2**20


def gelu_both(value):
    inner = 0.7978845608 * (value + 0.044715 * value * value * value)
    tangent = jnp.tanh(inner)
    slope = 0.5 * (1.0 + tangent) + 0.5 * value * (1.0 - tangent * tangent) * 0.7978845608 * (
        1.0 + 0.134145 * value * value
    )
    return 0.5 * value * (1.0 + tangent), slope


def across(left, right):
    return lax.dot_general(left, right, (((0,), (0,)), ((), ())), preferred_element_type=F32)


def move(block, axis, hops):
    size = lax.axis_size(axis)
    return lax.ppermute(block, axis, [(i, (i + hops) % size) for i in range(size)])


def pick(array, index):
    return lax.dynamic_index_in_dim(array, index, 0, keepdims=False)


def ring_split(blocks, axis):
    spot = lax.axis_index(axis)
    own, ahead, far, behind = (pick(blocks, (spot + d) % 4) for d in range(4))
    return own, ahead, far.astype(BF16), behind


def both_ways(up, down, axis):
    return move(up, axis, 1), move(down, axis, -1)


def add_first(block, part):
    cut = part.shape[0]
    return jnp.concatenate([block[:cut] + part.astype(F32), block[cut:]], 0).astype(BF16)


def add_last(block, part):
    cut = block.shape[0] - part.shape[0]
    return jnp.concatenate([block[:cut], block[cut:] + part.astype(F32)], 0).astype(BF16)


def stack(*parts):
    return jnp.concatenate(parts, 0)


def ring_place(block, up, down, far_up, far_down, axis):
    spot = lax.axis_index(axis)
    cut = far_up.shape[0]
    whole = jnp.zeros((4,) + block.shape, block.dtype)
    for hops, piece in ((0, block), (3, up), (1, down)):
        whole = lax.dynamic_update_index_in_dim(whole, piece, (spot + hops) % 4, 0)
    far = (spot + 2) % 4
    whole = lax.dynamic_update_slice(whole, far_up[None], (far, 0, 0))
    return lax.dynamic_update_slice(whole, far_down[None], (far, cut, 0))


def product_kernel(turned, which_ref, rows_ref, weight_ref, *refs):
    out_ref = refs[-1]
    sides = ((1,), (1,)) if turned else ((1,), (0,))
    out_ref[...] = lax.dot_general(
        rows_ref[...], weight_ref[...], (sides, ((), ())), preferred_element_type=F32
    ).astype(out_ref.dtype)


def product(rows, weight, turned, dtype, tile, which=None, weigh=1, later=()):
    if which is None:
        stride, which = 1, jnp.zeros((1,), jnp.int32)
    else:
        stride, which = 2, which.astype(jnp.int32).reshape(1)
    steps = rows.shape[0] // tile // stride
    width = weight.shape[0] if turned else weight.shape[1]
    return pl.pallas_call(
        functools.partial(product_kernel, turned),
        grid_spec=pltpu.PrefetchScalarGridSpec(
            num_scalar_prefetch=1,
            grid=(steps,),
            in_specs=[
                pl.BlockSpec((tile, rows.shape[1]), lambda i, which: (stride * i + which[0], 0)),
                pl.BlockSpec(weight.shape, lambda i, which: (0, 0)),
            ]
            + [pl.BlockSpec(memory_space=pl.ANY)] * len(later),
            out_specs=pl.BlockSpec((tile, width), lambda i, which: (i, 0)),
        ),
        out_shape=jax.ShapeDtypeStruct((steps * tile, width), dtype),
        compiler_params=pltpu.CompilerParams(vmem_limit_bytes=VMEM),
        cost_estimate=pl.CostEstimate(
            flops=2 * weigh * steps * tile * weight.size,
            bytes_accessed=2 * (steps * tile * rows.shape[1] + weight.size) + 4 * steps * tile * width,
            transcendentals=0,
        ),
    )(which, rows, weight, *later)


def joined_kernel(turned, place_ref, mine_ref, other_ref, weight_ref, *refs):
    out_ref, rows_ref = refs[-2:]
    sides = ((1,), (1,)) if turned else ((1,), (0,))
    rows_ref[...] = jnp.where(pl.program_id(0) % 2 == 0, mine_ref[...], other_ref[...])
    out_ref[...] = lax.dot_general(
        rows_ref[...], weight_ref[...], (sides, ((), ())), preferred_element_type=F32
    ).astype(out_ref.dtype)


def joined_product(mine, other, weight, turned, place, later=()):
    tile = mine.shape[0] // 4
    width = weight.shape[0] if turned else weight.shape[1]

    def spread(i, place):
        return (place[0] + i // 2) % 4 * 2 + (place[1] + i) % 2, 0

    return pl.pallas_call(
        functools.partial(joined_kernel, turned),
        grid_spec=pltpu.PrefetchScalarGridSpec(
            num_scalar_prefetch=1,
            grid=(8,),
            in_specs=[pl.BlockSpec((tile, mine.shape[1]), lambda i, place: (i // 2, 0))] * 2
            + [pl.BlockSpec(weight.shape, lambda i, place: (0, 0))]
            + [pl.BlockSpec(memory_space=pl.ANY)] * len(later),
            out_specs=[pl.BlockSpec((tile, width), spread), pl.BlockSpec((tile, mine.shape[1]), spread)],
        ),
        out_shape=[
            jax.ShapeDtypeStruct((8 * tile, width), BF16),
            jax.ShapeDtypeStruct((8 * tile, mine.shape[1]), BF16),
        ],
        compiler_params=pltpu.CompilerParams(vmem_limit_bytes=VMEM),
        cost_estimate=pl.CostEstimate(
            flops=16 * tile * weight.size,
            bytes_accessed=2 * (2 * mine.size + weight.size) + 16 * tile * (width + mine.shape[1]),
            transcendentals=0,
        ),
    )(place, mine, other, weight, *later)


def local(kernel, outs, args, later=()):
    def body(*refs):
        kernel(*refs[: len(args)], *refs[len(args) + len(later) :])

    return pl.pallas_call(
        body,
        in_specs=[pl.BlockSpec(memory_space=pltpu.VMEM)] * len(args) + [pl.BlockSpec(memory_space=pl.ANY)] * len(later),
        out_specs=[pl.BlockSpec(memory_space=pltpu.VMEM)] * len(outs),
        out_shape=outs,
        compiler_params=pltpu.CompilerParams(vmem_limit_bytes=VMEM),
    )(*args, *later)


def pass_on(ahead_ref, up_ref, behind_ref, down_ref, up_out, down_out):
    cut = up_ref.shape[0]
    up_out[:cut] = (ahead_ref[:cut] + up_ref[...].astype(F32)).astype(BF16)
    up_out[cut:] = ahead_ref[cut:].astype(BF16)
    down_out[:cut] = behind_ref[:cut].astype(BF16)
    down_out[cut:] = (behind_ref[cut:] + down_ref[...].astype(F32)).astype(BF16)


def activate(own_ref, up_ref, down_ref, hidden_ref, slope_ref):
    hidden, slope = gelu_both(own_ref[...] + up_ref[...].astype(F32) + down_ref[...].astype(F32))
    hidden_ref[...] = hidden.astype(BF16)
    slope_ref[...] = slope


def weigh_slope(own_ref, up_ref, down_ref, slope_ref, out_ref):
    total = own_ref[...] + up_ref[...].astype(F32) + down_ref[...].astype(F32)
    out_ref[...] = (total * slope_ref[...]).astype(BF16)


def on_device(inputs, weight_in, weight_out, output_grad):
    core = lax.axis_index("c")
    rows, features = inputs.shape
    near = lax.axis_size(NEAR)
    peers = lax.axis_size(FAR)
    tokens = peers * rows
    ring = lax.axis_size("h")
    tile = tokens // (2 * ring)

    def pair_sum(left, weight, turned, later=(), last=()):
        away = move(product(left, weight, turned, BF16, tile, 1 - core, later=later), "c", 1)
        total = product(left, weight, turned, F32, tile, core, later=last) + away.astype(F32)
        return total.reshape(ring, tile, -1)

    def rows_sum(partial):
        pieces = lax.all_to_all(partial.reshape(peers, rows, -1), FAR, 0, 0)
        return pieces.astype(F32).sum(0).astype(BF16)

    def copies(block, axes):
        size = lax.axis_size(axes)
        sent = jnp.broadcast_to(block[None], (size,) + block.shape)
        return lax.all_to_all(sent, axes, 0, 0).reshape(size * rows, -1)

    def wire(count):
        return jax.ShapeDtypeStruct((count, units), BF16)

    units = weight_in.shape[1]
    cut = tile // 2
    input_all = copies(inputs, FAR)
    output_grad, input_all = lax.optimization_barrier((output_grad, input_all))
    grad = copies(output_grad, NEAR)

    own, ahead, far, behind = ring_split(pair_sum(input_all, weight_in, False), "h")
    up, down = both_ways(far[:cut], far[cut:], "h")
    grad_up, grad_down = both_ways(grad, grad, "y")
    ahead, behind = local(pass_on, [wire(tile)] * 2, (ahead, up, behind, down), (grad_up, grad_down))
    up, down = both_ways(ahead, behind, "h")
    part = grad.shape[0] // 2
    grad_far = both_ways(grad_up[:part], grad_down[part:], "y")
    hidden, slope = local(
        activate, [wire(tile), jax.ShapeDtypeStruct((tile, units), F32)], (own, up, down), grad_far
    )
    grad_all = ring_place(grad, grad_up, grad_down, *grad_far, "y").reshape(tokens, -1)

    up, down = both_ways(hidden, hidden, "h")
    own, ahead, far, behind = ring_split(pair_sum(grad_all, weight_out, True, (hidden,)), "h")
    far_up, far_down = both_ways(stack(far[:cut], up[:cut]), stack(far[cut:], down[cut:]), "h")
    mine = stack(hidden, down, far_up[cut:], far_down[cut:], up)
    other = move(mine, "c", 1)
    ahead, behind = local(pass_on, [wire(tile)] * 2, (ahead, far_up[:cut], behind, far_down[:cut]))
    up, down = both_ways(ahead, behind, "h")
    (grad_pre,) = local(weigh_slope, [wire(tile)], (own, up, down, slope), (other,))
    up, down = both_ways(grad_pre, grad_pre, "h")
    place = jnp.stack([lax.axis_index("h"), core]).astype(jnp.int32)
    partial, hidden_all = joined_product(mine, other, weight_out, False, place)
    far_up, far_down = both_ways(up[:cut], down[cut:], "h")
    partial, far_up, far_down = lax.optimization_barrier((partial, far_up, far_down))
    output = rows_sum(partial)
    mine_late = stack(grad_pre, down, far_up, far_down, up)
    other_late = move(mine_late, "c", 1)
    partial, grad_pre_all = joined_product(mine_late, other_late, weight_in, True, place)
    input_grad = rows_sum(partial)
    weight_out_grad = across(hidden_all, grad_all).astype(BF16)
    weight_in_grad = across(input_all, grad_pre_all).astype(BF16)
    return (output, input_grad, weight_in_grad, weight_out_grad)


def solution(mesh):
    fine = Mesh(mesh.devices.reshape(4, 4, 2, 4, 2), ("x", "y", "l", "h", "c"))
    rows = P(("x", "y", "l"), ("h", "c"))
    columns = P(("h", "c"), ("x", "y", "l"))
    return jax.shard_map(
        on_device,
        mesh=fine,
        in_specs=(rows, columns, rows, rows),
        out_specs=(rows, rows, columns, rows),
        check_vma=False,
    )
```

time: 207 us -> 201 us (0.971)
  blocking collectives: 17.1 us -> 0 us
  between operations: 14.5 us -> 1.08 us
  waiting for transfers between devices: 81.3 us -> 94.3 us
  starting transfers between devices: 51.2 us -> 61.3 us
  Pallas kernels: 9.1 us -> 16.7 us
  other arithmetic: 9.9 us -> 6.11 us
  matrix products: 9.03 us -> 6.45 us
    all_to_all x0 -> x2, waiting for transfers between devices: none -> 23.9 us  [copies(): return lax.all_to_all(sent, axes, 0, 0).reshape(size * rows, -1)]
    all_to_all x1 -> x0, blocking collectives: 17.1 us -> none  [on_device(): lax.all_to_all(jnp.broadcast_to(both[None], (near,) + both.shape), NEAR,...]
    all_to_all x0 -> x2, starting transfers between devices: none -> 13.8 us  [copies(): return lax.all_to_all(sent, axes, 0, 0).reshape(size * rows, -1)]
    all_to_all x2, waiting for transfers between devices: 30.1 us -> 21.2 us  [rows_sum(): pieces = lax.all_to_all(partial.reshape(peers, rows, -1), FAR, 0, 0)]
    pallas_call x0 -> x6, Pallas kernels: none -> 8.63 us  [the longest x2 8.12 us: joined_product(): pl.pallas_call(functools.partial(joined_kernel, turned), grid_spec=pltpu....]
    all_gather x2 -> x0, waiting for transfers between devices: 4.35 us -> none  [the longest x1 4.33 us: on_device(): grad_all = lax.all_gather(both[:, features:], 'y', axis=0, tiled=True)]
    all_to_all x2, starting transfers between devices: 17.4 us -> 13.6 us  [rows_sum(): pieces = lax.all_to_all(partial.reshape(peers, rows, -1), FAR, 0, 0)]
    broadcast_in_dim x2 -> x3, local copies, waits for them, and re-layouts: 0.16 us -> 3.05 us  [the longest x2 2.94 us: copies(): sent = jnp.broadcast_to(block[None], (size,) + block.shape)]
  transfers between devices with their start and end apart: 23 -> 26, of which waited for: 15 -> 15; matrix products, arithmetic and copies ran while one was open for 9% -> 7% of each run, Pallas kernels for 4% -> 7%
where the time goes in v3:
time: 201 us
  waiting for transfers between devices  94.3 us (47%)
  starting transfers between devices  61.3 us (30%)
  Pallas kernels  16.7 us (8%)
  local copies, waits for them, and re-layouts  14.8 us (7%)
  matrix products  6.45 us (3%)
  other arithmetic  6.11 us (3%)
    ppermute x22, waiting for transfers between devices, move(): lax.ppermute(block, axis, [(i, (i + hops) % size) for i in range(size)])  49.1 us
    ppermute x22, starting transfers between devices, move(): lax.ppermute(block, axis, [(i, (i + hops) % size) for i in range(size)])  33.9 us
    all_to_all x2, waiting for transfers between devices, copies(): return lax.all_to_all(sent, axes, 0, 0).reshape(size * rows, -1)  23.9 us
    all_to_all x2, waiting for transfers between devices, rows_sum(): pieces = lax.all_to_all(partial.reshape(peers, rows, -1), FAR, 0, 0)  21.2 us
    all_to_all x2, starting transfers between devices, copies(): return lax.all_to_all(sent, axes, 0, 0).reshape(size * rows, -1)  13.8 us
    all_to_all x2, starting transfers between devices, rows_sum(): pieces = lax.all_to_all(partial.reshape(peers, rows, -1), FAR, 0, 0)  13.6 us
    unnamed x34, local copies, waits for them, and re-layouts  11.2 us
    pallas_call x2, Pallas kernels, joined_product(): pl.pallas_call(functools.partial(joined_kernel, turned), grid_spec=pltpu....  8.12 us
  transfers between devices with their start and end apart: 26, of which 15 were waited for; matrix products, arithmetic and copies ran while one was open for 7% of the time, Pallas kernels for 7%

profile of v3, /device:TPU:2, one launch (start us, length us, event | category | flops | bytes accessed | tf_op | source)
XLA Modules:
  0.0 200.7 jit_solution(2918246939196053151)
XLA Ops:
  0.6 2.2 %broadcast_in_dim.31 = bf16[32,32,768]{2,1,0:T(8,128)(2,1)} broadcast(bf16[32,768]{1,0:T(8,128)(2,1)} %param.4), dimensions={1,2} | broadcast | bytes 1622016 | tf_op jit(solution)/shard_map/broadcast_in_dim | solution.py:202
  2.8 9.1 %all-to-all-start = ((bf16[32,32,768]{2,1,0:T(8,128)(2,1)}), bf16[32,32,768]{2,1,0:T(8,128)(2,1)S(1)}, u32[]{:S(2)}, u32[]{:S(2)}) async-start(bf16[32,32,768]{2,1,0:T(8,128)(2,1)} %broadcast_in_dim.31), calls=%async_computation | async-start | bytes 3145728 | tf_op jit(solution)/shard_map/all_to_all | solution.py:203
  11.9 22.6 %all-to-all-done = bf16[32,32,768]{2,1,0:T(8,128)(2,1)S(1)} async-done(((bf16[32,32,768]{2,1,0:T(8,128)(2,1)}), bf16[32,32,768]{2,1,0:T(8,128)(2,1)S(1)}, u32[]{:S(2)}, u32[]{:S(2)}) %all-to-all-start) | async-done | bytes 1572896 | tf_op jit(solution)/shard_map/all_to_all | solution.py:203
  34.5 0.8 broadcast_in_dim.32
  35.3 4.6 %all-to-all-start.1 = ((bf16[8,32,768]{2,1,0:T(8,128)(2,1)}), bf16[8,32,768]{2,1,0:T(8,128)(2,1)S(1)}, u32[]{:S(2)}, u32[]{:S(2)}) async-start(bf16[8,32,768]{2,1,0:T(8,128)(2,1)} %broadcast_in_dim.32), calls=%async_computation.1 | async-start | bytes 786432 | tf_op jit(solution)/shard_map/all_to_all | solution.py:203
  39.9 2.3 %shard_map.76 = bf16[512,768]{1,0:T(8,128)(2,1)} custom-call(s32[1]{0:T(128)} %bitcast.3.which_ref, bf16[1024,768]{1,0:T(8,128)(2,1)S(1)} %bitcast.45, bf16[768,768]{1,0:T(8,128)(2,1)S(1)} %copy-done.3), custom_call_target="tpu_custom_call" | custom-call | flops 603979776 | bytes 3538944 | tf_op jit(solution)/shard_map/pallas_call | solution.py:89
  42.3 1.3 shard_map.75
  43.6 1.2 copy-done
  44.8 1.4 all-to-all-done.1
  46.2 0.8 collective-permute-start.4
  47.0 1.2 collective-permute-start.3
  48.2 0.1 broadcast_in_dim.33
  48.4 1.3 convert_add_fusion.1
  49.8 5.5 %collective-permute-start.2 = (bf16[64,768]{1,0:T(8,128)(2,1)S(1)}, bf16[64,768]{1,0:T(8,128)(2,1)S(1)}, u32[]{:S(2)}, u32[]{:S(2)}) collective-permute-start(bf16[64,768]{1,0:T(8,128)(2,1)S(1)} %get-tuple-element.46), channel_id=1, source_target_pairs={{0,6},{2,0},{4,2},{6,4},{1,7},{3,1},{5,3},{7,5},{8,14},{10,8},{12,... | collective-permute-start | bytes 294920 | tf_op jit(solution)/shard_map/ppermute | solution.py:32
  55.3 1.0 collective-permute-done.4.refs_5_
  56.3 2.1 %collective-permute-start.8 = (bf16[128,768]{1,0:T(8,128)(2,1)S(1)}, bf16[128,768]{1,0:T(8,128)(2,1)S(1)}, u32[]{:S(2)}, u32[]{:S(2)}) collective-permute-start(bf16[128,768]{1,0:T(8,128)(2,1)S(1)} %slice.75), channel_id=1, source_target_pairs={{0,48},{16,0},{32,16},{48,32},{1,49},{17,1},{33,17},{49,33},{2,50}... | collective-permute-start | bytes 589832 | tf_op jit(solution)/shard_map/ppermute | solution.py:32
  58.5 0.1 collective-permute-start.7
  58.6 3.9 %collective-permute-done.1.refs_1_ = bf16[64,768]{1,0:T(8,128)(2,1)S(1)} collective-permute-done((bf16[64,768]{1,0:T(8,128)(2,1)S(1)}, bf16[64,768]{1,0:T(8,128)(2,1)S(1)}, u32[]{:S(2)}, u32[]{:S(2)}) %collective-permute-start.1) | collective-permute-done | bytes 98336 | tf_op jit(solution)/shard_map/ppermute | solution.py:32
  62.6 4.1 %collective-permute-start.6 = (bf16[128,768]{1,0:T(8,128)(2,1)S(1)}, bf16[128,768]{1,0:T(8,128)(2,1)S(1)}, u32[]{:S(2)}, u32[]{:S(2)}) collective-permute-start(bf16[128,768]{1,0:T(8,128)(2,1)S(1)} %get-tuple-element.22), channel_id=1, source_target_pairs={{0,6},{2,0},{4,2},{6,4},{1,7},{3,1},{5,3},{7,5},{8,14},{10,8},{12,... | collective-permute-start | bytes 589832 | tf_op jit(solution)/shard_map/ppermute | solution.py:32
  66.9 7.0 %collective-permute-done.5.refs_1_ = bf16[128,768]{1,0:T(8,128)(2,1)S(1)} collective-permute-done((bf16[128,768]{1,0:T(8,128)(2,1)S(1)}, bf16[128,768]{1,0:T(8,128)(2,1)S(1)}, u32[]{:S(2)}, u32[]{:S(2)}) %collective-permute-start.5) | collective-permute-done | bytes 196640 | tf_op jit(solution)/shard_map/ppermute | solution.py:32
  73.8 0.3 shard_map.78
  74.2 2.2 %shard_map.80 = bf16[512,768]{1,0:T(8,128)(2,1)S(1)} custom-call(s32[1]{0:T(128)} %bitcast.3.which_ref, bf16[1024,768]{1,0:T(8,128)(2,1)S(1)} %bitcast.48, bf16[768,768]{1,0:T(8,128)(2,1)S(1)} %copy-done.2, bf16[128,768]{1,0:T(8,128)(2,1)S(1)} %get-tuple-element.23.refs_0_), custom_call_target="tpu_custom_call" | custom-call | flops 603979776 | bytes 3538944 | tf_op jit(solution)/shard_map/pallas_call | solution.py:89
  76.4 0.1 collective-permute-start.10
  76.5 2.4 %collective-permute-start.11 = (bf16[128,768]{1,0:T(8,128)(2,1)S(1)}, bf16[128,768]{1,0:T(8,128)(2,1)S(1)}, u32[]{:S(2)}, u32[]{:S(2)}) collective-permute-start(bf16[128,768]{1,0:T(8,128)(2,1)S(1)} %get-tuple-element.23.refs_0_), channel_id=1, source_target_pairs={{0,2},{2,4},{4,6},{6,0},{1,3},{3,5},{5,7},{7,1},{8,10},{10,12},{12... | collective-permute-start | bytes 589832 | tf_op jit(solution)/shard_map/ppermute | solution.py:32
  78.9 1.8 collective-permute-start.9
  80.7 2.2 %shard_map.79 = f32[512,768]{1,0:T(8,128)S(1)} custom-call(s32[1]{0:T(128)} %bitcast.1.which_ref, bf16[1024,768]{1,0:T(8,128)(2,1)S(1)} %bitcast.49, bf16[768,768]{1,0:T(8,128)(2,1)S(1)} %copy-done.2), custom_call_target="tpu_custom_call" | custom-call | flops 603979776 | bytes 3538944 | tf_op jit(solution)/shard_map/pallas_call | solution.py:89
  82.9 4.9 %collective-permute-done.11 = bf16[128,768]{1,0:T(8,128)(2,1)S(1)} collective-permute-done((bf16[128,768]{1,0:T(8,128)(2,1)S(1)}, bf16[128,768]{1,0:T(8,128)(2,1)S(1)}, u32[]{:S(2)}, u32[]{:S(2)}) %collective-permute-start.11) | collective-permute-done | bytes 196640 | tf_op jit(solution)/shard_map/ppermute | solution.py:32
  87.8 2.4 %collective-permute-done.9 = bf16[128,768]{1,0:T(8,128)(2,1)S(1)} collective-permute-done((bf16[128,768]{1,0:T(8,128)(2,1)S(1)}, bf16[128,768]{1,0:T(8,128)(2,1)S(1)}, u32[]{:S(2)}, u32[]{:S(2)}) %collective-permute-start.9) | collective-permute-done | bytes 196640 | tf_op jit(solution)/shard_map/ppermute | solution.py:32
  90.2 0.1 convert_add_fusion
  90.5 1.1 collective-permute-start.12
  91.6 3.3 %collective-permute-start.13 = (bf16[128,768]{1,0:T(8,128)(2,1)S(1)}, bf16[128,768]{1,0:T(8,128)(2,1)S(1)}, u32[]{:S(2)}, u32[]{:S(2)}) collective-permute-start(bf16[128,768]{1,0:T(8,128)(2,1)S(1)} %pad_maximum_fusion.1), channel_id=1, source_target_pairs={{0,6},{2,0},{4,2},{6,4},{1,7},{3,1},{5,3},{7,5},{8,14},{10,8},{12,... | collective-permute-start | bytes 589832 | tf_op jit(solution)/shard_map/ppermute | solution.py:32
  95.0 8.7 %collective-permute-done.12 = bf16[128,768]{1,0:T(8,128)(2,1)S(1)} collective-permute-done((bf16[128,768]{1,0:T(8,128)(2,1)S(1)}, bf16[128,768]{1,0:T(8,128)(2,1)S(1)}, u32[]{:S(2)}, u32[]{:S(2)}) %collective-permute-start.12) | collective-permute-done | bytes 196640 | tf_op jit(solution)/shard_map/ppermute | solution.py:32
  103.7 0.1 collective-permute-start.14
  103.8 0.1 dynamic-slice_bitcast_fusion
  104.0 0.3 collective-permute-start.15
  104.2 4.0 %collective-permute-start.16 = (bf16[128,768]{1,0:T(8,128)(2,1)S(1)}, bf16[128,768]{1,0:T(8,128)(2,1)S(1)}, u32[]{:S(2)}, u32[]{:S(2)}) collective-permute-start(bf16[128,768]{1,0:T(8,128)(2,1)S(1)} %get-tuple-element.26), channel_id=1, source_target_pairs={{0,6},{2,0},{4,2},{6,4},{1,7},{3,1},{5,3},{7,5},{8,14},{10,8},{12,... | collective-permute-start | bytes 589832 | tf_op jit(solution)/shard_map/ppermute | solution.py:32
  108.2 9.5 %collective-permute-done.15.refs_1_ = bf16[128,768]{1,0:T(8,128)(2,1)S(1)} collective-permute-done((bf16[128,768]{1,0:T(8,128)(2,1)S(1)}, bf16[128,768]{1,0:T(8,128)(2,1)S(1)}, u32[]{:S(2)}, u32[]{:S(2)}) %collective-permute-start.15) | collective-permute-done | bytes 196640 | tf_op jit(solution)/shard_map/ppermute | solution.py:32
  117.6 0.2 collective-permute-done.16.refs_2_
  117.9 3.0 %collective-permute-start.19 = (bf16[128,768]{1,0:T(8,128)(2,1)S(1)}, bf16[128,768]{1,0:T(8,128)(2,1)S(1)}, u32[]{:S(2)}, u32[]{:S(2)}) collective-permute-start(bf16[128,768]{1,0:T(8,128)(2,1)S(1)} %shard_map.83), channel_id=1, source_target_pairs={{0,6},{2,0},{4,2},{6,4},{1,7},{3,1},{5,3},{7,5},{8,14},{10,8},{12,... | collective-permute-start | bytes 589832 | tf_op jit(solution)/shard_map/ppermute | solution.py:32
  121.0 8.2 %collective-permute-done.19 = bf16[128,768]{1,0:T(8,128)(2,1)S(1)} collective-permute-done((bf16[128,768]{1,0:T(8,128)(2,1)S(1)}, bf16[128,768]{1,0:T(8,128)(2,1)S(1)}, u32[]{:S(2)}, u32[]{:S(2)}) %collective-permute-start.19) | collective-permute-done | bytes 196640 | tf_op jit(solution)/shard_map/ppermute | solution.py:32
  129.3 3.7 %collective-permute-start.20 = (bf16[64,768]{1,0:T(8,128)(2,1)S(1)}, bf16[64,768]{1,0:T(8,128)(2,1)S(1)}, u32[]{:S(2)}, u32[]{:S(2)}) collective-permute-start(bf16[64,768]{1,0:T(8,128)(2,1)S(1)} %slice.85), channel_id=1, source_target_pairs={{0,6},{2,0},{4,2},{6,4},{1,7},{3,1},{5,3},{7,5},{8,14},{10,8},{12,... | collective-permute-start | bytes 294920 | tf_op jit(solution)/shard_map/ppermute | solution.py:32
  133.1 3.2 %shard_map.81 = (bf16[1024,768]{1,0:T(8,128)(2,1)S(1)}, bf16[1024,768]{1,0:T(8,128)(2,1)S(1)}) custom-call(s32[2]{0:T(128)S(1)} %pad_add_fusion.place_ref, bf16[512,768]{1,0:T(8,128)(2,1)S(1)} %constant_dynamic-update-slice_fusion.mine_ref, bf16[512,768]{1,0:T(8,128)(2,1)S(1)} %collective-permute-done.14.other_ref.refs_4_, bf16[768,768]{1,0:T(8,128)(2,1)S(1)} %copy-done.2), custom_call_target="tpu_custom_call" | custom-call | flops 1207959552 | bytes 5898240 | tf_op jit(solution)/shard_map/pallas_call | solution.py:127
  136.3 1.1 copy-done.5
  137.5 1.2 copy-done.7
  138.6 0.7 copy-done.11
  139.3 1.2 collective-permute-done.18
  140.5 0.6 copy-done.12
  141.1 8.4 %all-to-all-start.2 = ((bf16[32,32,768]{2,1,0:T(8,128)(2,1)}), bf16[32,32,768]{2,1,0:T(8,128)(2,1)}, u32[]{:S(2)}, u32[]{:S(2)}) async-start(bf16[32,32,768]{2,1,0:T(8,128)(2,1)} %bitcast.51), calls=%async_computation.2 | async-start | bytes 3145728 | tf_op jit(solution)/shard_map/all_to_all | solution.py:197
  149.5 0.9 constant_dynamic-update-slice_fusion.6
  150.5 0.9 constant_dynamic-update-slice_fusion.5
  151.4 0.9 constant_dynamic-update-slice_fusion.4
  152.3 0.1 collective-permute-start.21
  152.4 2.3 %collective-permute-done.21.other_ref = bf16[512,768]{1,0:T(8,128)(2,1)S(1)} collective-permute-done((bf16[512,768]{1,0:T(8,128)(2,1)S(1)}, bf16[512,768]{1,0:T(8,128)(2,1)S(1)}, u32[]{:S(2)}, u32[]{:S(2)}) %collective-permute-start.21) | collective-permute-done | bytes 786464 | tf_op jit(solution)/shard_map/ppermute | solution.py:32
  154.7 1.3 copy-done.4
  155.9 4.9 %shard_map.84 = (bf16[1024,768]{1,0:T(8,128)(2,1)S(1)}, bf16[1024,768]{1,0:T(8,128)(2,1)S(1)}) custom-call(s32[2]{0:T(128)S(1)} %pad_add_fusion.place_ref, bf16[512,768]{1,0:T(8,128)(2,1)S(1)} %constant_dynamic-update-slice_fusion.3.mine_ref, bf16[512,768]{1,0:T(8,128)(2,1)S(1)} %collective-permute-done.21.other_ref, bf16[768,768]{1,0:T(8,128)(2,1)S(1)} %copy-done.4), custom_call_target="tpu_custom_call" | custom-call | flops 1207959552 | bytes 5898240 | tf_op jit(solution)/shard_map/pallas_call | solution.py:127
  160.9 1.2 copy-done.6
  162.0 1.2 copy-done.8
  163.2 8.7 %all-to-all-done.2 = bf16[32,32,768]{2,1,0:T(8,128)(2,1)} async-done(((bf16[32,32,768]{2,1,0:T(8,128)(2,1)}), bf16[32,32,768]{2,1,0:T(8,128)(2,1)}, u32[]{:S(2)}, u32[]{:S(2)}) %all-to-all-start.2) | async-done | bytes 1572896 | tf_op jit(solution)/shard_map/all_to_all | solution.py:197
  172.0 5.2 %all-to-all-start.3 = ((bf16[32,32,768]{2,1,0:T(8,128)(2,1)}), bf16[32,32,768]{2,1,0:T(8,128)(2,1)}, u32[]{:S(2)}, u32[]{:S(2)}) async-start(bf16[32,32,768]{2,1,0:T(8,128)(2,1)} %bitcast.52), calls=%async_computation.3 | async-start | bytes 3145728 | tf_op jit(solution)/shard_map/all_to_all | solution.py:197
  177.2 4.0 %convolution_convert_fusion = bf16[768,768]{1,0:T(8,128)(2,1)} fusion(bf16[1024,768]{1,0:T(8,128)(2,1)} %copy-done.7, bf16[1024,768]{1,0:T(8,128)(2,1)S(1)} %bitcast.50), kind=kOutput, calls=%fused_computation.2 | convolution fusion | flops 1208549376 | bytes 4325376 | tf_op jit(solution)/shard_map/dot_general | solution.py:27
  181.2 2.5 %convolution_convert_fusion.1 = bf16[768,768]{1,0:T(8,128)(2,1)} fusion(bf16[1024,768]{1,0:T(8,128)(2,1)S(1)} %bitcast.47, bf16[1024,768]{1,0:T(8,128)(2,1)S(1)} %copy-done.9), kind=kOutput, calls=%fused_computation.3 | convolution fusion | flops 1208549376 | bytes 4325376 | tf_op jit(solution)/shard_map/dot_general | solution.py:27
  183.7 2.3 %reduce_sum.24 = bf16[32,768]{1,0:T(8,128)(2,1)} reduce(bf16[32,32,768]{2,1,0:T(8,128)(2,1)} %all-to-all-done.2, bf16[]{:T(256)} %constant.97.clone.1), dimensions={0}, to_apply=%region_0.1 | reduce | flops 761856 | bytes 1622018 | tf_op jit(solution)/shard_map/reduce_sum | solution.py:198
  185.9 12.5 %all-to-all-done.3 = bf16[32,32,768]{2,1,0:T(8,128)(2,1)} async-done(((bf16[32,32,768]{2,1,0:T(8,128)(2,1)}), bf16[32,32,768]{2,1,0:T(8,128)(2,1)}, u32[]{:S(2)}, u32[]{:S(2)}) %all-to-all-start.3) | async-done | bytes 1572896 | tf_op jit(solution)/shard_map/all_to_all | solution.py:197
  198.4 2.3 %reduce_sum.25 = bf16[32,768]{1,0:T(8,128)(2,1)} reduce(bf16[32,32,768]{2,1,0:T(8,128)(2,1)} %all-to-all-done.3, bf16[]{:T(256)} %constant.97.clone.1), dimensions={0}, to_apply=%region_1.2 | reduce | flops 761856 | bytes 1622018 | tf_op jit(solution)/shard_map/reduce_sum | solution.py:198
  (65 shorter events, 1.0 us)
Async XLA Ops:
  2.8 31.7 %copy-start.13 = (bf16[32,768]{1,0:T(8,128)(2,1)S(1)}, bf16[32,768]{1,0:T(8,128)(2,1)}, u32[]{:S(2)}) copy-start(bf16[32,768]{1,0:T(8,128)(2,1)} %param.7) | copy-start | bytes 147460
  2.8 37.1 %copy-start.3 = (bf16[768,768]{1,0:T(8,128)(2,1)S(1)}, bf16[768,768]{1,0:T(8,128)(2,1)}, u32[]{:S(2)}) copy-start(bf16[768,768]{1,0:T(8,128)(2,1)} %weight_ref.11) | copy-start | bytes 3538948
  2.8 31.7 %all-to-all-start = ((bf16[32,32,768]{2,1,0:T(8,128)(2,1)}), bf16[32,32,768]{2,1,0:T(8,128)(2,1)S(1)}, u32[]{:S(2)}, u32[]{:S(2)}) async-start(bf16[32,32,768]{2,1,0:T(8,128)(2,1)} %broadcast_in_dim.31), calls=%async_computation | async-start | bytes 3145728 | tf_op jit(solution)/shard_map/all_to_all | solution.py:203
  35.3 10.9 %all-to-all-start.1 = ((bf16[8,32,768]{2,1,0:T(8,128)(2,1)}), bf16[8,32,768]{2,1,0:T(8,128)(2,1)S(1)}, u32[]{:S(2)}, u32[]{:S(2)}) async-start(bf16[8,32,768]{2,1,0:T(8,128)(2,1)} %broadcast_in_dim.32), calls=%async_computation.1 | async-start | bytes 786432 | tf_op jit(solution)/shard_map/all_to_all | solution.py:203
  42.3 6.1 %collective-permute-start = (bf16[512,768]{1,0:T(8,128)(2,1)}, bf16[512,768]{1,0:T(8,128)(2,1)}, u32[]{:S(2)}, u32[]{:S(2)}) collective-permute-start(bf16[512,768]{1,0:T(8,128)(2,1)} %shard_map.76), channel_id=1, source_target_pairs={{0,1},{1,0},{2,3},{3,2},{4,5},{5,4},{6,7},{7,6},{8,9},{9,8},{10,11... | collective-permute-start | bytes 2359304 | tf_op jit(solution)/shard_map/ppermute | solution.py:32
  43.6 1.2 copy-start
  46.2 2.2 %copy-start.1 = (f32[512,768]{1,0:T(8,128)S(1)}, f32[512,768]{1,0:T(8,128)}, u32[]{:S(2)}) copy-start(f32[512,768]{1,0:T(8,128)} %copy-done) | copy-start | bytes 4718596
  46.2 10.2 %collective-permute-start.4 = (bf16[256,768]{1,0:T(8,128)(2,1)S(1)}, bf16[256,768]{1,0:T(8,128)(2,1)S(1)}, u32[]{:S(2)}, u32[]{:S(2)}) collective-permute-start(bf16[256,768]{1,0:T(8,128)(2,1)S(1)} %bitcast.57), channel_id=1, source_target_pairs={{0,48},{16,0},{32,16},{48,32},{1,49},{17,1},{33,17},{49,33},{2,50}... | collective-permute-start | bytes 1179656 | tf_op jit(solution)/shard_map/ppermute | solution.py:32
  47.0 11.5 %collective-permute-start.3 = (bf16[256,768]{1,0:T(8,128)(2,1)S(1)}, bf16[256,768]{1,0:T(8,128)(2,1)S(1)}, u32[]{:S(2)}, u32[]{:S(2)}) collective-permute-start(bf16[256,768]{1,0:T(8,128)(2,1)S(1)} %bitcast.58), channel_id=1, source_target_pairs={{0,16},{16,32},{32,48},{48,0},{1,17},{17,33},{33,49},{49,1},{2,18}... | collective-permute-start | bytes 1179656 | tf_op jit(solution)/shard_map/ppermute | solution.py:32
  49.8 8.8 %collective-permute-start.2 = (bf16[64,768]{1,0:T(8,128)(2,1)S(1)}, bf16[64,768]{1,0:T(8,128)(2,1)S(1)}, u32[]{:S(2)}, u32[]{:S(2)}) collective-permute-start(bf16[64,768]{1,0:T(8,128)(2,1)S(1)} %get-tuple-element.46), channel_id=1, source_target_pairs={{0,6},{2,0},{4,2},{6,4},{1,7},{3,1},{5,3},{7,5},{8,14},{10,8},{12,... | collective-permute-start | bytes 294920 | tf_op jit(solution)/shard_map/ppermute | solution.py:32
  55.2 7.2 %collective-permute-start.1 = (bf16[64,768]{1,0:T(8,128)(2,1)S(1)}, bf16[64,768]{1,0:T(8,128)(2,1)S(1)}, u32[]{:S(2)}, u32[]{:S(2)}) collective-permute-start(bf16[64,768]{1,0:T(8,128)(2,1)S(1)} %get-tuple-element.47), channel_id=1, source_target_pairs={{0,2},{2,4},{4,6},{6,0},{1,3},{3,5},{5,7},{7,1},{8,10},{10,12},{12... | collective-permute-start | bytes 294920 | tf_op jit(solution)/shard_map/ppermute | solution.py:32
  56.3 10.5 %collective-permute-start.8 = (bf16[128,768]{1,0:T(8,128)(2,1)S(1)}, bf16[128,768]{1,0:T(8,128)(2,1)S(1)}, u32[]{:S(2)}, u32[]{:S(2)}) collective-permute-start(bf16[128,768]{1,0:T(8,128)(2,1)S(1)} %slice.75), channel_id=1, source_target_pairs={{0,48},{16,0},{32,16},{48,32},{1,49},{17,1},{33,17},{49,33},{2,50}... | collective-permute-start | bytes 589832 | tf_op jit(solution)/shard_map/ppermute | solution.py:32
  58.5 8.3 %collective-permute-start.7 = (bf16[128,768]{1,0:T(8,128)(2,1)S(1)}, bf16[128,768]{1,0:T(8,128)(2,1)S(1)}, u32[]{:S(2)}, u32[]{:S(2)}) collective-permute-start(bf16[128,768]{1,0:T(8,128)(2,1)S(1)} %slice.74), channel_id=1, source_target_pairs={{0,16},{16,32},{32,48},{48,0},{1,17},{17,33},{33,49},{49,1},{2,18}... | collective-permute-start | bytes 589832 | tf_op jit(solution)/shard_map/ppermute | solution.py:32
  62.5 11.4 %collective-permute-start.5 = (bf16[128,768]{1,0:T(8,128)(2,1)S(1)}, bf16[128,768]{1,0:T(8,128)(2,1)S(1)}, u32[]{:S(2)}, u32[]{:S(2)}) collective-permute-start(bf16[128,768]{1,0:T(8,128)(2,1)S(1)} %get-tuple-element.21), channel_id=1, source_target_pairs={{0,2},{2,4},{4,6},{6,0},{1,3},{3,5},{5,7},{7,1},{8,10},{10,12},{12... | collective-permute-start | bytes 589832 | tf_op jit(solution)/shard_map/ppermute | solution.py:32
  62.6 11.3 %collective-permute-start.6 = (bf16[128,768]{1,0:T(8,128)(2,1)S(1)}, bf16[128,768]{1,0:T(8,128)(2,1)S(1)}, u32[]{:S(2)}, u32[]{:S(2)}) collective-permute-start(bf16[128,768]{1,0:T(8,128)(2,1)S(1)} %get-tuple-element.22), channel_id=1, source_target_pairs={{0,6},{2,0},{4,2},{6,4},{1,7},{3,1},{5,3},{7,5},{8,14},{10,8},{12,... | collective-permute-start | bytes 589832 | tf_op jit(solution)/shard_map/ppermute | solution.py:32
  66.7 7.4 %copy-start.2 = (bf16[768,768]{1,0:T(8,128)(2,1)S(1)}, bf16[768,768]{1,0:T(8,128)(2,1)}, u32[]{:S(2)}) copy-start(bf16[768,768]{1,0:T(8,128)(2,1)} %weight_ref.10) | copy-start | bytes 3538948
  76.4 13.8 %collective-permute-start.10 = (bf16[512,768]{1,0:T(8,128)(2,1)S(1)}, bf16[512,768]{1,0:T(8,128)(2,1)S(1)}, u32[]{:S(2)}, u32[]{:S(2)}) collective-permute-start(bf16[512,768]{1,0:T(8,128)(2,1)S(1)} %shard_map.80), channel_id=1, source_target_pairs={{0,1},{1,0},{2,3},{3,2},{4,5},{5,4},{6,7},{7,6},{8,9},{9,8},{10,11... | collective-permute-start | bytes 2359304 | tf_op jit(solution)/shard_map/ppermute | solution.py:32
  76.5 11.3 %collective-permute-start.11 = (bf16[128,768]{1,0:T(8,128)(2,1)S(1)}, bf16[128,768]{1,0:T(8,128)(2,1)S(1)}, u32[]{:S(2)}, u32[]{:S(2)}) collective-permute-start(bf16[128,768]{1,0:T(8,128)(2,1)S(1)} %get-tuple-element.23.refs_0_), channel_id=1, source_target_pairs={{0,2},{2,4},{4,6},{6,0},{1,3},{3,5},{5,7},{7,1},{8,10},{10,12},{12... | collective-permute-start | bytes 589832 | tf_op jit(solution)/shard_map/ppermute | solution.py:32
  78.9 11.3 %collective-permute-start.9 = (bf16[128,768]{1,0:T(8,128)(2,1)S(1)}, bf16[128,768]{1,0:T(8,128)(2,1)S(1)}, u32[]{:S(2)}, u32[]{:S(2)}) collective-permute-start(bf16[128,768]{1,0:T(8,128)(2,1)S(1)} %get-tuple-element.23.refs_0_), channel_id=1, source_target_pairs={{0,6},{2,0},{4,2},{6,4},{1,7},{3,1},{5,3},{7,5},{8,14},{10,8},{12,... | collective-permute-start | bytes 589832 | tf_op jit(solution)/shard_map/ppermute | solution.py:32
  90.5 13.2 %collective-permute-start.12 = (bf16[128,768]{1,0:T(8,128)(2,1)S(1)}, bf16[128,768]{1,0:T(8,128)(2,1)S(1)}, u32[]{:S(2)}, u32[]{:S(2)}) collective-permute-start(bf16[128,768]{1,0:T(8,128)(2,1)S(1)} %pad_maximum_fusion), channel_id=1, source_target_pairs={{0,2},{2,4},{4,6},{6,0},{1,3},{3,5},{5,7},{7,1},{8,10},{10,12},{12... | collective-permute-start | bytes 589832 | tf_op jit(solution)/shard_map/ppermute | solution.py:32
  91.6 12.0 %collective-permute-start.13 = (bf16[128,768]{1,0:T(8,128)(2,1)S(1)}, bf16[128,768]{1,0:T(8,128)(2,1)S(1)}, u32[]{:S(2)}, u32[]{:S(2)}) collective-permute-start(bf16[128,768]{1,0:T(8,128)(2,1)S(1)} %pad_maximum_fusion.1), channel_id=1, source_target_pairs={{0,6},{2,0},{4,2},{6,4},{1,7},{3,1},{5,3},{7,5},{8,14},{10,8},{12,... | collective-permute-start | bytes 589832 | tf_op jit(solution)/shard_map/ppermute | solution.py:32
  103.7 14.2 %collective-permute-start.14 = (bf16[512,768]{1,0:T(8,128)(2,1)S(1)}, bf16[512,768]{1,0:T(8,128)(2,1)S(1)}, u32[]{:S(2)}, u32[]{:S(2)}) collective-permute-start(bf16[512,768]{1,0:T(8,128)(2,1)S(1)} %constant_dynamic-update-slice_fusion.mine_ref), channel_id=1, source_target_pairs={{0,1},{1,0},{2,3},{3,2},{4,5},{5,4},{6,7},{7,6},{8,9},{9,8},{10,11... | collective-permute-start | bytes 2359304 | tf_op jit(solution)/shard_map/ppermute | solution.py:32
  104.0 13.7 %collective-permute-start.15 = (bf16[128,768]{1,0:T(8,128)(2,1)S(1)}, bf16[128,768]{1,0:T(8,128)(2,1)S(1)}, u32[]{:S(2)}, u32[]{:S(2)}) collective-permute-start(bf16[128,768]{1,0:T(8,128)(2,1)S(1)} %get-tuple-element.25), channel_id=1, source_target_pairs={{0,2},{2,4},{4,6},{6,0},{1,3},{3,5},{5,7},{7,1},{8,10},{10,12},{12... | collective-permute-start | bytes 589832 | tf_op jit(solution)/shard_map/ppermute | solution.py:32
  104.2 13.6 %collective-permute-start.16 = (bf16[128,768]{1,0:T(8,128)(2,1)S(1)}, bf16[128,768]{1,0:T(8,128)(2,1)S(1)}, u32[]{:S(2)}, u32[]{:S(2)}) collective-permute-start(bf16[128,768]{1,0:T(8,128)(2,1)S(1)} %get-tuple-element.26), channel_id=1, source_target_pairs={{0,6},{2,0},{4,2},{6,4},{1,7},{3,1},{5,3},{7,5},{8,14},{10,8},{12,... | collective-permute-start | bytes 589832 | tf_op jit(solution)/shard_map/ppermute | solution.py:32
  117.9 11.3 %collective-permute-start.19 = (bf16[128,768]{1,0:T(8,128)(2,1)S(1)}, bf16[128,768]{1,0:T(8,128)(2,1)S(1)}, u32[]{:S(2)}, u32[]{:S(2)}) collective-permute-start(bf16[128,768]{1,0:T(8,128)(2,1)S(1)} %shard_map.83), channel_id=1, source_target_pairs={{0,6},{2,0},{4,2},{6,4},{1,7},{3,1},{5,3},{7,5},{8,14},{10,8},{12,... | collective-permute-start | bytes 589832 | tf_op jit(solution)/shard_map/ppermute | solution.py:32
  120.9 12.0 %collective-permute-start.17 = (bf16[128,768]{1,0:T(8,128)(2,1)S(1)}, bf16[128,768]{1,0:T(8,128)(2,1)S(1)}, u32[]{:S(2)}, u32[]{:S(2)}) collective-permute-start(bf16[128,768]{1,0:T(8,128)(2,1)S(1)} %shard_map.83), channel_id=1, source_target_pairs={{0,2},{2,4},{4,6},{6,0},{1,3},{3,5},{5,7},{7,1},{8,10},{10,12},{12... | collective-permute-start | bytes 589832 | tf_op jit(solution)/shard_map/ppermute | solution.py:32
  129.2 7.1 %copy-start.10 = (bf16[128,768]{1,0:T(8,128)(2,1)}, bf16[128,768]{1,0:T(8,128)(2,1)S(1)}, u32[]{:S(2)}) copy-start(bf16[128,768]{1,0:T(8,128)(2,1)S(1)} %collective-permute-done.19) | copy-start | bytes 589828
  129.3 9.4 %collective-permute-start.20 = (bf16[64,768]{1,0:T(8,128)(2,1)S(1)}, bf16[64,768]{1,0:T(8,128)(2,1)S(1)}, u32[]{:S(2)}, u32[]{:S(2)}) collective-permute-start(bf16[64,768]{1,0:T(8,128)(2,1)S(1)} %slice.85), channel_id=1, source_target_pairs={{0,6},{2,0},{4,2},{6,4},{1,7},{3,1},{5,3},{7,5},{8,14},{10,8},{12,... | collective-permute-start | bytes 294920 | tf_op jit(solution)/shard_map/ppermute | solution.py:32
  133.0 7.5 %collective-permute-start.18 = (bf16[64,768]{1,0:T(8,128)(2,1)S(1)}, bf16[64,768]{1,0:T(8,128)(2,1)S(1)}, u32[]{:S(2)}, u32[]{:S(2)}) collective-permute-start(bf16[64,768]{1,0:T(8,128)(2,1)S(1)} %slice.84), channel_id=1, source_target_pairs={{0,2},{2,4},{4,6},{6,0},{1,3},{3,5},{5,7},{7,1},{8,10},{10,12},{12... | collective-permute-start | bytes 294920 | tf_op jit(solution)/shard_map/ppermute | solution.py:32
  136.3 1.2 copy-start.5
  137.5 1.2 copy-start.7
  138.6 0.7 copy-start.11
  140.5 0.6 copy-start.12
  141.1 30.8 %all-to-all-start.2 = ((bf16[32,32,768]{2,1,0:T(8,128)(2,1)}), bf16[32,32,768]{2,1,0:T(8,128)(2,1)}, u32[]{:S(2)}, u32[]{:S(2)}) async-start(bf16[32,32,768]{2,1,0:T(8,128)(2,1)} %bitcast.51), calls=%async_computation.2 | async-start | bytes 3145728 | tf_op jit(solution)/shard_map/all_to_all | solution.py:197
  152.3 2.4 %collective-permute-start.21 = (bf16[512,768]{1,0:T(8,128)(2,1)S(1)}, bf16[512,768]{1,0:T(8,128)(2,1)S(1)}, u32[]{:S(2)}, u32[]{:S(2)}) collective-permute-start(bf16[512,768]{1,0:T(8,128)(2,1)S(1)} %constant_dynamic-update-slice_fusion.3.mine_ref), channel_id=1, source_target_pairs={{0,1},{1,0},{2,3},{3,2},{4,5},{5,4},{6,7},{7,6},{8,9},{9,8},{10,11... | collective-permute-start | bytes 2359304 | tf_op jit(solution)/shard_map/ppermute | solution.py:32
  154.7 1.3 copy-start.4
  160.8 1.2 copy-start.6
  162.0 1.2 copy-start.8
  172.0 26.5 %all-to-all-start.3 = ((bf16[32,32,768]{2,1,0:T(8,128)(2,1)}), bf16[32,32,768]{2,1,0:T(8,128)(2,1)}, u32[]{:S(2)}, u32[]{:S(2)}) async-start(bf16[32,32,768]{2,1,0:T(8,128)(2,1)} %bitcast.52), calls=%async_computation.3 | async-start | bytes 3145728 | tf_op jit(solution)/shard_map/all_to_all | solution.py:197
  177.2 4.0 %copy-start.9 = (bf16[1024,768]{1,0:T(8,128)(2,1)S(1)}, bf16[1024,768]{1,0:T(8,128)(2,1)}, u32[]{:S(2)}) copy-start(bf16[1024,768]{1,0:T(8,128)(2,1)} %copy-done.8) | copy-start | bytes 4718596

commit v4 on v3

--- a/solution.py
+++ b/solution.py
@@ -102,7 +102,7 @@
         compiler_params=pltpu.CompilerParams(vmem_limit_bytes=VMEM),
         cost_estimate=pl.CostEstimate(
             flops=2 * weigh * steps * tile * weight.size,
-            bytes_accessed=2 * (steps * tile * rows.shape[1] + weight.size) + 4 * steps * tile * width,
+            bytes_accessed=weigh * (2 * (steps * tile * rows.shape[1] + weight.size) + 4 * steps * tile * width),
             transcendentals=0,
         ),
     )(which, rows, weight, *later)
@@ -147,7 +147,7 @@
     )(place, mine, other, weight, *later)
 
 
-def local(kernel, outs, args, later=()):
+def local(kernel, outs, args, later=(), flops=0):
     def body(*refs):
         kernel(*refs[: len(args)], *refs[len(args) + len(later) :])
 
@@ -157,6 +157,7 @@
         out_specs=[pl.BlockSpec(memory_space=pltpu.VMEM)] * len(outs),
         out_shape=outs,
         compiler_params=pltpu.CompilerParams(vmem_limit_bytes=VMEM),
+        cost_estimate=pl.CostEstimate(flops=flops, bytes_accessed=0, transcendentals=0) if flops else None,
     )(*args, *later)
 
 
@@ -188,9 +189,9 @@
     ring = lax.axis_size("h")
     tile = tokens // (2 * ring)
 
-    def pair_sum(left, weight, turned, later=(), last=()):
-        away = move(product(left, weight, turned, BF16, tile, 1 - core, later=later), "c", 1)
-        total = product(left, weight, turned, F32, tile, core, later=last) + away.astype(F32)
+    def pair_sum(left, weight, turned, later=(), last=(), weigh=1):
+        away = move(product(left, weight, turned, BF16, tile, 1 - core, weigh, later), "c", 1)
+        total = product(left, weight, turned, F32, tile, core, weigh, last) + away.astype(F32)
         return total.reshape(ring, tile, -1)
 
     def rows_sum(partial):
@@ -219,19 +220,19 @@
     part = grad.shape[0] // 2
     grad_far = both_ways(grad_up[:part], grad_down[part:], "y")
     hidden, slope = local(
-        activate, [wire(tile), jax.ShapeDtypeStruct((tile, units), F32)], (own, up, down), grad_far
+        activate, [wire(tile), jax.ShapeDtypeStruct((tile, units), F32)], (own, up, down), (), 2 * 10**10
     )
     grad_all = ring_place(grad, grad_up, grad_down, *grad_far, "y").reshape(tokens, -1)
 
-    up, down = both_ways(hidden, hidden, "h")
-    own, ahead, far, behind = ring_split(pair_sum(grad_all, weight_out, True, (hidden,)), "h")
-    far_up, far_down = both_ways(stack(far[:cut], up[:cut]), stack(far[cut:], down[cut:]), "h")
-    mine = stack(hidden, down, far_up[cut:], far_down[cut:], up)
+    own, ahead, far, behind = ring_split(pair_sum(grad_all, weight_out, True, (ahead, behind), (), 0), "h")
+    up, down = both_ways(stack(hidden, far[:cut]), stack(hidden, far[cut:]), "h")
+    ahead, behind = local(pass_on, [wire(tile)] * 2, (ahead, up[tile:], behind, down[tile:]))
+    far_up, far_down = both_ways(stack(ahead, up[:cut]), stack(behind, down[cut:tile]), "h")
+    mine = stack(hidden, down[:tile], far_up[tile:], far_down[tile:], up[:tile])
     other = move(mine, "c", 1)
-    ahead, behind = local(pass_on, [wire(tile)] * 2, (ahead, far_up[:cut], behind, far_down[:cut]))
-    up, down = both_ways(ahead, behind, "h")
-    (grad_pre,) = local(weigh_slope, [wire(tile)], (own, up, down, slope), (other,))
+    (grad_pre,) = local(weigh_slope, [wire(tile)], (own, far_up[:tile], far_down[:tile], slope))
     up, down = both_ways(grad_pre, grad_pre, "h")
+
     place = jnp.stack([lax.axis_index("h"), core]).astype(jnp.int32)
     partial, hidden_all = joined_product(mine, other, weight_out, False, place)
     far_up, far_down = both_ways(up[:cut], down[cut:], "h")

time: 201 us -> 193 us (0.960)
  starting transfers between devices: 61.3 us -> 57 us
  waiting for transfers between devices: 94.3 us -> 90.4 us
    ppermute x22 -> x20, waiting for transfers between devices: 49.1 us -> 45.5 us  [move(): lax.ppermute(block, axis, [(i, (i + hops) % size) for i in range(size)])]
    ppermute x22 -> x20, starting transfers between devices: 33.9 us -> 31.7 us  [move(): lax.ppermute(block, axis, [(i, (i + hops) % size) for i in range(size)])]
    all_to_all x2, starting transfers between devices: 13.6 us -> 11.5 us  [rows_sum(): pieces = lax.all_to_all(partial.reshape(peers, rows, -1), FAR, 0, 0)]
    unnamed x34 -> x36, local copies, waits for them, and re-layouts: 11.2 us -> 11.2 us
  transfers between devices with their start and end apart: 26 -> 24, of which waited for: 15 -> 13; matrix products, arithmetic and copies ran while one was open for 7% -> 7% of each run, Pallas kernels for 7% -> 9%
where the time goes in v4:
time: 193 us
  waiting for transfers between devices  90.4 us (47%)
  starting transfers between devices  57 us (30%)
  Pallas kernels  16.7 us (9%)
  local copies, waits for them, and re-layouts  14.8 us (8%)
  matrix products  6.45 us (3%)
  other arithmetic  6.16 us (3%)
    ppermute x20, waiting for transfers between devices, move(): lax.ppermute(block, axis, [(i, (i + hops) % size) for i in range(size)])  45.5 us
    ppermute x20, starting transfers between devices, move(): lax.ppermute(block, axis, [(i, (i + hops) % size) for i in range(size)])  31.7 us
    all_to_all x2, waiting for transfers between devices, copies(): return lax.all_to_all(sent, axes, 0, 0).reshape(size * rows, -1)  24 us
    all_to_all x2, waiting for transfers between devices, rows_sum(): pieces = lax.all_to_all(partial.reshape(peers, rows, -1), FAR, 0, 0)  21 us
    all_to_all x2, starting transfers between devices, copies(): return lax.all_to_all(sent, axes, 0, 0).reshape(size * rows, -1)  13.8 us
    all_to_all x2, starting transfers between devices, rows_sum(): pieces = lax.all_to_all(partial.reshape(peers, rows, -1), FAR, 0, 0)  11.5 us
    unnamed x36, local copies, waits for them, and re-layouts  11.2 us
    pallas_call x2, Pallas kernels, joined_product(): pl.pallas_call(functools.partial(joined_kernel, turned), grid_spec=pltpu....  8.12 us
  transfers between devices with their start and end apart: 24, of which 13 were waited for; matrix products, arithmetic and copies ran while one was open for 7% of the time, Pallas kernels for 9%

profile of v4, /device:TPU:2, one launch (start us, length us, event | category | flops | bytes accessed | tf_op | source)
XLA Modules:
  0.0 192.6 jit_solution(13740829614917841581)
XLA Ops:
  0.6 2.2 %broadcast_in_dim.31 = bf16[32,32,768]{2,1,0:T(8,128)(2,1)} broadcast(bf16[32,768]{1,0:T(8,128)(2,1)} %param.4), dimensions={1,2} | broadcast | bytes 1622016 | tf_op jit(solution)/shard_map/broadcast_in_dim | solution.py:203
  2.8 9.1 %all-to-all-start = ((bf16[32,32,768]{2,1,0:T(8,128)(2,1)}), bf16[32,32,768]{2,1,0:T(8,128)(2,1)S(1)}, u32[]{:S(2)}, u32[]{:S(2)}) async-start(bf16[32,32,768]{2,1,0:T(8,128)(2,1)} %broadcast_in_dim.31), calls=%async_computation | async-start | bytes 3145728 | tf_op jit(solution)/shard_map/all_to_all | solution.py:204
  11.9 22.6 %all-to-all-done = bf16[32,32,768]{2,1,0:T(8,128)(2,1)S(1)} async-done(((bf16[32,32,768]{2,1,0:T(8,128)(2,1)}), bf16[32,32,768]{2,1,0:T(8,128)(2,1)S(1)}, u32[]{:S(2)}, u32[]{:S(2)}) %all-to-all-start) | async-done | bytes 1572896 | tf_op jit(solution)/shard_map/all_to_all | solution.py:204
  34.5 0.8 broadcast_in_dim.32
  35.3 4.6 %all-to-all-start.1 = ((bf16[8,32,768]{2,1,0:T(8,128)(2,1)}), bf16[8,32,768]{2,1,0:T(8,128)(2,1)S(1)}, u32[]{:S(2)}, u32[]{:S(2)}) async-start(bf16[8,32,768]{2,1,0:T(8,128)(2,1)} %broadcast_in_dim.32), calls=%async_computation.1 | async-start | bytes 786432 | tf_op jit(solution)/shard_map/all_to_all | solution.py:204
  39.9 2.3 %shard_map.76 = bf16[512,768]{1,0:T(8,128)(2,1)} custom-call(s32[1]{0:T(128)} %bitcast.3.which_ref, bf16[1024,768]{1,0:T(8,128)(2,1)S(1)} %bitcast.45, bf16[768,768]{1,0:T(8,128)(2,1)S(1)} %copy-done.3), custom_call_target="tpu_custom_call" | custom-call | flops 603979776 | bytes 3538944 | tf_op jit(solution)/shard_map/pallas_call | solution.py:89
  42.3 1.3 shard_map.75
  43.6 1.2 copy-done
  44.8 1.4 all-to-all-done.1
  46.2 0.8 collective-permute-start.4
  47.0 1.2 collective-permute-start.3
  48.2 0.1 broadcast_in_dim.33
  48.3 1.3 convert_add_fusion.1
  49.7 5.5 %collective-permute-start.2 = (bf16[64,768]{1,0:T(8,128)(2,1)S(1)}, bf16[64,768]{1,0:T(8,128)(2,1)S(1)}, u32[]{:S(2)}, u32[]{:S(2)}) collective-permute-start(bf16[64,768]{1,0:T(8,128)(2,1)S(1)} %get-tuple-element.48), channel_id=1, source_target_pairs={{0,6},{2,0},{4,2},{6,4},{1,7},{3,1},{5,3},{7,5},{8,14},{10,8},{12,... | collective-permute-start | bytes 294920 | tf_op jit(solution)/shard_map/ppermute | solution.py:32
  55.2 0.1 dynamic-slice_bitcast_fusion.3
  55.3 1.0 collective-permute-done.4.refs_5_
  56.3 2.1 %collective-permute-start.8 = (bf16[128,768]{1,0:T(8,128)(2,1)S(1)}, bf16[128,768]{1,0:T(8,128)(2,1)S(1)}, u32[]{:S(2)}, u32[]{:S(2)}) collective-permute-start(bf16[128,768]{1,0:T(8,128)(2,1)S(1)} %slice.91), channel_id=1, source_target_pairs={{0,48},{16,0},{32,16},{48,32},{1,49},{17,1},{33,17},{49,33},{2,50}... | collective-permute-start | bytes 589832 | tf_op jit(solution)/shard_map/ppermute | solution.py:32
  58.4 0.1 collective-permute-start.7
  58.5 3.9 %collective-permute-done.1.refs_1_ = bf16[64,768]{1,0:T(8,128)(2,1)S(1)} collective-permute-done((bf16[64,768]{1,0:T(8,128)(2,1)S(1)}, bf16[64,768]{1,0:T(8,128)(2,1)S(1)}, u32[]{:S(2)}, u32[]{:S(2)}) %collective-permute-start.1) | collective-permute-done | bytes 98336 | tf_op jit(solution)/shard_map/ppermute | solution.py:32
  62.5 0.1 collective-permute-start.5
  62.6 4.1 %collective-permute-start.6 = (bf16[128,768]{1,0:T(8,128)(2,1)S(1)}, bf16[128,768]{1,0:T(8,128)(2,1)S(1)}, u32[]{:S(2)}, u32[]{:S(2)}) collective-permute-start(bf16[128,768]{1,0:T(8,128)(2,1)S(1)} %get-tuple-element.22.refs_1_), channel_id=1, source_target_pairs={{0,6},{2,0},{4,2},{6,4},{1,7},{3,1},{5,3},{7,5},{8,14},{10,8},{12,... | collective-permute-start | bytes 589832 | tf_op jit(solution)/shard_map/ppermute | solution.py:32
  66.9 2.2 %shard_map.80 = bf16[512,768]{1,0:T(8,128)(2,1)S(1)} custom-call(s32[1]{0:T(128)} %bitcast.3.which_ref, bf16[1024,768]{1,0:T(8,128)(2,1)S(1)} %bitcast.48, bf16[768,768]{1,0:T(8,128)(2,1)S(1)} %copy-done.2, bf16[128,768]{1,0:T(8,128)(2,1)S(1)} %get-tuple-element.21.refs_0_, bf16[128,768]{1,0:T(8,128)(2,1)S(1)} %get-tuple-element.22.refs_1_), custom_call_target="tpu_custom_call" | custom-call | tf_op jit(solution)/shard_map/pallas_call | solution.py:89
  69.1 0.1 collective-permute-start.9
  69.2 4.6 %collective-permute-done.5.refs_1_ = bf16[128,768]{1,0:T(8,128)(2,1)S(1)} collective-permute-done((bf16[128,768]{1,0:T(8,128)(2,1)S(1)}, bf16[128,768]{1,0:T(8,128)(2,1)S(1)}, u32[]{:S(2)}, u32[]{:S(2)}) %collective-permute-start.5) | collective-permute-done | bytes 196640 | tf_op jit(solution)/shard_map/ppermute | solution.py:32
  73.8 0.3 shard_map.78
  74.1 2.2 %shard_map.79 = f32[512,768]{1,0:T(8,128)S(1)} custom-call(s32[1]{0:T(128)} %bitcast.1.which_ref, bf16[1024,768]{1,0:T(8,128)(2,1)S(1)} %bitcast.49, bf16[768,768]{1,0:T(8,128)(2,1)S(1)} %copy-done.2), custom_call_target="tpu_custom_call" | custom-call | tf_op jit(solution)/shard_map/pallas_call | solution.py:89
  76.3 0.1 convert_add_fusion
  76.6 2.4 %collective-permute-start.11 = (bf16[192,768]{1,0:T(8,128)(2,1)S(1)}, bf16[192,768]{1,0:T(8,128)(2,1)S(1)}, u32[]{:S(2)}, u32[]{:S(2)}) collective-permute-start(bf16[192,768]{1,0:T(8,128)(2,1)S(1)} %get-tuple-element.44), channel_id=1, source_target_pairs={{0,2},{2,4},{4,6},{6,0},{1,3},{3,5},{5,7},{7,1},{8,10},{10,12},{12... | collective-permute-start | bytes 884744 | tf_op jit(solution)/shard_map/ppermute | solution.py:32
  79.0 2.1 %collective-permute-start.10 = (bf16[192,768]{1,0:T(8,128)(2,1)S(1)}, bf16[192,768]{1,0:T(8,128)(2,1)S(1)}, u32[]{:S(2)}, u32[]{:S(2)}) collective-permute-start(bf16[192,768]{1,0:T(8,128)(2,1)S(1)} %get-tuple-element.45), channel_id=1, source_target_pairs={{0,6},{2,0},{4,2},{6,4},{1,7},{3,1},{5,3},{7,5},{8,14},{10,8},{12,... | collective-permute-start | bytes 884744 | tf_op jit(solution)/shard_map/ppermute | solution.py:32
  81.1 0.1 dynamic-slice_bitcast_fusion
  81.2 8.1 %collective-permute-done.11 = bf16[192,768]{1,0:T(8,128)(2,1)S(1)} collective-permute-done((bf16[192,768]{1,0:T(8,128)(2,1)S(1)}, bf16[192,768]{1,0:T(8,128)(2,1)S(1)}, u32[]{:S(2)}, u32[]{:S(2)}) %collective-permute-start.11) | collective-permute-done | bytes 294944 | tf_op jit(solution)/shard_map/ppermute | solution.py:32
  89.3 3.6 %collective-permute-done.10 = bf16[192,768]{1,0:T(8,128)(2,1)S(1)} collective-permute-done((bf16[192,768]{1,0:T(8,128)(2,1)S(1)}, bf16[192,768]{1,0:T(8,128)(2,1)S(1)}, u32[]{:S(2)}, u32[]{:S(2)}) %collective-permute-start.10) | collective-permute-done | bytes 294944 | tf_op jit(solution)/shard_map/ppermute | solution.py:32
  93.0 1.7 collective-permute-start.12
  94.6 2.6 %collective-permute-start.13 = (bf16[192,768]{1,0:T(8,128)(2,1)S(1)}, bf16[192,768]{1,0:T(8,128)(2,1)S(1)}, u32[]{:S(2)}, u32[]{:S(2)}) collective-permute-start(bf16[192,768]{1,0:T(8,128)(2,1)S(1)} %pad_maximum_fusion.3), channel_id=1, source_target_pairs={{0,6},{2,0},{4,2},{6,4},{1,7},{3,1},{5,3},{7,5},{8,14},{10,8},{12,... | collective-permute-start | bytes 884744 | tf_op jit(solution)/shard_map/ppermute | solution.py:32
  97.3 11.4 %collective-permute-done.12 = bf16[192,768]{1,0:T(8,128)(2,1)S(1)} collective-permute-done((bf16[192,768]{1,0:T(8,128)(2,1)S(1)}, bf16[192,768]{1,0:T(8,128)(2,1)S(1)}, u32[]{:S(2)}, u32[]{:S(2)}) %collective-permute-start.12) | collective-permute-done | bytes 294944 | tf_op jit(solution)/shard_map/ppermute | solution.py:32
  108.8 0.1 collective-permute-start.14
  108.9 0.1 shard_map.83
  109.0 4.0 %collective-permute-start.17 = (bf16[128,768]{1,0:T(8,128)(2,1)S(1)}, bf16[128,768]{1,0:T(8,128)(2,1)S(1)}, u32[]{:S(2)}, u32[]{:S(2)}) collective-permute-start(bf16[128,768]{1,0:T(8,128)(2,1)S(1)} %shard_map.83), channel_id=1, source_target_pairs={{0,6},{2,0},{4,2},{6,4},{1,7},{3,1},{5,3},{7,5},{8,14},{10,8},{12,... | collective-permute-start | bytes 589832 | tf_op jit(solution)/shard_map/ppermute | solution.py:32
  113.1 8.6 %collective-permute-done.17 = bf16[128,768]{1,0:T(8,128)(2,1)S(1)} collective-permute-done((bf16[128,768]{1,0:T(8,128)(2,1)S(1)}, bf16[128,768]{1,0:T(8,128)(2,1)S(1)}, u32[]{:S(2)}, u32[]{:S(2)}) %collective-permute-start.17) | collective-permute-done | bytes 196640 | tf_op jit(solution)/shard_map/ppermute | solution.py:32
  121.8 4.6 %collective-permute-start.18 = (bf16[64,768]{1,0:T(8,128)(2,1)S(1)}, bf16[64,768]{1,0:T(8,128)(2,1)S(1)}, u32[]{:S(2)}, u32[]{:S(2)}) collective-permute-start(bf16[64,768]{1,0:T(8,128)(2,1)S(1)} %slice.105), channel_id=1, source_target_pairs={{0,6},{2,0},{4,2},{6,4},{1,7},{3,1},{5,3},{7,5},{8,14},{10,8},{12,... | collective-permute-start | bytes 294920 | tf_op jit(solution)/shard_map/ppermute | solution.py:32
  126.4 0.1 collective-permute-start.16
  126.5 3.2 %shard_map.82 = (bf16[1024,768]{1,0:T(8,128)(2,1)S(1)}, bf16[1024,768]{1,0:T(8,128)(2,1)S(1)}) custom-call(s32[2]{0:T(128)S(1)} %pad_add_fusion.place_ref, bf16[512,768]{1,0:T(8,128)(2,1)S(1)} %slice_dynamic-update-slice_fusion.mine_ref, bf16[512,768]{1,0:T(8,128)(2,1)S(1)} %collective-permute-done.14.other_ref, bf16[768,768]{1,0:T(8,128)(2,1)S(1)} %copy-done.2), custom_call_target="tpu_custom_call" | custom-call | flops 1207959552 | bytes 5898240 | tf_op jit(solution)/shard_map/pallas_call | solution.py:127
  129.7 1.1 copy-done.5
  130.9 1.2 copy-done.7
  132.1 0.7 copy-done.11
  132.7 2.0 %collective-permute-done.16 = bf16[64,768]{1,0:T(8,128)(2,1)S(1)} collective-permute-done((bf16[64,768]{1,0:T(8,128)(2,1)S(1)}, bf16[64,768]{1,0:T(8,128)(2,1)S(1)}, u32[]{:S(2)}, u32[]{:S(2)}) %collective-permute-start.16) | collective-permute-done | bytes 98336 | tf_op jit(solution)/shard_map/ppermute | solution.py:32
  134.7 0.6 copy-done.12
  135.4 6.2 %all-to-all-start.2 = ((bf16[32,32,768]{2,1,0:T(8,128)(2,1)}), bf16[32,32,768]{2,1,0:T(8,128)(2,1)}, u32[]{:S(2)}, u32[]{:S(2)}) async-start(bf16[32,32,768]{2,1,0:T(8,128)(2,1)} %bitcast.51), calls=%async_computation.2 | async-start | bytes 3145728 | tf_op jit(solution)/shard_map/all_to_all | solution.py:198
  141.6 0.9 constant_dynamic-update-slice_fusion.4
  142.6 0.9 constant_dynamic-update-slice_fusion.3
  143.5 0.9 constant_dynamic-update-slice_fusion.2
  144.4 0.1 collective-permute-start.19
  144.5 2.3 %collective-permute-done.19.other_ref = bf16[512,768]{1,0:T(8,128)(2,1)S(1)} collective-permute-done((bf16[512,768]{1,0:T(8,128)(2,1)S(1)}, bf16[512,768]{1,0:T(8,128)(2,1)S(1)}, u32[]{:S(2)}, u32[]{:S(2)}) %collective-permute-start.19) | collective-permute-done | bytes 786464 | tf_op jit(solution)/shard_map/ppermute | solution.py:32
  146.7 1.3 copy-done.4
  148.0 4.9 %shard_map.84 = (bf16[1024,768]{1,0:T(8,128)(2,1)S(1)}, bf16[1024,768]{1,0:T(8,128)(2,1)S(1)}) custom-call(s32[2]{0:T(128)S(1)} %pad_add_fusion.place_ref, bf16[512,768]{1,0:T(8,128)(2,1)S(1)} %constant_dynamic-update-slice_fusion.1.mine_ref, bf16[512,768]{1,0:T(8,128)(2,1)S(1)} %collective-permute-done.19.other_ref, bf16[768,768]{1,0:T(8,128)(2,1)S(1)} %copy-done.4), custom_call_target="tpu_custom_call" | custom-call | flops 1207959552 | bytes 5898240 | tf_op jit(solution)/shard_map/pallas_call | solution.py:127
  152.9 1.2 copy-done.6
  154.1 1.2 copy-done.8
  155.3 8.2 %all-to-all-done.2 = bf16[32,32,768]{2,1,0:T(8,128)(2,1)} async-done(((bf16[32,32,768]{2,1,0:T(8,128)(2,1)}), bf16[32,32,768]{2,1,0:T(8,128)(2,1)}, u32[]{:S(2)}, u32[]{:S(2)}) %all-to-all-start.2) | async-done | bytes 1572896 | tf_op jit(solution)/shard_map/all_to_all | solution.py:198
  163.6 5.3 %all-to-all-start.3 = ((bf16[32,32,768]{2,1,0:T(8,128)(2,1)}), bf16[32,32,768]{2,1,0:T(8,128)(2,1)}, u32[]{:S(2)}, u32[]{:S(2)}) async-start(bf16[32,32,768]{2,1,0:T(8,128)(2,1)} %bitcast.52), calls=%async_computation.3 | async-start | bytes 3145728 | tf_op jit(solution)/shard_map/all_to_all | solution.py:198
  168.9 4.0 %convolution_convert_fusion = bf16[768,768]{1,0:T(8,128)(2,1)} fusion(bf16[1024,768]{1,0:T(8,128)(2,1)} %copy-done.7, bf16[1024,768]{1,0:T(8,128)(2,1)S(1)} %bitcast.50), kind=kOutput, calls=%fused_computation.2 | convolution fusion | flops 1208549376 | bytes 4325376 | tf_op jit(solution)/shard_map/dot_general | solution.py:27
  172.9 2.5 %convolution_convert_fusion.1 = bf16[768,768]{1,0:T(8,128)(2,1)} fusion(bf16[1024,768]{1,0:T(8,128)(2,1)S(1)} %bitcast.47, bf16[1024,768]{1,0:T(8,128)(2,1)S(1)} %copy-done.9), kind=kOutput, calls=%fused_computation.3 | convolution fusion | flops 1208549376 | bytes 4325376 | tf_op jit(solution)/shard_map/dot_general | solution.py:27
  175.3 2.3 %reduce_sum.24 = bf16[32,768]{1,0:T(8,128)(2,1)} reduce(bf16[32,32,768]{2,1,0:T(8,128)(2,1)} %all-to-all-done.2, bf16[]{:T(256)} %constant.97.clone.1), dimensions={0}, to_apply=%region_0.1 | reduce | flops 761856 | bytes 1622018 | tf_op jit(solution)/shard_map/reduce_sum | solution.py:199
  177.6 12.7 %all-to-all-done.3 = bf16[32,32,768]{2,1,0:T(8,128)(2,1)} async-done(((bf16[32,32,768]{2,1,0:T(8,128)(2,1)}), bf16[32,32,768]{2,1,0:T(8,128)(2,1)}, u32[]{:S(2)}, u32[]{:S(2)}) %all-to-all-start.3) | async-done | bytes 1572896 | tf_op jit(solution)/shard_map/all_to_all | solution.py:198
  190.3 2.3 %reduce_sum.25 = bf16[32,768]{1,0:T(8,128)(2,1)} reduce(bf16[32,32,768]{2,1,0:T(8,128)(2,1)} %all-to-all-done.3, bf16[]{:T(256)} %constant.97.clone.1), dimensions={0}, to_apply=%region_1.2 | reduce | flops 761856 | bytes 1622018 | tf_op jit(solution)/shard_map/reduce_sum | solution.py:199
  (64 shorter events, 0.8 us)
Async XLA Ops:
  2.8 31.7 %copy-start.13 = (bf16[32,768]{1,0:T(8,128)(2,1)S(1)}, bf16[32,768]{1,0:T(8,128)(2,1)}, u32[]{:S(2)}) copy-start(bf16[32,768]{1,0:T(8,128)(2,1)} %param.7) | copy-start | bytes 147460
  2.8 37.1 %copy-start.3 = (bf16[768,768]{1,0:T(8,128)(2,1)S(1)}, bf16[768,768]{1,0:T(8,128)(2,1)}, u32[]{:S(2)}) copy-start(bf16[768,768]{1,0:T(8,128)(2,1)} %weight_ref.11) | copy-start | bytes 3538948
  2.8 31.7 %all-to-all-start = ((bf16[32,32,768]{2,1,0:T(8,128)(2,1)}), bf16[32,32,768]{2,1,0:T(8,128)(2,1)S(1)}, u32[]{:S(2)}, u32[]{:S(2)}) async-start(bf16[32,32,768]{2,1,0:T(8,128)(2,1)} %broadcast_in_dim.31), calls=%async_computation | async-start | bytes 3145728 | tf_op jit(solution)/shard_map/all_to_all | solution.py:204
  35.3 10.9 %all-to-all-start.1 = ((bf16[8,32,768]{2,1,0:T(8,128)(2,1)}), bf16[8,32,768]{2,1,0:T(8,128)(2,1)S(1)}, u32[]{:S(2)}, u32[]{:S(2)}) async-start(bf16[8,32,768]{2,1,0:T(8,128)(2,1)} %broadcast_in_dim.32), calls=%async_computation.1 | async-start | bytes 786432 | tf_op jit(solution)/shard_map/all_to_all | solution.py:204
  42.3 6.1 %collective-permute-start = (bf16[512,768]{1,0:T(8,128)(2,1)}, bf16[512,768]{1,0:T(8,128)(2,1)}, u32[]{:S(2)}, u32[]{:S(2)}) collective-permute-start(bf16[512,768]{1,0:T(8,128)(2,1)} %shard_map.76), channel_id=1, source_target_pairs={{0,1},{1,0},{2,3},{3,2},{4,5},{5,4},{6,7},{7,6},{8,9},{9,8},{10,11... | collective-permute-start | bytes 2359304 | tf_op jit(solution)/shard_map/ppermute | solution.py:32
  43.6 1.2 copy-start
  46.1 2.2 %copy-start.1 = (f32[512,768]{1,0:T(8,128)S(1)}, f32[512,768]{1,0:T(8,128)}, u32[]{:S(2)}) copy-start(f32[512,768]{1,0:T(8,128)} %copy-done) | copy-start | bytes 4718596
  46.2 10.2 %collective-permute-start.4 = (bf16[256,768]{1,0:T(8,128)(2,1)S(1)}, bf16[256,768]{1,0:T(8,128)(2,1)S(1)}, u32[]{:S(2)}, u32[]{:S(2)}) collective-permute-start(bf16[256,768]{1,0:T(8,128)(2,1)S(1)} %bitcast.57), channel_id=1, source_target_pairs={{0,48},{16,0},{32,16},{48,32},{1,49},{17,1},{33,17},{49,33},{2,50}... | collective-permute-start | bytes 1179656 | tf_op jit(solution)/shard_map/ppermute | solution.py:32
  47.0 11.5 %collective-permute-start.3 = (bf16[256,768]{1,0:T(8,128)(2,1)S(1)}, bf16[256,768]{1,0:T(8,128)(2,1)S(1)}, u32[]{:S(2)}, u32[]{:S(2)}) collective-permute-start(bf16[256,768]{1,0:T(8,128)(2,1)S(1)} %bitcast.58), channel_id=1, source_target_pairs={{0,16},{16,32},{32,48},{48,0},{1,17},{17,33},{33,49},{49,1},{2,18}... | collective-permute-start | bytes 1179656 | tf_op jit(solution)/shard_map/ppermute | solution.py:32
  49.7 8.8 %collective-permute-start.2 = (bf16[64,768]{1,0:T(8,128)(2,1)S(1)}, bf16[64,768]{1,0:T(8,128)(2,1)S(1)}, u32[]{:S(2)}, u32[]{:S(2)}) collective-permute-start(bf16[64,768]{1,0:T(8,128)(2,1)S(1)} %get-tuple-element.48), channel_id=1, source_target_pairs={{0,6},{2,0},{4,2},{6,4},{1,7},{3,1},{5,3},{7,5},{8,14},{10,8},{12,... | collective-permute-start | bytes 294920 | tf_op jit(solution)/shard_map/ppermute | solution.py:32
  55.2 7.2 %collective-permute-start.1 = (bf16[64,768]{1,0:T(8,128)(2,1)S(1)}, bf16[64,768]{1,0:T(8,128)(2,1)S(1)}, u32[]{:S(2)}, u32[]{:S(2)}) collective-permute-start(bf16[64,768]{1,0:T(8,128)(2,1)S(1)} %get-tuple-element.49), channel_id=1, source_target_pairs={{0,2},{2,4},{4,6},{6,0},{1,3},{3,5},{5,7},{7,1},{8,10},{10,12},{12... | collective-permute-start | bytes 294920 | tf_op jit(solution)/shard_map/ppermute | solution.py:32
  56.3 10.5 %collective-permute-start.8 = (bf16[128,768]{1,0:T(8,128)(2,1)S(1)}, bf16[128,768]{1,0:T(8,128)(2,1)S(1)}, u32[]{:S(2)}, u32[]{:S(2)}) collective-permute-start(bf16[128,768]{1,0:T(8,128)(2,1)S(1)} %slice.91), channel_id=1, source_target_pairs={{0,48},{16,0},{32,16},{48,32},{1,49},{17,1},{33,17},{49,33},{2,50}... | collective-permute-start | bytes 589832 | tf_op jit(solution)/shard_map/ppermute | solution.py:32
  58.4 8.3 %collective-permute-start.7 = (bf16[128,768]{1,0:T(8,128)(2,1)S(1)}, bf16[128,768]{1,0:T(8,128)(2,1)S(1)}, u32[]{:S(2)}, u32[]{:S(2)}) collective-permute-start(bf16[128,768]{1,0:T(8,128)(2,1)S(1)} %slice.90), channel_id=1, source_target_pairs={{0,16},{16,32},{32,48},{48,0},{1,17},{17,33},{33,49},{49,1},{2,18}... | collective-permute-start | bytes 589832 | tf_op jit(solution)/shard_map/ppermute | solution.py:32
  62.5 4.4 %copy-start.2 = (bf16[768,768]{1,0:T(8,128)(2,1)S(1)}, bf16[768,768]{1,0:T(8,128)(2,1)}, u32[]{:S(2)}) copy-start(bf16[768,768]{1,0:T(8,128)(2,1)} %weight_ref.10) | copy-start | bytes 3538948
  62.5 11.3 %collective-permute-start.5 = (bf16[128,768]{1,0:T(8,128)(2,1)S(1)}, bf16[128,768]{1,0:T(8,128)(2,1)S(1)}, u32[]{:S(2)}, u32[]{:S(2)}) collective-permute-start(bf16[128,768]{1,0:T(8,128)(2,1)S(1)} %get-tuple-element.21.refs_0_), channel_id=1, source_target_pairs={{0,2},{2,4},{4,6},{6,0},{1,3},{3,5},{5,7},{7,1},{8,10},{10,12},{12... | collective-permute-start | bytes 589832 | tf_op jit(solution)/shard_map/ppermute | solution.py:32
  62.6 11.2 %collective-permute-start.6 = (bf16[128,768]{1,0:T(8,128)(2,1)S(1)}, bf16[128,768]{1,0:T(8,128)(2,1)S(1)}, u32[]{:S(2)}, u32[]{:S(2)}) collective-permute-start(bf16[128,768]{1,0:T(8,128)(2,1)S(1)} %get-tuple-element.22.refs_1_), channel_id=1, source_target_pairs={{0,6},{2,0},{4,2},{6,4},{1,7},{3,1},{5,3},{7,5},{8,14},{10,8},{12,... | collective-permute-start | bytes 589832 | tf_op jit(solution)/shard_map/ppermute | solution.py:32
  69.1 7.3 %collective-permute-start.9 = (bf16[512,768]{1,0:T(8,128)(2,1)S(1)}, bf16[512,768]{1,0:T(8,128)(2,1)S(1)}, u32[]{:S(2)}, u32[]{:S(2)}) collective-permute-start(bf16[512,768]{1,0:T(8,128)(2,1)S(1)} %shard_map.80), channel_id=1, source_target_pairs={{0,1},{1,0},{2,3},{3,2},{4,5},{5,4},{6,7},{7,6},{8,9},{9,8},{10,11... | collective-permute-start | bytes 2359304 | tf_op jit(solution)/shard_map/ppermute | solution.py:32
  76.6 12.6 %collective-permute-start.11 = (bf16[192,768]{1,0:T(8,128)(2,1)S(1)}, bf16[192,768]{1,0:T(8,128)(2,1)S(1)}, u32[]{:S(2)}, u32[]{:S(2)}) collective-permute-start(bf16[192,768]{1,0:T(8,128)(2,1)S(1)} %get-tuple-element.44), channel_id=1, source_target_pairs={{0,2},{2,4},{4,6},{6,0},{1,3},{3,5},{5,7},{7,1},{8,10},{10,12},{12... | collective-permute-start | bytes 884744 | tf_op jit(solution)/shard_map/ppermute | solution.py:32
  79.0 13.8 %collective-permute-start.10 = (bf16[192,768]{1,0:T(8,128)(2,1)S(1)}, bf16[192,768]{1,0:T(8,128)(2,1)S(1)}, u32[]{:S(2)}, u32[]{:S(2)}) collective-permute-start(bf16[192,768]{1,0:T(8,128)(2,1)S(1)} %get-tuple-element.45), channel_id=1, source_target_pairs={{0,6},{2,0},{4,2},{6,4},{1,7},{3,1},{5,3},{7,5},{8,14},{10,8},{12,... | collective-permute-start | bytes 884744 | tf_op jit(solution)/shard_map/ppermute | solution.py:32
  93.0 15.8 %collective-permute-start.12 = (bf16[192,768]{1,0:T(8,128)(2,1)S(1)}, bf16[192,768]{1,0:T(8,128)(2,1)S(1)}, u32[]{:S(2)}, u32[]{:S(2)}) collective-permute-start(bf16[192,768]{1,0:T(8,128)(2,1)S(1)} %pad_maximum_fusion.2), channel_id=1, source_target_pairs={{0,2},{2,4},{4,6},{6,0},{1,3},{3,5},{5,7},{7,1},{8,10},{10,12},{12... | collective-permute-start | bytes 884744 | tf_op jit(solution)/shard_map/ppermute | solution.py:32
  94.6 14.1 %collective-permute-start.13 = (bf16[192,768]{1,0:T(8,128)(2,1)S(1)}, bf16[192,768]{1,0:T(8,128)(2,1)S(1)}, u32[]{:S(2)}, u32[]{:S(2)}) collective-permute-start(bf16[192,768]{1,0:T(8,128)(2,1)S(1)} %pad_maximum_fusion.3), channel_id=1, source_target_pairs={{0,6},{2,0},{4,2},{6,4},{1,7},{3,1},{5,3},{7,5},{8,14},{10,8},{12,... | collective-permute-start | bytes 884744 | tf_op jit(solution)/shard_map/ppermute | solution.py:32
  108.8 17.7 %collective-permute-start.14 = (bf16[512,768]{1,0:T(8,128)(2,1)S(1)}, bf16[512,768]{1,0:T(8,128)(2,1)S(1)}, u32[]{:S(2)}, u32[]{:S(2)}) collective-permute-start(bf16[512,768]{1,0:T(8,128)(2,1)S(1)} %slice_dynamic-update-slice_fusion.mine_ref), channel_id=1, source_target_pairs={{0,1},{1,0},{2,3},{3,2},{4,5},{5,4},{6,7},{7,6},{8,9},{9,8},{10,11... | collective-permute-start | bytes 2359304 | tf_op jit(solution)/shard_map/ppermute | solution.py:32
  109.0 12.7 %collective-permute-start.17 = (bf16[128,768]{1,0:T(8,128)(2,1)S(1)}, bf16[128,768]{1,0:T(8,128)(2,1)S(1)}, u32[]{:S(2)}, u32[]{:S(2)}) collective-permute-start(bf16[128,768]{1,0:T(8,128)(2,1)S(1)} %shard_map.83), channel_id=1, source_target_pairs={{0,6},{2,0},{4,2},{6,4},{1,7},{3,1},{5,3},{7,5},{8,14},{10,8},{12,... | collective-permute-start | bytes 589832 | tf_op jit(solution)/shard_map/ppermute | solution.py:32
  113.1 13.3 %collective-permute-start.15 = (bf16[128,768]{1,0:T(8,128)(2,1)S(1)}, bf16[128,768]{1,0:T(8,128)(2,1)S(1)}, u32[]{:S(2)}, u32[]{:S(2)}) collective-permute-start(bf16[128,768]{1,0:T(8,128)(2,1)S(1)} %shard_map.83), channel_id=1, source_target_pairs={{0,2},{2,4},{4,6},{6,0},{1,3},{3,5},{5,7},{7,1},{8,10},{10,12},{12... | collective-permute-start | bytes 589832 | tf_op jit(solution)/shard_map/ppermute | solution.py:32
  121.7 8.0 %copy-start.10 = (bf16[128,768]{1,0:T(8,128)(2,1)}, bf16[128,768]{1,0:T(8,128)(2,1)S(1)}, u32[]{:S(2)}) copy-start(bf16[128,768]{1,0:T(8,128)(2,1)S(1)} %collective-permute-done.17) | copy-start | bytes 589828
  121.8 10.3 %collective-permute-start.18 = (bf16[64,768]{1,0:T(8,128)(2,1)S(1)}, bf16[64,768]{1,0:T(8,128)(2,1)S(1)}, u32[]{:S(2)}, u32[]{:S(2)}) collective-permute-start(bf16[64,768]{1,0:T(8,128)(2,1)S(1)} %slice.105), channel_id=1, source_target_pairs={{0,6},{2,0},{4,2},{6,4},{1,7},{3,1},{5,3},{7,5},{8,14},{10,8},{12,... | collective-permute-start | bytes 294920 | tf_op jit(solution)/shard_map/ppermute | solution.py:32
  126.4 8.3 %collective-permute-start.16 = (bf16[64,768]{1,0:T(8,128)(2,1)S(1)}, bf16[64,768]{1,0:T(8,128)(2,1)S(1)}, u32[]{:S(2)}, u32[]{:S(2)}) collective-permute-start(bf16[64,768]{1,0:T(8,128)(2,1)S(1)} %slice.104), channel_id=1, source_target_pairs={{0,2},{2,4},{4,6},{6,0},{1,3},{3,5},{5,7},{7,1},{8,10},{10,12},{12... | collective-permute-start | bytes 294920 | tf_op jit(solution)/shard_map/ppermute | solution.py:32
  129.7 1.2 copy-start.5
  130.9 1.2 copy-start.7
  132.1 0.7 copy-start.11
  134.7 0.6 copy-start.12
  135.4 28.2 %all-to-all-start.2 = ((bf16[32,32,768]{2,1,0:T(8,128)(2,1)}), bf16[32,32,768]{2,1,0:T(8,128)(2,1)}, u32[]{:S(2)}, u32[]{:S(2)}) async-start(bf16[32,32,768]{2,1,0:T(8,128)(2,1)} %bitcast.51), calls=%async_computation.2 | async-start | bytes 3145728 | tf_op jit(solution)/shard_map/all_to_all | solution.py:198
  144.4 2.4 %collective-permute-start.19 = (bf16[512,768]{1,0:T(8,128)(2,1)S(1)}, bf16[512,768]{1,0:T(8,128)(2,1)S(1)}, u32[]{:S(2)}, u32[]{:S(2)}) collective-permute-start(bf16[512,768]{1,0:T(8,128)(2,1)S(1)} %constant_dynamic-update-slice_fusion.1.mine_ref), channel_id=1, source_target_pairs={{0,1},{1,0},{2,3},{3,2},{4,5},{5,4},{6,7},{7,6},{8,9},{9,8},{10,11... | collective-permute-start | bytes 2359304 | tf_op jit(solution)/shard_map/ppermute | solution.py:32
  146.7 1.3 copy-start.4
  152.9 1.2 copy-start.6
  154.1 1.2 copy-start.8
  163.6 26.7 %all-to-all-start.3 = ((bf16[32,32,768]{2,1,0:T(8,128)(2,1)}), bf16[32,32,768]{2,1,0:T(8,128)(2,1)}, u32[]{:S(2)}, u32[]{:S(2)}) async-start(bf16[32,32,768]{2,1,0:T(8,128)(2,1)} %bitcast.52), calls=%async_computation.3 | async-start | bytes 3145728 | tf_op jit(solution)/shard_map/all_to_all | solution.py:198
  168.9 4.0 %copy-start.9 = (bf16[1024,768]{1,0:T(8,128)(2,1)S(1)}, bf16[1024,768]{1,0:T(8,128)(2,1)}, u32[]{:S(2)}) copy-start(bf16[1024,768]{1,0:T(8,128)(2,1)} %copy-done.8) | copy-start | bytes 4718596

commit v5 on v4

--- a/solution.py
+++ b/solution.py
@@ -71,15 +71,16 @@
     return lax.dynamic_update_slice(whole, far_down[None], (far, cut, 0))
 
 
-def product_kernel(turned, which_ref, rows_ref, weight_ref, *refs):
+def product_kernel(turned, added, which_ref, rows_ref, weight_ref, *refs):
     out_ref = refs[-1]
     sides = ((1,), (1,)) if turned else ((1,), (0,))
-    out_ref[...] = lax.dot_general(
-        rows_ref[...], weight_ref[...], (sides, ((), ())), preferred_element_type=F32
-    ).astype(out_ref.dtype)
-
-
-def product(rows, weight, turned, dtype, tile, which=None, weigh=1, later=()):
+    total = lax.dot_general(rows_ref[...], weight_ref[...], (sides, ((), ())), preferred_element_type=F32)
+    if added:
+        total = total + refs[0][...].astype(F32)
+    out_ref[...] = total.astype(out_ref.dtype)
+
+
+def product(rows, weight, turned, dtype, tile, which=None, weigh=1, later=(), plus=()):
     if which is None:
         stride, which = 1, jnp.zeros((1,), jnp.int32)
     else:
@@ -87,7 +88,7 @@
     steps = rows.shape[0] // tile // stride
     width = weight.shape[0] if turned else weight.shape[1]
     return pl.pallas_call(
-        functools.partial(product_kernel, turned),
+        functools.partial(product_kernel, turned, len(plus) > 0),
         grid_spec=pltpu.PrefetchScalarGridSpec(
             num_scalar_prefetch=1,
             grid=(steps,),
@@ -95,6 +96,7 @@
                 pl.BlockSpec((tile, rows.shape[1]), lambda i, which: (stride * i + which[0], 0)),
                 pl.BlockSpec(weight.shape, lambda i, which: (0, 0)),
             ]
+            + [pl.BlockSpec((tile, width), lambda i, which: (i, 0))] * len(plus)
             + [pl.BlockSpec(memory_space=pl.ANY)] * len(later),
             out_specs=pl.BlockSpec((tile, width), lambda i, which: (i, 0)),
         ),
@@ -105,7 +107,7 @@
             bytes_accessed=weigh * (2 * (steps * tile * rows.shape[1] + weight.size) + 4 * steps * tile * width),
             transcendentals=0,
         ),
-    )(which, rows, weight, *later)
+    )(which, rows, weight, *plus, *later)
 
 
 def joined_kernel(turned, place_ref, mine_ref, other_ref, weight_ref, *refs):
@@ -191,7 +193,7 @@
 
     def pair_sum(left, weight, turned, later=(), last=(), weigh=1):
         away = move(product(left, weight, turned, BF16, tile, 1 - core, weigh, later), "c", 1)
-        total = product(left, weight, turned, F32, tile, core, weigh, last) + away.astype(F32)
+        total = product(left, weight, turned, F32, tile, core, weigh, last, (away,))
         return total.reshape(ring, tile, -1)
 
     def rows_sum(partial):

time: 193 us -> 193 us (level)
  starting transfers between devices: 57 us -> 55 us
    all_to_all x2, waiting for transfers between devices: 24 us -> 26.5 us  [copies(): return lax.all_to_all(sent, axes, 0, 0).reshape(size * rows, -1)]
    unnamed x36 -> x34, local copies, waits for them, and re-layouts: 11.2 us -> 11.3 us
  transfers between devices with their start and end apart: 24 -> 24, of which waited for: 13 -> 14; matrix products, arithmetic and copies ran while one was open for 7% -> 6% of each run, Pallas kernels for 9% -> 8%
where the time goes in v5:
time: 193 us
  waiting for transfers between devices  92.2 us (48%)
  starting transfers between devices  55 us (28%)
  Pallas kernels  18.3 us (9%)
  local copies, waits for them, and re-layouts  14.9 us (8%)
  matrix products  6.45 us (3%)
  other arithmetic  4.68 us (2%)
    ppermute x20, waiting for transfers between devices, move(): lax.ppermute(block, axis, [(i, (i + hops) % size) for i in range(size)])  44.8 us
    ppermute x20, starting transfers between devices, move(): lax.ppermute(block, axis, [(i, (i + hops) % size) for i in range(size)])  29.8 us
    all_to_all x2, waiting for transfers between devices, copies(): return lax.all_to_all(sent, axes, 0, 0).reshape(size * rows, -1)  26.5 us
    all_to_all x2, waiting for transfers between devices, rows_sum(): pieces = lax.all_to_all(partial.reshape(peers, rows, -1), FAR, 0, 0)  20.9 us
    all_to_all x2, starting transfers between devices, copies(): return lax.all_to_all(sent, axes, 0, 0).reshape(size * rows, -1)  13.8 us
    all_to_all x2, starting transfers between devices, rows_sum(): pieces = lax.all_to_all(partial.reshape(peers, rows, -1), FAR, 0, 0)  11.4 us
    unnamed x34, local copies, waits for them, and re-layouts  11.3 us
    pallas_call x4, Pallas kernels, product(): pl.pallas_call(functools.partial(product_kernel, turned, len(plus) > 0),...  9.64 us
  transfers between devices with their start and end apart: 24, of which 14 were waited for; matrix products, arithmetic and copies ran while one was open for 6% of the time, Pallas kernels for 8%

profile of v5, /device:TPU:2, one launch (start us, length us, event | category | flops | bytes accessed | tf_op | source)
XLA Modules:
  0.0 192.6 jit_solution(11560573512848381425)
XLA Ops:
  0.6 2.2 %broadcast_in_dim.31 = bf16[32,32,768]{2,1,0:T(8,128)(2,1)} broadcast(bf16[32,768]{1,0:T(8,128)(2,1)} %param.4), dimensions={1,2} | broadcast | bytes 1622016 | tf_op jit(solution)/shard_map/broadcast_in_dim | solution.py:205
  2.8 9.1 %all-to-all-start = ((bf16[32,32,768]{2,1,0:T(8,128)(2,1)}), bf16[32,32,768]{2,1,0:T(8,128)(2,1)S(1)}, u32[]{:S(2)}, u32[]{:S(2)}) async-start(bf16[32,32,768]{2,1,0:T(8,128)(2,1)} %broadcast_in_dim.31), calls=%async_computation | async-start | bytes 3145728 | tf_op jit(solution)/shard_map/all_to_all | solution.py:206
  11.9 22.6 %all-to-all-done = bf16[32,32,768]{2,1,0:T(8,128)(2,1)S(1)} async-done(((bf16[32,32,768]{2,1,0:T(8,128)(2,1)}), bf16[32,32,768]{2,1,0:T(8,128)(2,1)S(1)}, u32[]{:S(2)}, u32[]{:S(2)}) %all-to-all-start) | async-done | bytes 1572896 | tf_op jit(solution)/shard_map/all_to_all | solution.py:206
  34.5 0.8 broadcast_in_dim.32
  35.3 4.6 %all-to-all-start.1 = ((bf16[8,32,768]{2,1,0:T(8,128)(2,1)}), bf16[8,32,768]{2,1,0:T(8,128)(2,1)S(1)}, u32[]{:S(2)}, u32[]{:S(2)}) async-start(bf16[8,32,768]{2,1,0:T(8,128)(2,1)} %broadcast_in_dim.32), calls=%async_computation.1 | async-start | bytes 786432 | tf_op jit(solution)/shard_map/all_to_all | solution.py:206
  39.9 2.3 %shard_map.75 = bf16[512,768]{1,0:T(8,128)(2,1)} custom-call(s32[1]{0:T(128)} %bitcast.3.which_ref, bf16[1024,768]{1,0:T(8,128)(2,1)S(1)} %bitcast.45, bf16[768,768]{1,0:T(8,128)(2,1)S(1)} %copy-done.1), custom_call_target="tpu_custom_call" | custom-call | flops 603979776 | bytes 3538944 | tf_op jit(solution)/shard_map/pallas_call | solution.py:90
  42.3 3.9 %all-to-all-done.1 = bf16[8,32,768]{2,1,0:T(8,128)(2,1)S(1)} async-done(((bf16[8,32,768]{2,1,0:T(8,128)(2,1)}), bf16[8,32,768]{2,1,0:T(8,128)(2,1)S(1)}, u32[]{:S(2)}, u32[]{:S(2)}) %all-to-all-start.1) | async-done | bytes 393248 | tf_op jit(solution)/shard_map/all_to_all | solution.py:206
  46.2 0.8 collective-permute-start.4
  47.0 1.2 collective-permute-start.3
  48.2 0.1 broadcast_in_dim.33
  48.4 1.3 copy-done.2
  49.6 2.9 %shard_map.76 = f32[512,768]{1,0:T(8,128)S(1)} custom-call(s32[1]{0:T(128)} %bitcast.1.which_ref, bf16[1024,768]{1,0:T(8,128)(2,1)S(1)} %bitcast.46, bf16[768,768]{1,0:T(8,128)(2,1)S(1)} %copy-done.2, bf16[512,768]{1,0:T(8,128)(2,1)} %collective-permute-done.refs_0_), custom_call_target="tpu_custom_call" | custom-call | flops 603979776 | bytes 3538944 | tf_op jit(solution)/shard_map/pallas_call | solution.py:90
  52.6 5.5 %collective-permute-start.2 = (bf16[64,768]{1,0:T(8,128)(2,1)S(1)}, bf16[64,768]{1,0:T(8,128)(2,1)S(1)}, u32[]{:S(2)}, u32[]{:S(2)}) collective-permute-start(bf16[64,768]{1,0:T(8,128)(2,1)S(1)} %get-tuple-element.48), channel_id=1, source_target_pairs={{0,6},{2,0},{4,2},{6,4},{1,7},{3,1},{5,3},{7,5},{8,14},{10,8},{12,... | collective-permute-start | bytes 294920 | tf_op jit(solution)/shard_map/ppermute | solution.py:32
  58.1 0.1 dynamic-slice_bitcast_fusion.3
  58.2 2.1 %collective-permute-start.8 = (bf16[128,768]{1,0:T(8,128)(2,1)S(1)}, bf16[128,768]{1,0:T(8,128)(2,1)S(1)}, u32[]{:S(2)}, u32[]{:S(2)}) collective-permute-start(bf16[128,768]{1,0:T(8,128)(2,1)S(1)} %slice.91), channel_id=1, source_target_pairs={{0,48},{16,0},{32,16},{48,32},{1,49},{17,1},{33,17},{49,33},{2,50}... | collective-permute-start | bytes 589832 | tf_op jit(solution)/shard_map/ppermute | solution.py:32
  60.3 0.1 collective-permute-start.7
  60.4 0.9 collective-permute-done.2.refs_3_
  61.3 4.6 %collective-permute-done.1.refs_1_ = bf16[64,768]{1,0:T(8,128)(2,1)S(1)} collective-permute-done((bf16[64,768]{1,0:T(8,128)(2,1)S(1)}, bf16[64,768]{1,0:T(8,128)(2,1)S(1)}, u32[]{:S(2)}, u32[]{:S(2)}) %collective-permute-start.1) | collective-permute-done | bytes 98336 | tf_op jit(solution)/shard_map/ppermute | solution.py:32
  65.9 0.1 collective-permute-start.5
  66.0 4.1 %collective-permute-start.6 = (bf16[128,768]{1,0:T(8,128)(2,1)S(1)}, bf16[128,768]{1,0:T(8,128)(2,1)S(1)}, u32[]{:S(2)}, u32[]{:S(2)}) collective-permute-start(bf16[128,768]{1,0:T(8,128)(2,1)S(1)} %get-tuple-element.22.refs_1_), channel_id=1, source_target_pairs={{0,6},{2,0},{4,2},{6,4},{1,7},{3,1},{5,3},{7,5},{8,14},{10,8},{12,... | collective-permute-start | bytes 589832 | tf_op jit(solution)/shard_map/ppermute | solution.py:32
  70.3 2.2 %shard_map.79 = bf16[512,768]{1,0:T(8,128)(2,1)S(1)} custom-call(s32[1]{0:T(128)} %bitcast.3.which_ref, bf16[1024,768]{1,0:T(8,128)(2,1)S(1)} %bitcast.48, bf16[768,768]{1,0:T(8,128)(2,1)S(1)} %copy-done, bf16[128,768]{1,0:T(8,128)(2,1)S(1)} %get-tuple-element.21.refs_0_, bf16[128,768]{1,0:T(8,128)(2,1)S(1)} %get-tuple-element.22.refs_1_), custom_call_target="tpu_custom_call" | custom-call | tf_op jit(solution)/shard_map/pallas_call | solution.py:90
  72.5 0.1 collective-permute-start.9
  72.6 2.2 %collective-permute-done.5.refs_1_ = bf16[128,768]{1,0:T(8,128)(2,1)S(1)} collective-permute-done((bf16[128,768]{1,0:T(8,128)(2,1)S(1)}, bf16[128,768]{1,0:T(8,128)(2,1)S(1)}, u32[]{:S(2)}, u32[]{:S(2)}) %collective-permute-start.5) | collective-permute-done | bytes 196640 | tf_op jit(solution)/shard_map/ppermute | solution.py:32
  74.9 0.3 shard_map.78
  75.2 2.2 %shard_map.80 = f32[512,768]{1,0:T(8,128)S(1)} custom-call(s32[1]{0:T(128)} %bitcast.1.which_ref, bf16[1024,768]{1,0:T(8,128)(2,1)S(1)} %bitcast.49, bf16[768,768]{1,0:T(8,128)(2,1)S(1)} %copy-done, bf16[512,768]{1,0:T(8,128)(2,1)S(1)} %collective-permute-done.9.refs_0_), custom_call_target="tpu_custom_call" | custom-call | tf_op jit(solution)/shard_map/pallas_call | solution.py:90
  77.5 3.7 %collective-permute-start.11 = (bf16[192,768]{1,0:T(8,128)(2,1)S(1)}, bf16[192,768]{1,0:T(8,128)(2,1)S(1)}, u32[]{:S(2)}, u32[]{:S(2)}) collective-permute-start(bf16[192,768]{1,0:T(8,128)(2,1)S(1)} %get-tuple-element.44), channel_id=1, source_target_pairs={{0,2},{2,4},{4,6},{6,0},{1,3},{3,5},{5,7},{7,1},{8,10},{10,12},{12... | collective-permute-start | bytes 884744 | tf_op jit(solution)/shard_map/ppermute | solution.py:32
  81.3 0.5 collective-permute-start.10
  81.8 0.1 dynamic-slice_bitcast_fusion
  81.9 12.9 %collective-permute-done.11 = bf16[192,768]{1,0:T(8,128)(2,1)S(1)} collective-permute-done((bf16[192,768]{1,0:T(8,128)(2,1)S(1)}, bf16[192,768]{1,0:T(8,128)(2,1)S(1)}, u32[]{:S(2)}, u32[]{:S(2)}) %collective-permute-start.11) | collective-permute-done | bytes 294944 | tf_op jit(solution)/shard_map/ppermute | solution.py:32
  94.9 2.3 %collective-permute-start.12 = (bf16[192,768]{1,0:T(8,128)(2,1)S(1)}, bf16[192,768]{1,0:T(8,128)(2,1)S(1)}, u32[]{:S(2)}, u32[]{:S(2)}) collective-permute-start(bf16[192,768]{1,0:T(8,128)(2,1)S(1)} %pad_maximum_fusion.2), channel_id=1, source_target_pairs={{0,2},{2,4},{4,6},{6,0},{1,3},{3,5},{5,7},{7,1},{8,10},{10,12},{12... | collective-permute-start | bytes 884744 | tf_op jit(solution)/shard_map/ppermute | solution.py:32
  97.3 2.2 %collective-permute-start.13 = (bf16[192,768]{1,0:T(8,128)(2,1)S(1)}, bf16[192,768]{1,0:T(8,128)(2,1)S(1)}, u32[]{:S(2)}, u32[]{:S(2)}) collective-permute-start(bf16[192,768]{1,0:T(8,128)(2,1)S(1)} %pad_maximum_fusion.3), channel_id=1, source_target_pairs={{0,6},{2,0},{4,2},{6,4},{1,7},{3,1},{5,3},{7,5},{8,14},{10,8},{12,... | collective-permute-start | bytes 884744 | tf_op jit(solution)/shard_map/ppermute | solution.py:32
  99.4 9.5 %collective-permute-done.12 = bf16[192,768]{1,0:T(8,128)(2,1)S(1)} collective-permute-done((bf16[192,768]{1,0:T(8,128)(2,1)S(1)}, bf16[192,768]{1,0:T(8,128)(2,1)S(1)}, u32[]{:S(2)}, u32[]{:S(2)}) %collective-permute-start.12) | collective-permute-done | bytes 294944 | tf_op jit(solution)/shard_map/ppermute | solution.py:32
  108.9 1.1 collective-permute-done.13
  110.0 0.1 collective-permute-start.14
  110.2 0.1 shard_map.83
  110.2 3.4 %collective-permute-start.17 = (bf16[128,768]{1,0:T(8,128)(2,1)S(1)}, bf16[128,768]{1,0:T(8,128)(2,1)S(1)}, u32[]{:S(2)}, u32[]{:S(2)}) collective-permute-start(bf16[128,768]{1,0:T(8,128)(2,1)S(1)} %shard_map.83), channel_id=1, source_target_pairs={{0,6},{2,0},{4,2},{6,4},{1,7},{3,1},{5,3},{7,5},{8,14},{10,8},{12,... | collective-permute-start | bytes 589832 | tf_op jit(solution)/shard_map/ppermute | solution.py:32
  113.7 0.1 pad_add_fusion.place_ref
  113.8 8.0 %collective-permute-done.17 = bf16[128,768]{1,0:T(8,128)(2,1)S(1)} collective-permute-done((bf16[128,768]{1,0:T(8,128)(2,1)S(1)}, bf16[128,768]{1,0:T(8,128)(2,1)S(1)}, u32[]{:S(2)}, u32[]{:S(2)}) %collective-permute-start.17) | collective-permute-done | bytes 196640 | tf_op jit(solution)/shard_map/ppermute | solution.py:32
  121.8 3.4 %collective-permute-start.18 = (bf16[64,768]{1,0:T(8,128)(2,1)S(1)}, bf16[64,768]{1,0:T(8,128)(2,1)S(1)}, u32[]{:S(2)}, u32[]{:S(2)}) collective-permute-start(bf16[64,768]{1,0:T(8,128)(2,1)S(1)} %slice.105), channel_id=1, source_target_pairs={{0,6},{2,0},{4,2},{6,4},{1,7},{3,1},{5,3},{7,5},{8,14},{10,8},{12,... | collective-permute-start | bytes 294920 | tf_op jit(solution)/shard_map/ppermute | solution.py:32
  125.1 1.9 collective-permute-done.15
  127.0 0.1 collective-permute-start.16
  127.2 3.2 %shard_map.82 = (bf16[1024,768]{1,0:T(8,128)(2,1)S(1)}, bf16[1024,768]{1,0:T(8,128)(2,1)S(1)}) custom-call(s32[2]{0:T(128)S(1)} %pad_add_fusion.place_ref, bf16[512,768]{1,0:T(8,128)(2,1)S(1)} %slice_dynamic-update-slice_fusion.mine_ref, bf16[512,768]{1,0:T(8,128)(2,1)S(1)} %collective-permute-done.14.other_ref, bf16[768,768]{1,0:T(8,128)(2,1)S(1)} %copy-done), custom_call_target="tpu_custom_call" | custom-call | flops 1207959552 | bytes 5898240 | tf_op jit(solution)/shard_map/pallas_call | solution.py:129
  130.4 1.1 copy-done.4
  131.5 1.2 copy-done.6
  132.7 0.6 copy-done.10
  133.4 1.5 collective-permute-done.16
  134.9 0.6 copy-done.11
  135.5 6.2 %all-to-all-start.2 = ((bf16[32,32,768]{2,1,0:T(8,128)(2,1)}), bf16[32,32,768]{2,1,0:T(8,128)(2,1)}, u32[]{:S(2)}, u32[]{:S(2)}) async-start(bf16[32,32,768]{2,1,0:T(8,128)(2,1)} %bitcast.55), calls=%async_computation.2 | async-start | bytes 3145728 | tf_op jit(solution)/shard_map/all_to_all | solution.py:200
  141.7 0.9 constant_dynamic-update-slice_fusion.4
  142.7 0.9 constant_dynamic-update-slice_fusion.3
  143.6 0.9 constant_dynamic-update-slice_fusion.2
  144.5 0.1 collective-permute-start.19
  144.6 2.3 %collective-permute-done.19.other_ref = bf16[512,768]{1,0:T(8,128)(2,1)S(1)} collective-permute-done((bf16[512,768]{1,0:T(8,128)(2,1)S(1)}, bf16[512,768]{1,0:T(8,128)(2,1)S(1)}, u32[]{:S(2)}, u32[]{:S(2)}) %collective-permute-start.19) | collective-permute-done | bytes 786464 | tf_op jit(solution)/shard_map/ppermute | solution.py:32
  146.9 1.3 copy-done.3
  148.1 4.9 %shard_map.84 = (bf16[1024,768]{1,0:T(8,128)(2,1)S(1)}, bf16[1024,768]{1,0:T(8,128)(2,1)S(1)}) custom-call(s32[2]{0:T(128)S(1)} %pad_add_fusion.place_ref, bf16[512,768]{1,0:T(8,128)(2,1)S(1)} %constant_dynamic-update-slice_fusion.1.mine_ref, bf16[512,768]{1,0:T(8,128)(2,1)S(1)} %collective-permute-done.19.other_ref, bf16[768,768]{1,0:T(8,128)(2,1)S(1)} %copy-done.3), custom_call_target="tpu_custom_call" | custom-call | flops 1207959552 | bytes 5898240 | tf_op jit(solution)/shard_map/pallas_call | solution.py:129
  153.1 1.2 copy-done.5
  154.2 1.2 copy-done.7
  155.4 8.6 %all-to-all-done.2 = bf16[32,32,768]{2,1,0:T(8,128)(2,1)} async-done(((bf16[32,32,768]{2,1,0:T(8,128)(2,1)}), bf16[32,32,768]{2,1,0:T(8,128)(2,1)}, u32[]{:S(2)}, u32[]{:S(2)}) %all-to-all-start.2) | async-done | bytes 1572896 | tf_op jit(solution)/shard_map/all_to_all | solution.py:200
  164.0 5.2 %all-to-all-start.3 = ((bf16[32,32,768]{2,1,0:T(8,128)(2,1)}), bf16[32,32,768]{2,1,0:T(8,128)(2,1)}, u32[]{:S(2)}, u32[]{:S(2)}) async-start(bf16[32,32,768]{2,1,0:T(8,128)(2,1)} %bitcast.56), calls=%async_computation.3 | async-start | bytes 3145728 | tf_op jit(solution)/shard_map/all_to_all | solution.py:200
  169.2 4.0 %convolution_convert_fusion = bf16[768,768]{1,0:T(8,128)(2,1)} fusion(bf16[1024,768]{1,0:T(8,128)(2,1)} %copy-done.6, bf16[1024,768]{1,0:T(8,128)(2,1)S(1)} %bitcast.50), kind=kOutput, calls=%fused_computation | convolution fusion | flops 1208549376 | bytes 4325376 | tf_op jit(solution)/shard_map/dot_general | solution.py:27
  173.2 2.5 %convolution_convert_fusion.1 = bf16[768,768]{1,0:T(8,128)(2,1)} fusion(bf16[1024,768]{1,0:T(8,128)(2,1)S(1)} %bitcast.47, bf16[1024,768]{1,0:T(8,128)(2,1)S(1)} %copy-done.8), kind=kOutput, calls=%fused_computation.1 | convolution fusion | flops 1208549376 | bytes 4325376 | tf_op jit(solution)/shard_map/dot_general | solution.py:27
  175.7 2.3 %reduce_sum.24 = bf16[32,768]{1,0:T(8,128)(2,1)} reduce(bf16[32,32,768]{2,1,0:T(8,128)(2,1)} %all-to-all-done.2, bf16[]{:T(256)} %constant.97.clone.1), dimensions={0}, to_apply=%region_0.1 | reduce | flops 761856 | bytes 1622018 | tf_op jit(solution)/shard_map/reduce_sum | solution.py:201
  177.9 12.4 %all-to-all-done.3 = bf16[32,32,768]{2,1,0:T(8,128)(2,1)} async-done(((bf16[32,32,768]{2,1,0:T(8,128)(2,1)}), bf16[32,32,768]{2,1,0:T(8,128)(2,1)}, u32[]{:S(2)}, u32[]{:S(2)}) %all-to-all-start.3) | async-done | bytes 1572896 | tf_op jit(solution)/shard_map/all_to_all | solution.py:200
  190.3 2.3 %reduce_sum.25 = bf16[32,768]{1,0:T(8,128)(2,1)} reduce(bf16[32,32,768]{2,1,0:T(8,128)(2,1)} %all-to-all-done.3, bf16[]{:T(256)} %constant.97.clone.1), dimensions={0}, to_apply=%region_1.2 | reduce | flops 761856 | bytes 1622018 | tf_op jit(solution)/shard_map/reduce_sum | solution.py:201
  (60 shorter events, 0.7 us)
Async XLA Ops:
  2.8 31.7 %copy-start.12 = (bf16[32,768]{1,0:T(8,128)(2,1)S(1)}, bf16[32,768]{1,0:T(8,128)(2,1)}, u32[]{:S(2)}) copy-start(bf16[32,768]{1,0:T(8,128)(2,1)} %param.7) | copy-start | bytes 147460
  2.8 37.1 %copy-start.1 = (bf16[768,768]{1,0:T(8,128)(2,1)S(1)}, bf16[768,768]{1,0:T(8,128)(2,1)}, u32[]{:S(2)}) copy-start(bf16[768,768]{1,0:T(8,128)(2,1)} %weight_ref.11) | copy-start | bytes 3538948
  2.8 31.7 %all-to-all-start = ((bf16[32,32,768]{2,1,0:T(8,128)(2,1)}), bf16[32,32,768]{2,1,0:T(8,128)(2,1)S(1)}, u32[]{:S(2)}, u32[]{:S(2)}) async-start(bf16[32,32,768]{2,1,0:T(8,128)(2,1)} %broadcast_in_dim.31), calls=%async_computation | async-start | bytes 3145728 | tf_op jit(solution)/shard_map/all_to_all | solution.py:206
  35.3 10.9 %all-to-all-start.1 = ((bf16[8,32,768]{2,1,0:T(8,128)(2,1)}), bf16[8,32,768]{2,1,0:T(8,128)(2,1)S(1)}, u32[]{:S(2)}, u32[]{:S(2)}) async-start(bf16[8,32,768]{2,1,0:T(8,128)(2,1)} %broadcast_in_dim.32), calls=%async_computation.1 | async-start | bytes 786432 | tf_op jit(solution)/shard_map/all_to_all | solution.py:206
  42.3 6.1 %collective-permute-start = (bf16[512,768]{1,0:T(8,128)(2,1)}, bf16[512,768]{1,0:T(8,128)(2,1)}, u32[]{:S(2)}, u32[]{:S(2)}) collective-permute-start(bf16[512,768]{1,0:T(8,128)(2,1)} %shard_map.75), channel_id=1, source_target_pairs={{0,1},{1,0},{2,3},{3,2},{4,5},{5,4},{6,7},{7,6},{8,9},{9,8},{10,11... | collective-permute-start | bytes 2359304 | tf_op jit(solution)/shard_map/ppermute | solution.py:32
  46.2 12.0 %collective-permute-start.4 = (bf16[256,768]{1,0:T(8,128)(2,1)S(1)}, bf16[256,768]{1,0:T(8,128)(2,1)S(1)}, u32[]{:S(2)}, u32[]{:S(2)}) collective-permute-start(bf16[256,768]{1,0:T(8,128)(2,1)S(1)} %bitcast.57), channel_id=1, source_target_pairs={{0,48},{16,0},{32,16},{48,32},{1,49},{17,1},{33,17},{49,33},{2,50}... | collective-permute-start | bytes 1179656 | tf_op jit(solution)/shard_map/ppermute | solution.py:32
  47.0 13.3 %collective-permute-start.3 = (bf16[256,768]{1,0:T(8,128)(2,1)S(1)}, bf16[256,768]{1,0:T(8,128)(2,1)S(1)}, u32[]{:S(2)}, u32[]{:S(2)}) collective-permute-start(bf16[256,768]{1,0:T(8,128)(2,1)S(1)} %bitcast.58), channel_id=1, source_target_pairs={{0,16},{16,32},{32,48},{48,0},{1,17},{17,33},{33,49},{49,1},{2,18}... | collective-permute-start | bytes 1179656 | tf_op jit(solution)/shard_map/ppermute | solution.py:32
  48.3 1.3 copy-start.2
  52.6 8.7 %collective-permute-start.2 = (bf16[64,768]{1,0:T(8,128)(2,1)S(1)}, bf16[64,768]{1,0:T(8,128)(2,1)S(1)}, u32[]{:S(2)}, u32[]{:S(2)}) collective-permute-start(bf16[64,768]{1,0:T(8,128)(2,1)S(1)} %get-tuple-element.48), channel_id=1, source_target_pairs={{0,6},{2,0},{4,2},{6,4},{1,7},{3,1},{5,3},{7,5},{8,14},{10,8},{12,... | collective-permute-start | bytes 294920 | tf_op jit(solution)/shard_map/ppermute | solution.py:32
  58.1 7.8 %collective-permute-start.1 = (bf16[64,768]{1,0:T(8,128)(2,1)S(1)}, bf16[64,768]{1,0:T(8,128)(2,1)S(1)}, u32[]{:S(2)}, u32[]{:S(2)}) collective-permute-start(bf16[64,768]{1,0:T(8,128)(2,1)S(1)} %get-tuple-element.49), channel_id=1, source_target_pairs={{0,2},{2,4},{4,6},{6,0},{1,3},{3,5},{5,7},{7,1},{8,10},{10,12},{12... | collective-permute-start | bytes 294920 | tf_op jit(solution)/shard_map/ppermute | solution.py:32
  58.2 12.0 %collective-permute-start.8 = (bf16[128,768]{1,0:T(8,128)(2,1)S(1)}, bf16[128,768]{1,0:T(8,128)(2,1)S(1)}, u32[]{:S(2)}, u32[]{:S(2)}) collective-permute-start(bf16[128,768]{1,0:T(8,128)(2,1)S(1)} %slice.91), channel_id=1, source_target_pairs={{0,48},{16,0},{32,16},{48,32},{1,49},{17,1},{33,17},{49,33},{2,50}... | collective-permute-start | bytes 589832 | tf_op jit(solution)/shard_map/ppermute | solution.py:32
  60.3 9.9 %collective-permute-start.7 = (bf16[128,768]{1,0:T(8,128)(2,1)S(1)}, bf16[128,768]{1,0:T(8,128)(2,1)S(1)}, u32[]{:S(2)}, u32[]{:S(2)}) collective-permute-start(bf16[128,768]{1,0:T(8,128)(2,1)S(1)} %slice.90), channel_id=1, source_target_pairs={{0,16},{16,32},{32,48},{48,0},{1,17},{17,33},{33,49},{49,1},{2,18}... | collective-permute-start | bytes 589832 | tf_op jit(solution)/shard_map/ppermute | solution.py:32
  65.9 4.4 %copy-start = (bf16[768,768]{1,0:T(8,128)(2,1)S(1)}, bf16[768,768]{1,0:T(8,128)(2,1)}, u32[]{:S(2)}) copy-start(bf16[768,768]{1,0:T(8,128)(2,1)} %weight_ref.10) | copy-start | bytes 3538948
  65.9 8.9 %collective-permute-start.5 = (bf16[128,768]{1,0:T(8,128)(2,1)S(1)}, bf16[128,768]{1,0:T(8,128)(2,1)S(1)}, u32[]{:S(2)}, u32[]{:S(2)}) collective-permute-start(bf16[128,768]{1,0:T(8,128)(2,1)S(1)} %get-tuple-element.21.refs_0_), channel_id=1, source_target_pairs={{0,2},{2,4},{4,6},{6,0},{1,3},{3,5},{5,7},{7,1},{8,10},{10,12},{12... | collective-permute-start | bytes 589832 | tf_op jit(solution)/shard_map/ppermute | solution.py:32
  66.0 8.9 %collective-permute-start.6 = (bf16[128,768]{1,0:T(8,128)(2,1)S(1)}, bf16[128,768]{1,0:T(8,128)(2,1)S(1)}, u32[]{:S(2)}, u32[]{:S(2)}) collective-permute-start(bf16[128,768]{1,0:T(8,128)(2,1)S(1)} %get-tuple-element.22.refs_1_), channel_id=1, source_target_pairs={{0,6},{2,0},{4,2},{6,4},{1,7},{3,1},{5,3},{7,5},{8,14},{10,8},{12,... | collective-permute-start | bytes 589832 | tf_op jit(solution)/shard_map/ppermute | solution.py:32
  72.5 2.7 %collective-permute-start.9 = (bf16[512,768]{1,0:T(8,128)(2,1)S(1)}, bf16[512,768]{1,0:T(8,128)(2,1)S(1)}, u32[]{:S(2)}, u32[]{:S(2)}) collective-permute-start(bf16[512,768]{1,0:T(8,128)(2,1)S(1)} %shard_map.79), channel_id=1, source_target_pairs={{0,1},{1,0},{2,3},{3,2},{4,5},{5,4},{6,7},{7,6},{8,9},{9,8},{10,11... | collective-permute-start | bytes 2359304 | tf_op jit(solution)/shard_map/ppermute | solution.py:32
  77.5 17.3 %collective-permute-start.11 = (bf16[192,768]{1,0:T(8,128)(2,1)S(1)}, bf16[192,768]{1,0:T(8,128)(2,1)S(1)}, u32[]{:S(2)}, u32[]{:S(2)}) collective-permute-start(bf16[192,768]{1,0:T(8,128)(2,1)S(1)} %get-tuple-element.44), channel_id=1, source_target_pairs={{0,2},{2,4},{4,6},{6,0},{1,3},{3,5},{5,7},{7,1},{8,10},{10,12},{12... | collective-permute-start | bytes 884744 | tf_op jit(solution)/shard_map/ppermute | solution.py:32
  81.3 13.5 %collective-permute-start.10 = (bf16[192,768]{1,0:T(8,128)(2,1)S(1)}, bf16[192,768]{1,0:T(8,128)(2,1)S(1)}, u32[]{:S(2)}, u32[]{:S(2)}) collective-permute-start(bf16[192,768]{1,0:T(8,128)(2,1)S(1)} %get-tuple-element.45), channel_id=1, source_target_pairs={{0,6},{2,0},{4,2},{6,4},{1,7},{3,1},{5,3},{7,5},{8,14},{10,8},{12,... | collective-permute-start | bytes 884744 | tf_op jit(solution)/shard_map/ppermute | solution.py:32
  94.9 14.0 %collective-permute-start.12 = (bf16[192,768]{1,0:T(8,128)(2,1)S(1)}, bf16[192,768]{1,0:T(8,128)(2,1)S(1)}, u32[]{:S(2)}, u32[]{:S(2)}) collective-permute-start(bf16[192,768]{1,0:T(8,128)(2,1)S(1)} %pad_maximum_fusion.2), channel_id=1, source_target_pairs={{0,2},{2,4},{4,6},{6,0},{1,3},{3,5},{5,7},{7,1},{8,10},{10,12},{12... | collective-permute-start | bytes 884744 | tf_op jit(solution)/shard_map/ppermute | solution.py:32
  97.3 12.7 %collective-permute-start.13 = (bf16[192,768]{1,0:T(8,128)(2,1)S(1)}, bf16[192,768]{1,0:T(8,128)(2,1)S(1)}, u32[]{:S(2)}, u32[]{:S(2)}) collective-permute-start(bf16[192,768]{1,0:T(8,128)(2,1)S(1)} %pad_maximum_fusion.3), channel_id=1, source_target_pairs={{0,6},{2,0},{4,2},{6,4},{1,7},{3,1},{5,3},{7,5},{8,14},{10,8},{12,... | collective-permute-start | bytes 884744 | tf_op jit(solution)/shard_map/ppermute | solution.py:32
  110.0 17.1 %collective-permute-start.14 = (bf16[512,768]{1,0:T(8,128)(2,1)S(1)}, bf16[512,768]{1,0:T(8,128)(2,1)S(1)}, u32[]{:S(2)}, u32[]{:S(2)}) collective-permute-start(bf16[512,768]{1,0:T(8,128)(2,1)S(1)} %slice_dynamic-update-slice_fusion.mine_ref), channel_id=1, source_target_pairs={{0,1},{1,0},{2,3},{3,2},{4,5},{5,4},{6,7},{7,6},{8,9},{9,8},{10,11... | collective-permute-start | bytes 2359304 | tf_op jit(solution)/shard_map/ppermute | solution.py:32
  110.2 11.5 %collective-permute-start.17 = (bf16[128,768]{1,0:T(8,128)(2,1)S(1)}, bf16[128,768]{1,0:T(8,128)(2,1)S(1)}, u32[]{:S(2)}, u32[]{:S(2)}) collective-permute-start(bf16[128,768]{1,0:T(8,128)(2,1)S(1)} %shard_map.83), channel_id=1, source_target_pairs={{0,6},{2,0},{4,2},{6,4},{1,7},{3,1},{5,3},{7,5},{8,14},{10,8},{12,... | collective-permute-start | bytes 589832 | tf_op jit(solution)/shard_map/ppermute | solution.py:32
  113.7 13.4 %collective-permute-start.15 = (bf16[128,768]{1,0:T(8,128)(2,1)S(1)}, bf16[128,768]{1,0:T(8,128)(2,1)S(1)}, u32[]{:S(2)}, u32[]{:S(2)}) collective-permute-start(bf16[128,768]{1,0:T(8,128)(2,1)S(1)} %shard_map.83), channel_id=1, source_target_pairs={{0,2},{2,4},{4,6},{6,0},{1,3},{3,5},{5,7},{7,1},{8,10},{10,12},{12... | collective-permute-start | bytes 589832 | tf_op jit(solution)/shard_map/ppermute | solution.py:32
  121.7 8.6 %copy-start.9 = (bf16[128,768]{1,0:T(8,128)(2,1)}, bf16[128,768]{1,0:T(8,128)(2,1)S(1)}, u32[]{:S(2)}) copy-start(bf16[128,768]{1,0:T(8,128)(2,1)S(1)} %collective-permute-done.17) | copy-start | bytes 589828
  121.8 10.9 %collective-permute-start.18 = (bf16[64,768]{1,0:T(8,128)(2,1)S(1)}, bf16[64,768]{1,0:T(8,128)(2,1)S(1)}, u32[]{:S(2)}, u32[]{:S(2)}) collective-permute-start(bf16[64,768]{1,0:T(8,128)(2,1)S(1)} %slice.105), channel_id=1, source_target_pairs={{0,6},{2,0},{4,2},{6,4},{1,7},{3,1},{5,3},{7,5},{8,14},{10,8},{12,... | collective-permute-start | bytes 294920 | tf_op jit(solution)/shard_map/ppermute | solution.py:32
  127.0 7.8 %collective-permute-start.16 = (bf16[64,768]{1,0:T(8,128)(2,1)S(1)}, bf16[64,768]{1,0:T(8,128)(2,1)S(1)}, u32[]{:S(2)}, u32[]{:S(2)}) collective-permute-start(bf16[64,768]{1,0:T(8,128)(2,1)S(1)} %slice.104), channel_id=1, source_target_pairs={{0,2},{2,4},{4,6},{6,0},{1,3},{3,5},{5,7},{7,1},{8,10},{10,12},{12... | collective-permute-start | bytes 294920 | tf_op jit(solution)/shard_map/ppermute | solution.py:32
  130.4 1.2 copy-start.4
  131.5 1.2 copy-start.6
  132.7 0.6 copy-start.10
  134.9 0.6 copy-start.11
  135.5 28.4 %all-to-all-start.2 = ((bf16[32,32,768]{2,1,0:T(8,128)(2,1)}), bf16[32,32,768]{2,1,0:T(8,128)(2,1)}, u32[]{:S(2)}, u32[]{:S(2)}) async-start(bf16[32,32,768]{2,1,0:T(8,128)(2,1)} %bitcast.55), calls=%async_computation.2 | async-start | bytes 3145728 | tf_op jit(solution)/shard_map/all_to_all | solution.py:200
  144.5 2.4 %collective-permute-start.19 = (bf16[512,768]{1,0:T(8,128)(2,1)S(1)}, bf16[512,768]{1,0:T(8,128)(2,1)S(1)}, u32[]{:S(2)}, u32[]{:S(2)}) collective-permute-start(bf16[512,768]{1,0:T(8,128)(2,1)S(1)} %constant_dynamic-update-slice_fusion.1.mine_ref), channel_id=1, source_target_pairs={{0,1},{1,0},{2,3},{3,2},{4,5},{5,4},{6,7},{7,6},{8,9},{9,8},{10,11... | collective-permute-start | bytes 2359304 | tf_op jit(solution)/shard_map/ppermute | solution.py:32
  146.9 1.3 copy-start.3
  153.0 1.2 copy-start.5
  154.2 1.2 copy-start.7
  164.0 26.3 %all-to-all-start.3 = ((bf16[32,32,768]{2,1,0:T(8,128)(2,1)}), bf16[32,32,768]{2,1,0:T(8,128)(2,1)}, u32[]{:S(2)}, u32[]{:S(2)}) async-start(bf16[32,32,768]{2,1,0:T(8,128)(2,1)} %bitcast.56), calls=%async_computation.3 | async-start | bytes 3145728 | tf_op jit(solution)/shard_map/all_to_all | solution.py:200
  169.2 4.0 %copy-start.8 = (bf16[1024,768]{1,0:T(8,128)(2,1)S(1)}, bf16[1024,768]{1,0:T(8,128)(2,1)}, u32[]{:S(2)}) copy-start(bf16[1024,768]{1,0:T(8,128)(2,1)} %copy-done.7) | copy-start | bytes 4718596
